TPU v7x, 32 devices: a whole 2x2x4 slice. The times are simulated.
32 devices in a mesh: dp: 2 (over x), lat: 4 (over y, core), lon: 4 (over z).
Axes of the slice: x: 2, y: 2, z: 4, core: 2. Of those that a mesh axis runs over, the one named last changes fastest.
Arguments:
- inputs: bfloat16 [2, 128, 64, 1024], P('dp', 'lat', 'lon'), may hold values from -40 to 40
- grad_out: bfloat16 [2, 128, 64, 1024], P('dp', 'lat', 'lon'), may hold values from -6 to 6
- w_qkv: bfloat16 [1024, 3072], replicated, may hold values from -0.1875 to 0.1875
Outputs:
- grad_inputs: bfloat16 [2, 128, 64, 1024], P('dp', 'lat', 'lon')
- grad_w_qkv: float32 [1024, 3072], P(('dp', 'lat', 'lon'))
All inputs are finite; a program needn't handle non-finite values.
Results may differ from a plain program's by a relative error of at most 0.011.
Values may be sent and summed in bfloat16 or wider, within the bound.
No kernel may reach another device: no remote copies, remote signals or barrier semaphores. Data moves between devices by JAX's collectives and lax.ppermute only.
A program may use at most 192 MiB of HBM per device.

v0:
```python
import functools

import jax
import jax.numpy as jnp
import numpy as np
from jax import lax
from jax.experimental import pallas as pl
from jax.experimental.pallas import tpu as pltpu
from jax.sharding import PartitionSpec as P

HEADS = 16
WIN = 13
MARGIN = WIN // 2
TILE_R = 4
GROUP = 4
KEY_COLS = 32
HALO_COLS = 16
REGION_R = 16
PAD_R = 2
EDGE_R = MARGIN + PAD_R
NEG = -1e30
BF = jnp.bfloat16
F32 = jnp.float32
MIB = 1024 * 1024
FINISH_FLOPS = 9 * 10**9
LANES = 128
ATTENTION_MIB = 32

NT = (((1,), (1,)), ((), ()))
TN = (((0,), (0,)), ((), ()))
NN = (((1,), (0,)), ((), ()))


def dot(a, b, dims=NN):
    return lax.dot_general(a, b, dims, preferred_element_type=F32)


def region_top(tile, band_start, band_rows, total_rows):
    lowest = jnp.where(band_start == 0, TILE_R, 0)
    highest = jnp.where(band_start + band_rows == total_rows, band_rows - 2 * TILE_R, band_rows)
    return jnp.clip(tile * TILE_R, lowest, highest)


def mask_kernel(band_rows, band_cols, total_rows, start_ref, mask_ref):
    band_start = start_ref[0]
    tile = pl.program_id(0)
    shape = mask_ref.shape[1:]
    first = region_top(tile, band_start, band_rows, total_rows)
    key = lax.broadcasted_iota(jnp.int32, shape, 0)
    query = lax.broadcasted_iota(jnp.int32, shape, 1) & (TILE_R * band_cols - 1)
    key_row = band_start - MARGIN + first + (key >> (KEY_COLS.bit_length() - 1))
    place = key & (KEY_COLS - 1)
    query_row = band_start + tile * TILE_R + (query >> (band_cols.bit_length() - 1))
    query_col = query & (band_cols - 1)
    window = jnp.clip(query_row - MARGIN, 0, total_rows - WIN)
    row_inside = (key_row >= window) & (key_row < window + WIN)
    key_col = jnp.where(
        place < band_cols,
        place,
        jnp.where(place < band_cols + MARGIN, place - band_cols - MARGIN, place - MARGIN),
    )
    col_inside = (jnp.abs(key_col - query_col) <= MARGIN) & (place < band_cols + 2 * MARGIN)
    mask_ref[0] = jnp.where(row_inside & col_inside, 0.0, NEG).astype(BF)


def window_masks(start, band_rows, band_cols, total_rows):
    tiles = band_rows // TILE_R
    shape = (REGION_R * KEY_COLS, 2 * TILE_R * band_cols)
    return pl.pallas_call(
        functools.partial(mask_kernel, band_rows, band_cols, total_rows),
        grid=(tiles,),
        in_specs=[pl.BlockSpec(memory_space=pltpu.SMEM)],
        out_specs=pl.BlockSpec((1,) + shape, lambda t: (t, 0, 0)),
        out_shape=jax.ShapeDtypeStruct((tiles,) + shape, BF),
        cost_estimate=pl.CostEstimate(flops=10**7, bytes_accessed=2**21, transcendentals=0),
    )(start)


def attention_kernel(band_rows, band_cols, total_rows, head_width, extra, first, count, shift, *refs):
    (place_ref, mask_ref, left_ref, right_ref, rows_a, rows_b, corners_a, corners_b,
     qkv_hbm, grad_hbm, w_hbm) = refs[:11]
    before_a, before_b = refs[11 : 11 + shift], refs[11 + shift : 11 + 2 * shift]
    (dq_all, out_a_all, out_b_all, mid_all, to_left_all, to_right_all,
     halo_ref, spot_ref, q_ref, k_ref, v_ref, dk_ref, dv_ref,
     own_refs, w_refs, own_sem, w_sem) = refs[11 + extra :]
    band_start = place_ref[0]
    even = place_ref[1] == 0
    tiles = band_rows // TILE_R
    queries = TILE_R * band_cols
    keys = REGION_R * KEY_COLS
    width = GROUP * head_width
    lanes = GROUP * queries
    region_rows = band_rows + 2 * MARGIN
    side = MARGIN * band_rows
    edge = MARGIN * band_cols
    corner = 2 * MARGIN * EDGE_R
    at_above = 2 * side
    at_below = at_above + edge
    at_cl = at_below + edge
    at_cr = at_cl + corner
    halves = [(i, slice(i * LANES, (i + 1) * LANES)) for i in range(width // LANES)]

    step = pl.program_id(0)
    dq_ref, mid_ref, to_left_ref, to_right_ref = (
        ref.at[step] for ref in (dq_all, mid_all, to_left_all, to_right_all)
    )
    out_a, out_b = (ref.at[step + shift] for ref in (out_a_all, out_b_all))
    groups = HEADS // GROUP

    def copies(slot, parts):
        at = lambda part: pl.ds(pl.multiple_of((part * groups + first + slot) * width, width), width)
        for part, source, where, i in parts:
            target, sem = (w_refs, w_sem) if where else (own_refs, own_sem)
            yield pltpu.make_async_copy(source.at[:, at(part)], target.at[slot, i], sem.at[slot, i])

    for_k = ((1, w_hbm, 1, 0), (1, qkv_hbm, 0, 1))
    for_v = ((2, w_hbm, 1, 1), (2, qkv_hbm, 0, 2))
    for_q = ((0, qkv_hbm, 0, 0), (0, grad_hbm, 0, 3))

    @pl.when(step == 0)
    def _():
        for ref, kept in ((out_a_all, before_a), (out_b_all, before_b)):
            for i in range(shift):
                ref[i] = kept[0][i]
        for slot in range(count):
            for copy in copies(slot, for_k + for_v + for_q):
                copy.start()
        halo_ref[:side] = left_ref[...]
        halo_ref[side:at_above] = right_ref[...]
        for above, below, size, refs_ab in (
            (at_above, at_below, edge, (rows_a, rows_b)),
            (at_cl, at_cr, corner, (corners_a, corners_b)),
        ):
            for ref, at in zip(refs_ab, (jnp.where(even, below, above), jnp.where(even, above, below))):
                halo_ref[pl.ds(pl.multiple_of(at, 16), size), :] = ref[...]
        spot_ref[...] = jnp.zeros_like(spot_ref)

    def place(target, own, weights):
        fresh = dot(halo_ref[...], weights)
        for col in range(MARGIN):
            start = MARGIN * HALO_COLS + col
            for part, at in halves:
                spot_ref[part, pl.ds(start, band_rows, stride=HALO_COLS), :] = fresh[
                    col * band_rows : (col + 1) * band_rows, at
                ]
                spot_ref[part, pl.ds(start + MARGIN, band_rows, stride=HALO_COLS), :] = fresh[
                    side + col * band_rows : side + (col + 1) * band_rows, at
                ]
        for corner_at, skip, row in ((at_cl, PAD_R, 0), (at_cr, 0, MARGIN + band_rows)):
            for col in range(2 * MARGIN):
                base = corner_at + col * EDGE_R + skip
                spot = pl.ds(row * HALO_COLS + col, MARGIN, stride=HALO_COLS)
                for part, at in halves:
                    spot_ref[part, spot, :] = fresh[base : base + MARGIN, at]
        for row in range(region_rows):
            base = row * KEY_COLS
            inner = row - MARGIN
            if inner < 0:
                ours = fresh[at_above + row * band_cols : at_above + (row + 1) * band_cols].astype(BF)
            elif inner < band_rows:
                ours = own[inner * band_cols : (inner + 1) * band_cols, :]
            else:
                past = at_below + (inner - band_rows) * band_cols
                ours = fresh[past : past + band_cols].astype(BF)
            target[base : base + band_cols, :] = ours
            for part, at in halves:
                target[base + band_cols : base + KEY_COLS, at] = spot_ref[
                    part, row * HALO_COLS : (row + 1) * HALO_COLS, :
                ].astype(BF)

    grad_ref = own_refs.at[step, 3]
    for copy in copies(step, for_k + for_v + for_q):
        copy.wait()
    place(k_ref, own_refs.at[step, 1], w_refs[step, 0])
    place(v_ref, own_refs.at[step, 2], w_refs[step, 1])
    q_ref[...] = own_refs[step, 0] * BF(head_width**-0.5)
    dk_ref[...] = jnp.zeros_like(dk_ref)
    dv_ref[...] = jnp.zeros_like(dv_ref)

    def spread(rows):
        block = jnp.concatenate([rows] * GROUP, axis=0)
        head_row = lax.broadcasted_iota(jnp.int32, (lanes, width), 0) // queries
        head_col = lax.broadcasted_iota(jnp.int32, (lanes, width), 1) // head_width
        return jnp.where(head_row == head_col, block, jnp.zeros_like(block))

    def one_tile(tile, carry):
        first = region_top(tile, band_start, band_rows, total_rows)
        region = pl.ds(pl.multiple_of(first * KEY_COLS, TILE_R * KEY_COLS), keys)
        total = pl.ds(pl.multiple_of((first + PAD_R) * KEY_COLS, PAD_R * KEY_COLS), keys)
        mine = pl.ds(pl.multiple_of(tile * queries, queries), queries)
        q_wide = spread(q_ref[mine, :])
        g_wide = spread(grad_ref[mine, :])
        mask = mask_ref[tile].astype(F32)
        scores = dot(k_ref[region, :], q_wide, NT) + jnp.concatenate([mask, mask], axis=1)
        dots = dot(v_ref[region, :], g_wide, NT)
        exponent = jnp.exp(scores - jnp.max(scores, axis=0, keepdims=True))
        inverse = 1.0 / jnp.sum(exponent, axis=0, keepdims=True)
        delta = jnp.sum(exponent * dots, axis=0, keepdims=True) * inverse
        attn = exponent * inverse
        dscore = (attn * (dots - delta)).astype(BF)
        dv = dot(attn.astype(BF), g_wide)
        dk = dot(dscore, q_wide)
        for part, at in halves:
            dv_ref[part, total, :] += dv[:, at]
            dk_ref[part, total, :] += dk[:, at]
        dq_wide = dot(dscore, k_ref[region, :], TN)
        head_col = lax.broadcasted_iota(jnp.int32, (queries, width), 1) // head_width
        dq = jnp.zeros((queries, width), F32)
        for head in range(GROUP):
            dq = jnp.where(head_col == head, dq_wide[head * queries : (head + 1) * queries], dq)
        dq_ref[mine, :] = (dq * head_width**-0.5).astype(BF)
        return carry

    lax.fori_loop(0, tiles, one_tile, 0, unroll=4)

    middle = (PAD_R + MARGIN) * KEY_COLS
    below = (PAD_R + MARGIN + band_rows) * KEY_COLS
    for part, acc in enumerate((dk_ref, dv_ref)):
        for lane, at in halves:
            for out, own_at, side_at in (
                (out_a, jnp.where(even, below, PAD_R * KEY_COLS), jnp.where(even, below, 0)),
                (out_b, jnp.where(even, PAD_R * KEY_COLS, below), jnp.where(even, 0, below)),
            ):
                for row in range(MARGIN):
                    start = pl.multiple_of(own_at + row * KEY_COLS, KEY_COLS)
                    out[part, row * band_cols : (row + 1) * band_cols, at] = acc[
                        lane, pl.ds(start, band_cols), :
                    ].astype(BF)
                for pair in range(MARGIN):
                    here = slice(edge + pair * 2 * EDGE_R, edge + (pair + 1) * 2 * EDGE_R)
                    start = side_at + band_cols + 2 * pair
                    out[part, here, at] = jnp.concatenate(
                        [
                            acc[lane, pl.ds(start, EDGE_R, stride=KEY_COLS), :],
                            acc[lane, pl.ds(start + 1, EDGE_R, stride=KEY_COLS), :],
                        ],
                        axis=0,
                    ).astype(BF)
            for row in range(band_rows):
                base = middle + row * KEY_COLS
                mid_ref[part, row * band_cols : (row + 1) * band_cols, at] = acc[
                    lane, base : base + band_cols, :
                ].astype(BF)
            for col in range(MARGIN):
                here = slice(col * band_rows, (col + 1) * band_rows)
                start = middle + band_cols + col
                to_left_ref[part, here, at] = acc[
                    lane, pl.ds(start, band_rows, stride=KEY_COLS), :
                ].astype(BF)
                to_right_ref[part, here, at] = acc[
                    lane, pl.ds(start + MARGIN, band_rows, stride=KEY_COLS), :
                ].astype(BF)


def attention_grads(first, count, place, masks, halo, qkv, grad_out, w_qkv, shape, before, after):
    band_rows, band_cols, total_rows = shape
    tokens, width = grad_out.shape
    head_width = width // HEADS
    block = GROUP * head_width
    region_tokens = (band_rows + 2 * MARGIN) * KEY_COLS
    total_tokens = (band_rows + 2 * MARGIN + 2 * PAD_R) * KEY_COLS
    side = MARGIN * band_rows
    edge = MARGIN * (band_cols + 2 * EDGE_R)
    corner = 2 * MARGIN * EDGE_R
    halo_tokens = 2 * (side + MARGIN * band_cols + corner)
    shift = before[0].shape[0] if before else 0
    vmem = pl.BlockSpec(memory_space=pltpu.VMEM)
    shapes = [
        (count, tokens, block),
        (count + shift, 2, edge, block),
        (count + shift, 2, edge, block),
        (count, 2, tokens, block),
        (count, 2, side, block),
        (count, 2, side, block),
    ]
    return pl.pallas_call(
        functools.partial(
            attention_kernel, band_rows, band_cols, total_rows, head_width,
            len(before) + len(after), first, count, shift,
        ),
        grid=(count,),
        in_specs=[pl.BlockSpec(memory_space=pltpu.SMEM)]
        + [vmem] * (1 + len(halo))
        + [pl.BlockSpec(memory_space=pltpu.HBM)] * 3
        + [vmem] * len(before)
        + [pl.BlockSpec(memory_space=pl.ANY)] * len(after),
        out_specs=[vmem] * len(shapes),
        out_shape=[jax.ShapeDtypeStruct(s, BF) for s in shapes],
        scratch_shapes=[
            pltpu.VMEM((halo_tokens, width), BF),
            pltpu.VMEM((block // LANES, (band_rows + 2 * MARGIN) * HALO_COLS, LANES), F32),
            pltpu.VMEM((tokens, block), BF),
            pltpu.VMEM((region_tokens, block), BF),
            pltpu.VMEM((region_tokens, block), BF),
            pltpu.VMEM((block // LANES, total_tokens, LANES), F32),
            pltpu.VMEM((block // LANES, total_tokens, LANES), F32),
            pltpu.VMEM((count, 4, tokens, block), BF),
            pltpu.VMEM((count, 2, width, block), BF),
            pltpu.SemaphoreType.DMA((count, 4)),
            pltpu.SemaphoreType.DMA((count, 2)),
        ],
        compiler_params=pltpu.CompilerParams(
            dimension_semantics=("arbitrary",), vmem_limit_bytes=ATTENTION_MIB * MIB
        ),
        cost_estimate=pl.CostEstimate(
            flops=count * 14 * 10**9, bytes_accessed=count * 8 * MIB, transcendentals=count * 10**6
        ),
    )(place, masks, *halo, qkv, grad_out, w_qkv, *before, *after)


def on_chip(kernel, out_shape, operands, after=(), scratch=(), flops=10**5, place=()):
    count = len(operands) + len(place)

    def run(*refs):
        kernel(*refs[:count], *refs[count + len(after) :])

    return pl.pallas_call(
        run,
        in_specs=[pl.BlockSpec(memory_space=pltpu.SMEM)] * len(place)
        + [pl.BlockSpec(memory_space=pltpu.VMEM)] * len(operands)
        + [pl.BlockSpec(memory_space=pl.ANY)] * len(after),
        out_specs=[pl.BlockSpec(memory_space=pltpu.VMEM)] * len(out_shape),
        out_shape=[jax.ShapeDtypeStruct(s, d) for s, d in out_shape],
        scratch_shapes=list(scratch),
        compiler_params=pltpu.CompilerParams(vmem_limit_bytes=24 * MIB),
        cost_estimate=pl.CostEstimate(flops=flops, bytes_accessed=10**4, transcendentals=0),
    )(*place, *operands, *after)


def lanes_of(width):
    return [(i, slice(i * LANES, (i + 1) * LANES)) for i in range(width // LANES)]


def project(own, w_qkv, after):
    tokens, width = own.shape
    columns = w_qkv.shape[1]
    block = 4 * LANES

    def kernel(own_ref, w_ref, *refs):
        refs[-1][...] = dot(own_ref[...], w_ref[...]).astype(BF)

    return pl.pallas_call(
        kernel,
        grid=(columns // block,),
        in_specs=[
            pl.BlockSpec((tokens, width), lambda g: (0, 0)),
            pl.BlockSpec((width, block), lambda g: (0, g)),
        ]
        + [pl.BlockSpec(memory_space=pl.ANY)] * len(after),
        out_specs=pl.BlockSpec((tokens, block), lambda g: (0, g)),
        out_shape=jax.ShapeDtypeStruct((tokens, columns), BF),
        compiler_params=pltpu.CompilerParams(vmem_limit_bytes=24 * MIB),
        cost_estimate=pl.CostEstimate(flops=10**9, bytes_accessed=MIB, transcendentals=0),
    )(own, w_qkv, *after)


def input_grads(columns, w_qkv, after):
    tokens = columns[0].shape[-2]
    width, total = w_qkv.shape
    count = len(columns)
    pieces = list(pieces_of(columns))
    steps = len(pieces) // 2

    def kernel(*refs):
        w_ref, (out_ref, done_ref, acc_ref) = refs[count], refs[-3:]
        for step in range(steps):

            @pl.when(pl.program_id(0) == step)
            def _():
                both = [piece(refs, *where) for where in pieces[2 * step : 2 * step + 2]]
                product = dot(jnp.concatenate(both, axis=1), w_ref[...], NT)
                if step == 0:
                    acc_ref[...] = product
                elif step < steps - 1:
                    acc_ref[...] += product
                else:
                    out_ref[...] = (acc_ref[...] + product).astype(BF)
                    done_ref[...] = jnp.zeros_like(done_ref)

    return pl.pallas_call(
        kernel,
        grid=(steps,),
        in_specs=[pl.BlockSpec(memory_space=pltpu.VMEM)] * count
        + [pl.BlockSpec((width, total // steps), lambda g: (0, g))]
        + [pl.BlockSpec(memory_space=pl.ANY)] * len(after),
        out_specs=[
            pl.BlockSpec((tokens, width), lambda g: (0, 0)),
            pl.BlockSpec((8, LANES), lambda g: (0, 0)),
        ],
        out_shape=[
            jax.ShapeDtypeStruct((tokens, width), BF),
            jax.ShapeDtypeStruct((8, LANES), F32),
        ],
        scratch_shapes=[pltpu.VMEM((tokens, width), F32)],
        compiler_params=pltpu.CompilerParams(vmem_limit_bytes=24 * MIB),
        cost_estimate=pl.CostEstimate(flops=4 * 10**9, bytes_accessed=MIB, transcendentals=0),
    )(*columns, w_qkv, *after)


def row_blocks(place, own, orders, after):
    tokens, width = own.shape
    devices = len(orders[0])
    size = width // devices
    step = max(1, 16 // size)

    def kernel(place_ref, own_ref, low_ref, high_ref, wide_ref):
        for at in range(0, width, 2 * LANES):
            wide_ref[at : at + 2 * LANES, :] = own_ref[:, at : at + 2 * LANES].astype(F32).T
        even = place_ref[1] == 0
        me = place_ref[2]
        for j in range(0, devices, step):
            rows = []
            for k in range(j, j + step):
                owner = me ^ jnp.where(even, int(orders[0][k]), int(orders[1][k]))
                rows.append(wide_ref[pl.ds(pl.multiple_of(owner * size, size), size), :])
            half, base = divmod(j * size, width // 2)
            block = rows[0] if step == 1 else jnp.concatenate(rows, axis=0)
            (low_ref, high_ref)[half][base : base + step * size, :] = block.astype(BF)

    out = ((width // 2, tokens), BF)
    scratch = [pltpu.VMEM((width, tokens), F32)]
    return on_chip(kernel, [out, out], [own], after=after, scratch=scratch, place=[place])


def pack_sides(own, band_rows, band_cols):
    tokens, width = own.shape

    def kernel(own_ref, last_ref, first_ref, wide_ref):
        for lane, at in lanes_of(width):
            wide_ref[lane] = own_ref[:, at].astype(F32)
            for col in range(MARGIN):
                here = slice(col * band_rows, (col + 1) * band_rows)
                last = pl.ds(band_cols - MARGIN + col, band_rows, stride=band_cols)
                last_ref[here, at] = wide_ref[lane, last, :].astype(BF)
                first = pl.ds(col, band_rows, stride=band_cols)
                first_ref[here, at] = wide_ref[lane, first, :].astype(BF)

    out = ((MARGIN * band_rows, width), BF)
    scratch = [pltpu.VMEM((width // LANES, tokens, LANES), F32)]
    return on_chip(kernel, [out, out], [own], scratch=scratch)


def pack_rows(place, own, band_cols, after):
    tokens, width = own.shape
    edge = MARGIN * band_cols

    def kernel(place_ref, own_ref, out_a, out_b):
        even = place_ref[1] == 0
        last, first = own_ref[tokens - edge :, :], own_ref[:edge, :]
        out_a[...] = jnp.where(even, last, first)
        out_b[...] = jnp.where(even, first, last)

    out = ((edge, width), BF)
    return on_chip(kernel, [out, out], [own], after=after, place=[place])


def pack_corners(place, left, right, band_rows, after):
    width = left.shape[1]

    def kernel(place_ref, left_ref, right_ref, out_a, out_b):
        even = place_ref[1] == 0
        for side, side_ref in enumerate((left_ref, right_ref)):
            for col in range(0, MARGIN, 2):
                base = (side * MARGIN + col) * EDGE_R
                last, first = (
                    jnp.concatenate(
                        [
                            side_ref[at : at + EDGE_R, :].astype(F32)
                            for at in (start, start + band_rows)
                        ]
                    )
                    for start in ((col + 1) * band_rows - EDGE_R, col * band_rows)
                )
                here = slice(base, base + 2 * EDGE_R)
                out_a[here, :] = jnp.where(even, last, first).astype(BF)
                out_b[here, :] = jnp.where(even, first, last).astype(BF)

    out = ((2 * MARGIN * EDGE_R, width), BF)
    return on_chip(kernel, [out, out], [left, right], after=after, place=[place])


def merge_sides(place, lefts, rights, rim_a, rim_b, band_rows, band_cols, after=()):
    edge = MARGIN * band_cols
    calls = len(lefts)
    slots = rim_a.shape[0]
    each = slots // calls

    def kernel(place_ref, *refs):
        sides = refs[:calls], refs[calls : 2 * calls]
        a_ref, b_ref, *outs = refs[2 * calls :]
        even = place_ref[1] == 0
        for slot in range(slots):
            for part in range(2):
                for col in range(2 * MARGIN):
                    source = sides[col // MARGIN][slot // each]
                    base = (col % MARGIN) * band_rows
                    pair = slice(edge + (col // 2) * 2 * EDGE_R, edge + (col // 2 + 1) * 2 * EDGE_R)
                    odd = slice((col % 2) * EDGE_R, (col % 2 + 1) * EDGE_R)
                    rows = source[slot % each, part, base : base + band_rows, :].astype(F32)
                    from_a, from_b = (
                        ref[slot, part, pair, :].astype(F32)[odd] for ref in (a_ref, b_ref)
                    )
                    first = rows[:EDGE_R] + jnp.where(even, from_b, from_a)
                    last = rows[band_rows - EDGE_R :] + jnp.where(even, from_a, from_b)
                    outs[col // MARGIN][slot, part, base : base + band_rows, :] = jnp.concatenate(
                        [first, rows[EDGE_R : band_rows - EDGE_R], last], axis=0
                    ).astype(BF)

    out = ((slots,) + lefts[0].shape[1:], BF)
    return on_chip(kernel, [out, out], [*lefts, *rights, rim_a, rim_b], after, place=[place])


def finish(place, mids, rim_a, rim_b, left, right, parts, band_rows, band_cols, after, flops):
    calls = len(mids)
    slots, _, _, block = rim_a.shape
    each = slots // calls
    edge = MARGIN * band_cols
    tokens = band_rows * band_cols

    def kernel(place_ref, *refs):
        a_ref, b_ref, left_ref, right_ref, *outs, acc_ref = refs[calls:]
        even = place_ref[1] == 0
        for out_ref, part in zip(outs, parts):
            for slot in range(slots):
                for lane, at in lanes_of(block):
                    acc_ref[lane] = refs[slot // each][slot % each, part, :, at].astype(F32)
                    from_a, from_b = (
                        r[slot, part, :edge, at].astype(F32) for r in (a_ref, b_ref)
                    )
                    acc_ref[lane, :edge, :] += jnp.where(even, from_b, from_a)
                    acc_ref[lane, tokens - edge :, :] += jnp.where(even, from_a, from_b)
                    for col in range(MARGIN):
                        here = slice(col * band_rows, (col + 1) * band_rows)
                        first = pl.ds(col, band_rows, stride=band_cols)
                        last = pl.ds(band_cols - MARGIN + col, band_rows, stride=band_cols)
                        acc_ref[lane, first, :] += left_ref[slot, part, here, at].astype(F32)
                        acc_ref[lane, last, :] += right_ref[slot, part, here, at].astype(F32)
                    start = slot * block + lane * LANES
                    out_ref[:, start : start + LANES] = acc_ref[lane].astype(BF)

    out = [((tokens, slots * block), BF)] * len(parts)
    scratch = [pltpu.VMEM((block // LANES, tokens, LANES), F32)]
    operands = [*mids, rim_a, rim_b, left, right]
    return on_chip(kernel, out, operands, after, scratch, flops, [place])


def pieces_of(arrays):
    for i, array in enumerate(arrays):
        slots = range(array.shape[0]) if array.ndim == 3 else [None]
        for slot in slots:
            for start in range(0, array.shape[-1], 2 * LANES):
                yield i, slot, start


def piece(refs, i, slot, start):
    here = slice(start, start + 2 * LANES)
    return refs[i][:, here] if slot is None else refs[i][slot, :, here]


def grad_rows(rows, columns, scale, kind, after=()):
    features, count = rows.shape[0], len(columns)
    pieces = list(pieces_of(columns))

    def kernel(rows_ref, *refs):
        for at, where in enumerate(pieces):
            part = dot(rows_ref[...], piece(refs, *where))
            here = slice(at * 2 * LANES, (at + 1) * 2 * LANES)
            refs[count][:, here] = (part * scale).astype(kind)

    out = [((features, len(pieces) * 2 * LANES), kind)]
    return on_chip(kernel, out, [rows, *columns], after)[0]


def add_split(keep, received, after=()):
    half, columns = keep.shape[0] // 2, keep.shape[1]

    def kernel(keep_ref, received_ref, sums_ref, send_ref):
        sums_ref[...] = keep_ref[:half, :] + received_ref[:half, :].astype(F32)
        send_ref[...] = (keep_ref[half:, :] + received_ref[half:, :].astype(F32)).astype(BF)

    return on_chip(kernel, [((half, columns), F32), ((half, columns), BF)], [keep, received], after)


def gather_sums(groups, places, width):
    flat = [array for group in groups for array in group]

    def kernel(*refs):
        out_ref = refs[-1]
        for i, moves in enumerate(places):
            keep_ref, received_ref = refs[2 * i : 2 * i + 2]
            for source, size, target in moves:
                here = slice(source, source + size)
                total = keep_ref[:, here] + received_ref[:, here].astype(F32)
                out_ref[:, target : target + size] = total

    return on_chip(kernel, [((flat[0].shape[0], width), F32)], flat)[0]


def shifted(array, axis, by, wrap):
    size = lax.axis_size(axis)
    route = [(i, (i + by) % size) for i in range(size) if wrap or 0 <= i + by < size]
    return lax.ppermute(array, axis, route)


def swapped(array_a, array_b, axis):
    size = lax.axis_size(axis)
    pairs = [(i, i + 1) for i in range(size - 1)]
    route = lambda chosen: chosen + [(j, i) for i, j in chosen]
    return [
        lax.ppermute(array, axis, route(pairs[offset::2]))
        for array, offset in ((array_a, 0), (array_b, 1))
    ]


def exchanged(array, axis, flip):
    return lax.ppermute(array, axis, [(i, i ^ flip) for i in range(lax.axis_size(axis))])


def bits_of(axis):
    return [(axis, 1 << b) for b in range((lax.axis_size(axis) - 1).bit_length())]


def reduce_stages():
    first, *lat_bits = bits_of("lat")
    bits = bits_of("dp") + lat_bits
    return first, list(zip(bits, reversed(bits))) + [(bit, bit) for bit in bits_of("lon")]


def feature_orders(first, stages):
    n_lon, n_lat = lax.axis_size("lon"), lax.axis_size("lat")
    unit = {"lon": 1, "lat": n_lon, "dp": n_lon * n_lat}
    lower = []
    for kind in range(2):
        order = np.zeros(1, np.int64)
        for stage in reversed(stages):
            axis, bit = stage[kind]
            order = np.concatenate([order, order + unit[axis] * bit])
        lower.append(order)
    flip = unit[first[0]] * first[1]
    return [np.concatenate([lower[kind], lower[1 - kind] ^ flip]) for kind in range(2)]


def exchanged_stage(array, stage):
    if stage[0] == stage[1]:
        return exchanged(array, *stage[0])
    n_lat, n_dp = lax.axis_size("lat"), lax.axis_size("dp")
    route = []
    for i in range(n_dp * n_lat):
        axis, bit = stage[i % n_lat % 2]
        route.append((i, i ^ (bit * n_lat if axis == "dp" else bit)))
    return lax.ppermute(array, ("dp", "lat"), route)


def body(inputs, grad_out, w_qkv):
    _, band_rows, band_cols, width = inputs.shape
    n_lat, n_lon, n_dp = lax.axis_size("lat"), lax.axis_size("lon"), lax.axis_size("dp")
    band_start = lax.axis_index("lat") * band_rows
    total_rows = band_rows * n_lat
    tokens = band_rows * band_cols
    slots = HEADS // GROUP // 2
    shape = (band_rows, band_cols, total_rows)
    own = inputs.reshape(tokens, width)
    flat_grad = grad_out.reshape(tokens, width)

    last_cols, first_cols = pack_sides(own, band_rows, band_cols)
    left = shifted(last_cols, "lon", 1, True)
    right = shifted(first_cols, "lon", -1, True)
    me = (lax.axis_index("dp") * n_lat + lax.axis_index("lat")) * n_lon + lax.axis_index("lon")
    start = jnp.stack([band_start, lax.axis_index("lat") % 2, me])
    rim_rows = swapped(*pack_rows(start, own, band_cols, [last_cols]), "lat")

    masks = window_masks(start, band_rows, band_cols, total_rows)
    qkv = project(own, w_qkv, [last_cols])
    first, stages = reduce_stages()
    half = width // 2
    rows_keep, rows_send = row_blocks(start, own, feature_orders(first, stages), [last_cols])
    corners = pack_corners(start, left, right, band_rows, [masks, qkv, rows_keep, rows_send])
    halo = (left, right, *rim_rows, *swapped(*corners, "lat"))
    scale = float(tokens * n_dp * n_lat * n_lon) ** -0.5

    attend = lambda first, count, before, after: attention_grads(
        first, count, start, masks, halo, qkv, flat_grad, w_qkv, shape, before, after
    )

    def return_sides(calls, rims, after):
        to_left, to_right = merge_sides(
            start, [c[4] for c in calls], [c[5] for c in calls], *rims, band_rows, band_cols, after
        )
        from_right = shifted(to_left, "lon", -1, True)
        from_left = shifted(to_right, "lon", 1, True)
        return to_left, from_left, from_right

    def finished(calls, rims, sides, parts, after, flops):
        mids = [c[3] for c in calls]
        return finish(start, mids, *rims, *sides, parts, band_rows, band_cols, after, flops)

    groups = HEADS // GROUP
    one = attend(0, slots, [], [])
    rims_1 = swapped(one[1], one[2], "lat")
    two = attend(slots, groups - slots - 1, [], [one[0]])
    sent, *sides_1 = return_sides([one], rims_1, [two[0]])
    three = attend(groups - 1, 1, [two[1], two[2]], [sent])
    rims_2 = swapped(three[1], three[2], "lat")
    dq = [one[0], two[0], three[0]]

    dk_1, dv_1 = finished([one], rims_1, sides_1, (0, 1), [three[0]], 2 * 10**9)
    sent, *sides_2 = return_sides([two, three], rims_2, [dk_1])
    send = grad_rows(rows_send, [*dq, dk_1, dv_1], scale, BF, after=[sent])
    received = exchanged(send, *first)
    keep = grad_rows(rows_keep, [*dq, dk_1, dv_1], scale, F32, after=[send])
    keep, send = add_split(keep, received)

    (dk_2,) = finished([two, three], rims_2, sides_2, (0,), [keep], FINISH_FLOPS)
    received = exchanged_stage(send, stages[0])
    keep, send = add_split(keep, received, [dk_2])
    received = exchanged_stage(send, stages[1])
    (dv_2,) = finished([two, three], rims_2, sides_2, (1,), [keep], 10**5)
    send_2 = grad_rows(rows_send, [dk_2, dv_2], scale, BF)
    received_2 = exchanged(send_2, *first)
    keep_2 = grad_rows(rows_keep, [dk_2, dv_2], scale, F32, after=[send_2])
    keep_2, send_2 = add_split(keep_2, received_2)
    received_2 = exchanged_stage(send_2, stages[0])
    grad_inputs, done = input_grads([*dq, dk_1, dk_2, dv_1, dv_2], w_qkv, [send_2])
    keep, send = add_split(keep, received, [done])
    for i in range(2, len(stages)):
        received = exchanged_stage(send, stages[i])
        keep_2, send_2 = add_split(keep_2, received_2, [keep])
        received_2 = exchanged_stage(send_2, stages[i - 1])
        if i + 1 < len(stages):
            keep, send = add_split(keep, received, [keep_2])
    keep_2, send_2 = add_split(keep_2, received_2)
    received_2 = exchanged_stage(send_2, stages[-1])
    groups = [(keep, received), (keep_2, received_2)]
    places = [
        [(0, width, 0), (width, half, width), (width + half, half, 2 * width)],
        [(0, half, width + half), (half, half, 2 * width + half)],
    ]
    grad_w = gather_sums(groups, places, 3 * width)
    return (grad_inputs.reshape(inputs.shape), grad_w)


def solution(mesh):
    in_specs = (P("dp", "lat", "lon", None), P("dp", "lat", "lon", None), P())
    out_specs = (P("dp", "lat", "lon", None), P(("dp", "lat", "lon"), None))
    return jax.shard_map(body, mesh=mesh, in_specs=in_specs, out_specs=out_specs, check_vma=False)
```

profile of v0, /device:TPU:0, one launch (start us, length us, event | category | flops | bytes accessed | tf_op | source)
XLA Modules:
  0.0 147.5 jit_solution(18079226163206349202)
XLA Ops:
  3.4 5.0 %collective-permute-start.1 = (bf16[192,1024]{1,0:T(8,128)(2,1)}, bf16[192,1024]{1,0:T(8,128)(2,1)S(1)}, u32[]{:S(2)}, u32[]{:S(2)}) collective-permute-start(bf16[192,1024]{1,0:T(8,128)(2,1)} %get-tuple-element.53), channel_id=1, source_target_pairs={{0,3},{1,0},{2,1},{3,2},{4,7},{5,4},{6,5},{7,6},{8,11},{9,8},{10,9... | collective-permute-start | bytes 1179656 | tf_op jit(solution)/shard_map/ppermute | solution.py:602
  13.4 4.0 %shard_map.50.refs_3_.refs_1_ = bf16[8,512,128]{2,1,0:T(8,128)(2,1)} custom-call(s32[3]{0:T(128)} %copy-done.5), custom_call_target="tpu_custom_call" | custom-call | flops 10000000 | bytes 2097152 | tf_op jit(solution)/shard_map/pallas_call | solution.py:69
  17.4 2.8 %copy-done.3 = bf16[1024,3072]{1,0:T(8,128)(2,1)S(1)} copy-done((bf16[1024,3072]{1,0:T(8,128)(2,1)S(1)}, bf16[1024,3072]{1,0:T(8,128)(2,1)}, u32[]{:S(2)}) %copy-start.3) | copy-done | bytes 6291480
  20.2 4.9 %shard_map.53.refs_4_.refs_8_ = bf16[512,3072]{1,0:T(8,128)(2,1)S(1)} custom-call(bf16[512,1024]{1,0:T(8,128)(2,1)S(1)} %bitcast.9, bf16[1024,3072]{1,0:T(8,128)(2,1)S(1)} %copy-done.3, bf16[192,1024]{1,0:T(8,128)(2,1)S(1)} %get-tuple-element.52.refs_2_.refs_0_), custom_call_target="tpu_custom_call" | custom-call | flops 1000000000 | bytes 1048576 | tf_op jit(solution)/shard_map/pallas_call | solution.py:342
  29.1 17.3 %shard_map.56 = (bf16[2,512,256]{2,1,0:T(8,128)(2,1)S(1)}, bf16[2,2,192,256]{3,2,1,0:T(8,128)(2,1)S(1)}, bf16[2,2,192,256]{3,2,1,0:T(8,128)(2,1)S(1)}, bf16[2,2,...) custom-call(s32[3]{0:T(128)S(1)} %copy-done.6, ...), custom_call_target="tpu_custom_call" | custom-call | flops 28000000000 | bytes 16777216 | tf_op jit(solution)/shard_map/pallas_call | solution.py:276
  46.4 6.0 %collective-permute-start.6 = (bf16[2,2,192,256]{3,2,1,0:T(8,128)(2,1)S(1)}, bf16[2,2,192,256]{3,2,1,0:T(8,128)(2,1)S(1)}, u32[]{:S(2)}, u32[]{:S(2)}) collective-permute-start(bf16[2,2,192,256]{3,2,1,0:T(8,128)(2,1)S(1)} %get-tuple-element.66), channel_id=1, source_target_pairs={{0,4},{8,12},{4,0},{12,8},{1,5},{9,13},{5,1},{13,9},{2,6},{10,14},... | collective-permute-start | bytes 1179656 | tf_op jit(solution)/shard_map/ppermute | solution.py:610
  53.3 9.2 %shard_map.57 = (bf16[1,512,256]{2,1,0:T(8,128)(2,1)S(1)}, bf16[1,2,192,256]{3,2,1,0:T(8,128)(2,1)S(1)}, bf16[1,2,192,256]{3,2,1,0:T(8,128)(2,1)S(1)}, bf16[1,2,...) custom-call(s32[3]{0:T(128)S(1)} %copy-done.6, ...), custom_call_target="tpu_custom_call" | custom-call | flops 14000000000 | bytes 8388608 | tf_op jit(solution)/shard_map/pallas_call | solution.py:276
  64.3 2.8 %collective-permute-start.9 = (bf16[2,2,192,256]{3,2,1,0:T(8,128)(2,1)S(1)}, bf16[2,2,192,256]{3,2,1,0:T(8,128)(2,1)S(1)}, u32[]{:S(2)}, u32[]{:S(2)}) collective-permute-start(bf16[2,2,192,256]{3,2,1,0:T(8,128)(2,1)S(1)} %get-tuple-element.68.refs_13_), channel_id=1, source_target_pairs={{0,3},{1,0},{2,1},{3,2},{4,7},{5,4},{6,5},{7,6},{8,11},{9,8},{10,9... | collective-permute-start | bytes 1179656 | tf_op jit(solution)/shard_map/ppermute | solution.py:602
  67.1 9.2 %shard_map.59 = (bf16[1,512,256]{2,1,0:T(8,128)(2,1)S(1)}, bf16[2,2,192,256]{3,2,1,0:T(8,128)(2,1)S(1)}, bf16[2,2,192,256]{3,2,1,0:T(8,128)(2,1)S(1)}, bf16[1,2,...) custom-call(s32[3]{0:T(128)S(1)} %copy-done.6, ...), custom_call_target="tpu_custom_call" | custom-call | flops 14000000000 | bytes 8388608 | tf_op jit(solution)/shard_map/pallas_call | solution.py:276
  76.3 1.7 %collective-permute-start.10 = (bf16[2,2,192,256]{3,2,1,0:T(8,128)(2,1)S(1)}, bf16[2,2,192,256]{3,2,1,0:T(8,128)(2,1)S(1)}, u32[]{:S(2)}, u32[]{:S(2)}) collective-permute-start(bf16[2,2,192,256]{3,2,1,0:T(8,128)(2,1)S(1)} %get-tuple-element.75), channel_id=1, source_target_pairs={{0,4},{8,12},{4,0},{12,8},{1,5},{9,13},{5,1},{13,9},{2,6},{10,14},... | collective-permute-start | bytes 1179656 | tf_op jit(solution)/shard_map/ppermute | solution.py:610
  78.9 5.0 %collective-permute-done.9.refs_5_ = bf16[2,2,192,256]{3,2,1,0:T(8,128)(2,1)S(1)} collective-permute-done((bf16[2,2,192,256]{3,2,1,0:T(8,128)(2,1)S(1)}, bf16[2,2,192,256]{3,2,1,0:T(8,128)(2,1)S(1)}, u32[]{:S(2)}, u32[]{:S(2)}) %collective-permute-start.9) | collective-permute-done | bytes 393248 | tf_op jit(solution)/shard_map/ppermute | solution.py:602
  83.9 1.9 %shard_map.60 = (bf16[512,512]{1,0:T(8,128)(2,1)S(1)}, bf16[512,512]{1,0:T(8,128)(2,1)S(1)}) custom-call(s32[3]{0:T(128)S(1)} %copy-done.6, bf16[2,2,512,256]{3,2,1,0:T(8,128)(2,1)S(1)} %get-tuple-element.70.refs_1_, bf16[2,2,192,256]{3,2,1,0:T(8,128)(2,1)S(1)} %collective-permute-done.6.refs_3_.refs_2_, ...), custom_call_target="tpu_custom_call" | custom-call | flops 2000000000 | bytes 10000 | tf_op jit(solution)/shard_map/pallas_call | solution.py:317
  90.0 2.9 %collective-permute-start.13 = (bf16[2,2,192,256]{3,2,1,0:T(8,128)(2,1)S(1)}, bf16[2,2,192,256]{3,2,1,0:T(8,128)(2,1)S(1)}, u32[]{:S(2)}, u32[]{:S(2)}) collective-permute-start(bf16[2,2,192,256]{3,2,1,0:T(8,128)(2,1)S(1)} %get-tuple-element.82.refs_6_), channel_id=1, source_target_pairs={{0,3},{1,0},{2,1},{3,2},{4,7},{5,4},{6,5},{7,6},{8,11},{9,8},{10,9... | collective-permute-start | bytes 1179656 | tf_op jit(solution)/shard_map/ppermute | solution.py:602
  94.6 1.6 %collective-permute-start.15 = (bf16[256,2048]{1,0:T(8,128)(2,1)S(1)}, bf16[256,2048]{1,0:T(8,128)(2,1)S(1)}, u32[]{:S(2)}, u32[]{:S(2)}) collective-permute-start(bf16[256,2048]{1,0:T(8,128)(2,1)S(1)} %get-tuple-element.85), channel_id=1, source_target_pairs={{0,16},{4,12},{8,24},{12,4},{16,0},{20,28},{24,8},{28,20},{1,17},{... | collective-permute-start | bytes 3145736 | tf_op jit(solution)/shard_map/ppermute | solution.py:651
  96.2 6.7 %collective-permute-done.12.refs_5_ = bf16[2,2,192,256]{3,2,1,0:T(8,128)(2,1)S(1)} collective-permute-done((bf16[2,2,192,256]{3,2,1,0:T(8,128)(2,1)S(1)}, bf16[2,2,192,256]{3,2,1,0:T(8,128)(2,1)S(1)}, u32[]{:S(2)}, u32[]{:S(2)}) %collective-permute-start.12) | collective-permute-done | bytes 393248 | tf_op jit(solution)/shard_map/ppermute | solution.py:602
  102.9 6.7 %collective-permute-done.13.refs_6_ = bf16[2,2,192,256]{3,2,1,0:T(8,128)(2,1)S(1)} collective-permute-done((bf16[2,2,192,256]{3,2,1,0:T(8,128)(2,1)S(1)}, bf16[2,2,192,256]{3,2,1,0:T(8,128)(2,1)S(1)}, u32[]{:S(2)}, u32[]{:S(2)}) %collective-permute-start.13) | collective-permute-done | bytes 393248 | tf_op jit(solution)/shard_map/ppermute | solution.py:602
  115.9 1.6 %collective-permute-start.19 = (bf16[256,1024]{1,0:T(8,128)(2,1)S(1)}, bf16[256,1024]{1,0:T(8,128)(2,1)S(1)}, u32[]{:S(2)}, u32[]{:S(2)}) collective-permute-start(bf16[256,1024]{1,0:T(8,128)(2,1)S(1)} %get-tuple-element.87.refs_8_), channel_id=1, source_target_pairs={{0,16},{4,12},{8,24},{12,4},{16,0},{20,28},{24,8},{28,20},{1,17},{... | collective-permute-start | bytes 1572872 | tf_op jit(solution)/shard_map/ppermute | solution.py:651
  117.5 6.1 %shard_map.71 = (bf16[512,1024]{1,0:T(8,128)(2,1)}, f32[8,128]{1,0:T(8,128)S(1)}) custom-call(bf16[2,512,256]{2,1,0:T(8,128)(2,1)S(1)} %get-tuple-element.60.refs_11_.refs_1_.refs_0_, bf16[1,512,256]{2,1,0:T(8,128)(2,1)S(1)} %get-tuple-element.61.refs_5_.refs_2_.refs_1_, bf16[1,512,256]{2,1,0:T(8,128)(2,1)S(1)} %get-tuple-element.69.refs_6_.refs_3_.refs_2_, ...), custom_call_target="tpu_custom_call" | custom-call | flops 4000000000 | bytes 1048576 | tf_op jit(solution)/shard_map/pallas_call | solution.py:380
  123.6 2.3 %collective-permute-done.17.refs_1_ = bf16[128,2048]{1,0:T(8,128)(2,1)S(1)} collective-permute-done((bf16[128,2048]{1,0:T(8,128)(2,1)S(1)}, bf16[128,2048]{1,0:T(8,128)(2,1)S(1)}, u32[]{:S(2)}, u32[]{:S(2)}) %collective-permute-start.17) | collective-permute-done | bytes 524320 | tf_op jit(solution)/shard_map/ppermute | solution.py:651
  128.3 4.2 %collective-permute-done.18.refs_1_ = bf16[64,2048]{1,0:T(8,128)(2,1)S(1)} collective-permute-done((bf16[64,2048]{1,0:T(8,128)(2,1)S(1)}, bf16[64,2048]{1,0:T(8,128)(2,1)S(1)}, u32[]{:S(2)}, u32[]{:S(2)}) %collective-permute-start.18) | collective-permute-done | bytes 262176 | tf_op jit(solution)/shard_map/ppermute | solution.py:616
  134.8 1.9 %collective-permute-start.20 = (bf16[32,2048]{1,0:T(8,128)(2,1)S(1)}, bf16[32,2048]{1,0:T(8,128)(2,1)S(1)}, u32[]{:S(2)}, u32[]{:S(2)}) collective-permute-start(bf16[32,2048]{1,0:T(8,128)(2,1)S(1)} %get-tuple-element.96), channel_id=1, source_target_pairs={{0,2},{1,3},{2,0},{3,1},{4,6},{5,7},{6,4},{7,5},{8,10},{9,11},{10,... | collective-permute-start | bytes 393224 | tf_op jit(solution)/shard_map/ppermute | solution.py:616
  136.7 4.7 %collective-permute-done.22.refs_1_ = bf16[64,1024]{1,0:T(8,128)(2,1)S(1)} collective-permute-done((bf16[64,1024]{1,0:T(8,128)(2,1)S(1)}, bf16[64,1024]{1,0:T(8,128)(2,1)S(1)}, u32[]{:S(2)}, u32[]{:S(2)}) %collective-permute-start.22) | collective-permute-done | bytes 131104 | tf_op jit(solution)/shard_map/ppermute | solution.py:616
  141.9 2.1 %collective-permute-done.20.refs_1_ = bf16[32,2048]{1,0:T(8,128)(2,1)S(1)} collective-permute-done((bf16[32,2048]{1,0:T(8,128)(2,1)S(1)}, bf16[32,2048]{1,0:T(8,128)(2,1)S(1)}, u32[]{:S(2)}, u32[]{:S(2)}) %collective-permute-start.20) | collective-permute-done | bytes 131104 | tf_op jit(solution)/shard_map/ppermute | solution.py:616
  144.0 2.8 %collective-permute-done.23.refs_3_ = bf16[32,1024]{1,0:T(8,128)(2,1)S(1)} collective-permute-done((bf16[32,1024]{1,0:T(8,128)(2,1)S(1)}, bf16[32,1024]{1,0:T(8,128)(2,1)S(1)}, u32[]{:S(2)}, u32[]{:S(2)}) %collective-permute-start.23) | collective-permute-done | bytes 65568 | tf_op jit(solution)/shard_map/ppermute | solution.py:616
  (69 shorter events, 33.2 us)
Async XLA Ops:
  3.4 21.7 %collective-permute-start.1 = (bf16[192,1024]{1,0:T(8,128)(2,1)}, bf16[192,1024]{1,0:T(8,128)(2,1)S(1)}, u32[]{:S(2)}, u32[]{:S(2)}) collective-permute-start(bf16[192,1024]{1,0:T(8,128)(2,1)} %get-tuple-element.53), channel_id=1, source_target_pairs={{0,3},{1,0},{2,1},{3,2},{4,7},{5,4},{6,5},{7,6},{8,11},{9,8},{10,9... | collective-permute-start | bytes 1179656 | tf_op jit(solution)/shard_map/ppermute | solution.py:602
  8.4 17.9 %collective-permute-start = (bf16[192,1024]{1,0:T(8,128)(2,1)S(1)}, bf16[192,1024]{1,0:T(8,128)(2,1)S(1)}, u32[]{:S(2)}, u32[]{:S(2)}) collective-permute-start(bf16[192,1024]{1,0:T(8,128)(2,1)S(1)} %get-tuple-element.52.refs_2_.refs_0_), channel_id=1, source_target_pairs={{0,1},{1,2},{2,3},{3,0},{4,5},{5,6},{6,7},{7,4},{8,9},{9,10},{10,1... | collective-permute-start | bytes 1179656 | tf_op jit(solution)/shard_map/ppermute | solution.py:602
  11.0 17.7 %collective-permute-start.2 = (bf16[96,1024]{1,0:T(8,128)(2,1)}, bf16[96,1024]{1,0:T(8,128)(2,1)S(1)}, u32[]{:S(2)}, u32[]{:S(2)}) collective-permute-start(bf16[96,1024]{1,0:T(8,128)(2,1)} %get-tuple-element.54), channel_id=1, source_target_pairs={{0,4},{8,12},{4,0},{12,8},{1,5},{9,13},{5,1},{13,9},{2,6},{10,14},... | collective-permute-start | bytes 589832 | tf_op jit(solution)/shard_map/ppermute | solution.py:610
  11.0 17.7 %collective-permute-start.3 = (bf16[96,1024]{1,0:T(8,128)(2,1)}, bf16[96,1024]{1,0:T(8,128)(2,1)}, u32[]{:S(2)}, u32[]{:S(2)}) collective-permute-start(bf16[96,1024]{1,0:T(8,128)(2,1)} %get-tuple-element.55), channel_id=1, source_target_pairs={{4,8},{8,4},{5,9},{9,5},{6,10},{10,6},{7,11},{11,7},{20,24},{24,20... | collective-permute-start | bytes 589832 | tf_op jit(solution)/shard_map/ppermute | solution.py:610
  27.0 2.1 %collective-permute-start.4 = (bf16[96,1024]{1,0:T(8,128)(2,1)S(1)}, bf16[96,1024]{1,0:T(8,128)(2,1)S(1)}, u32[]{:S(2)}, u32[]{:S(2)}) collective-permute-start(bf16[96,1024]{1,0:T(8,128)(2,1)S(1)} %get-tuple-element.58), channel_id=1, source_target_pairs={{0,4},{8,12},{4,0},{12,8},{1,5},{9,13},{5,1},{13,9},{2,6},{10,14},... | collective-permute-start | bytes 589832 | tf_op jit(solution)/shard_map/ppermute | solution.py:610
  28.0 1.1 collective-permute-start.5
  46.4 16.1 %collective-permute-start.6 = (bf16[2,2,192,256]{3,2,1,0:T(8,128)(2,1)S(1)}, bf16[2,2,192,256]{3,2,1,0:T(8,128)(2,1)S(1)}, u32[]{:S(2)}, u32[]{:S(2)}) collective-permute-start(bf16[2,2,192,256]{3,2,1,0:T(8,128)(2,1)S(1)} %get-tuple-element.66), channel_id=1, source_target_pairs={{0,4},{8,12},{4,0},{12,8},{1,5},{9,13},{5,1},{13,9},{2,6},{10,14},... | collective-permute-start | bytes 1179656 | tf_op jit(solution)/shard_map/ppermute | solution.py:610
  52.4 10.1 %collective-permute-start.7 = (bf16[2,2,192,256]{3,2,1,0:T(8,128)(2,1)S(1)}, bf16[2,2,192,256]{3,2,1,0:T(8,128)(2,1)S(1)}, u32[]{:S(2)}, u32[]{:S(2)}) collective-permute-start(bf16[2,2,192,256]{3,2,1,0:T(8,128)(2,1)S(1)} %get-tuple-element.67), channel_id=1, source_target_pairs={{4,8},{8,4},{5,9},{9,5},{6,10},{10,6},{7,11},{11,7},{20,24},{24,20... | collective-permute-start | bytes 1179656 | tf_op jit(solution)/shard_map/ppermute | solution.py:610
  63.2 15.7 %collective-permute-start.8 = (bf16[2,2,192,256]{3,2,1,0:T(8,128)(2,1)S(1)}, bf16[2,2,192,256]{3,2,1,0:T(8,128)(2,1)S(1)}, u32[]{:S(2)}, u32[]{:S(2)}) collective-permute-start(bf16[2,2,192,256]{3,2,1,0:T(8,128)(2,1)S(1)} %get-tuple-element.71), channel_id=1, source_target_pairs={{0,1},{1,2},{2,3},{3,0},{4,5},{5,6},{6,7},{7,4},{8,9},{9,10},{10,1... | collective-permute-start | bytes 1179656 | tf_op jit(solution)/shard_map/ppermute | solution.py:602
  64.3 19.6 %collective-permute-start.9 = (bf16[2,2,192,256]{3,2,1,0:T(8,128)(2,1)S(1)}, bf16[2,2,192,256]{3,2,1,0:T(8,128)(2,1)S(1)}, u32[]{:S(2)}, u32[]{:S(2)}) collective-permute-start(bf16[2,2,192,256]{3,2,1,0:T(8,128)(2,1)S(1)} %get-tuple-element.68.refs_13_), channel_id=1, source_target_pairs={{0,3},{1,0},{2,1},{3,2},{4,7},{5,4},{6,5},{7,6},{8,11},{9,8},{10,9... | collective-permute-start | bytes 1179656 | tf_op jit(solution)/shard_map/ppermute | solution.py:602
  76.3 9.5 %collective-permute-start.10 = (bf16[2,2,192,256]{3,2,1,0:T(8,128)(2,1)S(1)}, bf16[2,2,192,256]{3,2,1,0:T(8,128)(2,1)S(1)}, u32[]{:S(2)}, u32[]{:S(2)}) collective-permute-start(bf16[2,2,192,256]{3,2,1,0:T(8,128)(2,1)S(1)} %get-tuple-element.75), channel_id=1, source_target_pairs={{0,4},{8,12},{4,0},{12,8},{1,5},{9,13},{5,1},{13,9},{2,6},{10,14},... | collective-permute-start | bytes 1179656 | tf_op jit(solution)/shard_map/ppermute | solution.py:610
  78.0 7.9 %collective-permute-start.11 = (bf16[2,2,192,256]{3,2,1,0:T(8,128)(2,1)S(1)}, bf16[2,2,192,256]{3,2,1,0:T(8,128)(2,1)S(1)}, u32[]{:S(2)}, u32[]{:S(2)}) collective-permute-start(bf16[2,2,192,256]{3,2,1,0:T(8,128)(2,1)S(1)} %get-tuple-element.76), channel_id=1, source_target_pairs={{4,8},{8,4},{5,9},{9,5},{6,10},{10,6},{7,11},{11,7},{20,24},{24,20... | collective-permute-start | bytes 1179656 | tf_op jit(solution)/shard_map/ppermute | solution.py:610
  87.8 6.4 %collective-permute-start.14 = (bf16[512,2048]{1,0:T(8,128)(2,1)S(1)}, bf16[512,2048]{1,0:T(8,128)(2,1)S(1)}, u32[]{:S(2)}, u32[]{:S(2)}) collective-permute-start(bf16[512,2048]{1,0:T(8,128)(2,1)S(1)} %shard_map.62.refs_6_), channel_id=1, source_target_pairs={{0,4},{4,0},{8,12},{12,8},{1,5},{5,1},{9,13},{13,9},{2,6},{6,2},{1... | collective-permute-start | bytes 6291464 | tf_op jit(solution)/shard_map/ppermute | solution.py:616
  89.1 13.8 %collective-permute-start.12 = (bf16[2,2,192,256]{3,2,1,0:T(8,128)(2,1)S(1)}, bf16[2,2,192,256]{3,2,1,0:T(8,128)(2,1)S(1)}, u32[]{:S(2)}, u32[]{:S(2)}) collective-permute-start(bf16[2,2,192,256]{3,2,1,0:T(8,128)(2,1)S(1)} %get-tuple-element.81), channel_id=1, source_target_pairs={{0,1},{1,2},{2,3},{3,0},{4,5},{5,6},{6,7},{7,4},{8,9},{9,10},{10,1... | collective-permute-start | bytes 1179656 | tf_op jit(solution)/shard_map/ppermute | solution.py:602
  90.0 19.6 %collective-permute-start.13 = (bf16[2,2,192,256]{3,2,1,0:T(8,128)(2,1)S(1)}, bf16[2,2,192,256]{3,2,1,0:T(8,128)(2,1)S(1)}, u32[]{:S(2)}, u32[]{:S(2)}) collective-permute-start(bf16[2,2,192,256]{3,2,1,0:T(8,128)(2,1)S(1)} %get-tuple-element.82.refs_6_), channel_id=1, source_target_pairs={{0,3},{1,0},{2,1},{3,2},{4,7},{5,4},{6,5},{7,6},{8,11},{9,8},{10,9... | collective-permute-start | bytes 1179656 | tf_op jit(solution)/shard_map/ppermute | solution.py:602
  94.6 16.2 %collective-permute-start.15 = (bf16[256,2048]{1,0:T(8,128)(2,1)S(1)}, bf16[256,2048]{1,0:T(8,128)(2,1)S(1)}, u32[]{:S(2)}, u32[]{:S(2)}) collective-permute-start(bf16[256,2048]{1,0:T(8,128)(2,1)S(1)} %get-tuple-element.85), channel_id=1, source_target_pairs={{0,16},{4,12},{8,24},{12,4},{16,0},{20,28},{24,8},{28,20},{1,17},{... | collective-permute-start | bytes 3145736 | tf_op jit(solution)/shard_map/ppermute | solution.py:651
  113.0 2.7 %collective-permute-start.16 = (bf16[512,1024]{1,0:T(8,128)(2,1)S(1)}, bf16[512,1024]{1,0:T(8,128)(2,1)S(1)}, u32[]{:S(2)}, u32[]{:S(2)}) collective-permute-start(bf16[512,1024]{1,0:T(8,128)(2,1)S(1)} %shard_map.68.refs_3_), channel_id=1, source_target_pairs={{0,4},{4,0},{8,12},{12,8},{1,5},{5,1},{9,13},{13,9},{2,6},{6,2},{1... | collective-permute-start | bytes 3145736 | tf_op jit(solution)/shard_map/ppermute | solution.py:616
  113.1 12.8 %collective-permute-start.17 = (bf16[128,2048]{1,0:T(8,128)(2,1)S(1)}, bf16[128,2048]{1,0:T(8,128)(2,1)S(1)}, u32[]{:S(2)}, u32[]{:S(2)}) collective-permute-start(bf16[128,2048]{1,0:T(8,128)(2,1)S(1)} %get-tuple-element.89), channel_id=1, source_target_pairs={{0,8},{4,20},{8,0},{12,28},{16,24},{20,4},{24,16},{28,12},{1,9},{5... | collective-permute-start | bytes 1572872 | tf_op jit(solution)/shard_map/ppermute | solution.py:651
  115.9 11.5 %collective-permute-start.19 = (bf16[256,1024]{1,0:T(8,128)(2,1)S(1)}, bf16[256,1024]{1,0:T(8,128)(2,1)S(1)}, u32[]{:S(2)}, u32[]{:S(2)}) collective-permute-start(bf16[256,1024]{1,0:T(8,128)(2,1)S(1)} %get-tuple-element.87.refs_8_), channel_id=1, source_target_pairs={{0,16},{4,12},{8,24},{12,4},{16,0},{20,28},{24,8},{28,20},{1,17},{... | collective-permute-start | bytes 1572872 | tf_op jit(solution)/shard_map/ppermute | solution.py:651
  126.0 6.5 %collective-permute-start.18 = (bf16[64,2048]{1,0:T(8,128)(2,1)S(1)}, bf16[64,2048]{1,0:T(8,128)(2,1)S(1)}, u32[]{:S(2)}, u32[]{:S(2)}) collective-permute-start(bf16[64,2048]{1,0:T(8,128)(2,1)S(1)} %get-tuple-element.92), channel_id=1, source_target_pairs={{0,1},{1,0},{2,3},{3,2},{4,5},{5,4},{6,7},{7,6},{8,9},{9,8},{10,11... | collective-permute-start | bytes 786440 | tf_op jit(solution)/shard_map/ppermute | solution.py:616
  127.5 6.4 %collective-permute-start.21 = (bf16[128,1024]{1,0:T(8,128)(2,1)S(1)}, bf16[128,1024]{1,0:T(8,128)(2,1)S(1)}, u32[]{:S(2)}, u32[]{:S(2)}) collective-permute-start(bf16[128,1024]{1,0:T(8,128)(2,1)S(1)} %get-tuple-element.97), channel_id=1, source_target_pairs={{0,8},{4,20},{8,0},{12,28},{16,24},{20,4},{24,16},{28,12},{1,9},{5... | collective-permute-start | bytes 786440 | tf_op jit(solution)/shard_map/ppermute | solution.py:651
  134.0 7.4 %collective-permute-start.22 = (bf16[64,1024]{1,0:T(8,128)(2,1)S(1)}, bf16[64,1024]{1,0:T(8,128)(2,1)S(1)}, u32[]{:S(2)}, u32[]{:S(2)}) collective-permute-start(bf16[64,1024]{1,0:T(8,128)(2,1)S(1)} %get-tuple-element.99), channel_id=1, source_target_pairs={{0,1},{1,0},{2,3},{3,2},{4,5},{5,4},{6,7},{7,6},{8,9},{9,8},{10,11... | collective-permute-start | bytes 393224 | tf_op jit(solution)/shard_map/ppermute | solution.py:616
  134.8 9.2 %collective-permute-start.20 = (bf16[32,2048]{1,0:T(8,128)(2,1)S(1)}, bf16[32,2048]{1,0:T(8,128)(2,1)S(1)}, u32[]{:S(2)}, u32[]{:S(2)}) collective-permute-start(bf16[32,2048]{1,0:T(8,128)(2,1)S(1)} %get-tuple-element.96), channel_id=1, source_target_pairs={{0,2},{1,3},{2,0},{3,1},{4,6},{5,7},{6,4},{7,5},{8,10},{9,11},{10,... | collective-permute-start | bytes 393224 | tf_op jit(solution)/shard_map/ppermute | solution.py:616
  141.5 5.2 %collective-permute-start.23 = (bf16[32,1024]{1,0:T(8,128)(2,1)S(1)}, bf16[32,1024]{1,0:T(8,128)(2,1)S(1)}, u32[]{:S(2)}, u32[]{:S(2)}) collective-permute-start(bf16[32,1024]{1,0:T(8,128)(2,1)S(1)} %get-tuple-element.101), channel_id=1, source_target_pairs={{0,2},{1,3},{2,0},{3,1},{4,6},{5,7},{6,4},{7,5},{8,10},{9,11},{10,... | collective-permute-start | bytes 196616 | tf_op jit(solution)/shard_map/ppermute | solution.py:616
  (8 other events, 39.5 us)
where the time goes:
time: 148 us; the launch traced here: 147 us
  Pallas kernels  66.7 us (45%)
  waiting for transfers between devices  39.7 us (27%)
  starting transfers between devices  34.8 us (24%)
  local copies, waits for them, and re-layouts  5.25 us (4%)
    pallas_call x3, Pallas kernels, attention_grads(): pl.pallas_call(functools.partial(attention_kernel, band_rows, band_cols,...  35.7 us
    ppermute x6, waiting for transfers between devices, shifted(): return lax.ppermute(array, axis, route)  19.6 us
    pallas_call x22, Pallas kernels, on_chip(): pl.pallas_call(run, in_specs=[pl.BlockSpec(memory_space=pltpu.SMEM)] * le...  16 us
    ppermute x6, waiting for transfers between devices, exchanged(): lax.ppermute(array, axis, [(i, i ^ flip) for i in range(lax.axis_size(axi...  14.9 us
    ppermute x6, starting transfers between devices, shifted(): return lax.ppermute(array, axis, route)  12.8 us
    ppermute x8, starting transfers between devices, swapped(): lax.ppermute(array, axis, route(pairs[offset::2]))  12.5 us
    pallas_call x1, Pallas kernels, input_grads(): pl.pallas_call(kernel, grid=(steps,), in_specs=[pl.BlockSpec(memory_space...  6.1 us
    unnamed x16, local copies, waits for them, and re-layouts  5.25 us
  transfers between devices with their start and end apart: 24, of which 13 were waited for; matrix products, arithmetic and copies ran while one was open for 0% of the time, Pallas kernels for 29%

commit v1 on v0

--- a/solution.py
+++ b/solution.py
@@ -77,12 +77,12 @@
 
 
 def attention_kernel(band_rows, band_cols, total_rows, head_width, extra, first, count, shift, *refs):
-    (place_ref, mask_ref, left_ref, right_ref, rows_a, rows_b, corners_a, corners_b,
-     qkv_hbm, grad_hbm, w_hbm) = refs[:11]
-    before_a, before_b = refs[11 : 11 + shift], refs[11 + shift : 11 + 2 * shift]
+    (place_ref, mask_ref, take_ref, left_ref, right_ref, rows_a, rows_b, corners_a, corners_b,
+     qkv_hbm, grad_hbm, w_hbm) = refs[:12]
+    before_a, before_b = refs[12 : 12 + shift], refs[12 + shift : 12 + 2 * shift]
     (dq_all, out_a_all, out_b_all, mid_all, to_left_all, to_right_all,
      halo_ref, spot_ref, q_ref, k_ref, v_ref, dk_ref, dv_ref,
-     own_refs, w_refs, own_sem, w_sem) = refs[11 + extra :]
+     side_ref, own_refs, w_refs, own_sem, w_sem) = refs[12 + extra :]
     band_start = place_ref[0]
     even = place_ref[1] == 0
     tiles = band_rows // TILE_R
@@ -241,18 +241,17 @@
                 mid_ref[part, row * band_cols : (row + 1) * band_cols, at] = acc[
                     lane, base : base + band_cols, :
                 ].astype(BF)
-            for col in range(MARGIN):
-                here = slice(col * band_rows, (col + 1) * band_rows)
-                start = middle + band_cols + col
-                to_left_ref[part, here, at] = acc[
-                    lane, pl.ds(start, band_rows, stride=KEY_COLS), :
+            for row in range(band_rows):
+                start = middle + row * KEY_COLS + band_cols
+                side_ref[row * HALO_COLS : (row + 1) * HALO_COLS, at] = acc[
+                    lane, start : start + HALO_COLS, :
                 ].astype(BF)
-                to_right_ref[part, here, at] = acc[
-                    lane, pl.ds(start + MARGIN, band_rows, stride=KEY_COLS), :
-                ].astype(BF)
-
-
-def attention_grads(first, count, place, masks, halo, qkv, grad_out, w_qkv, shape, before, after):
+        sides = dot(take_ref[...], side_ref[...]).astype(BF)
+        to_left_ref[part] = sides[:side]
+        to_right_ref[part] = sides[side:]
+
+
+def attention_grads(first, count, place, masks, take, halo, qkv, grad_out, w_qkv, shape, before, after):
     band_rows, band_cols, total_rows = shape
     tokens, width = grad_out.shape
     head_width = width // HEADS
@@ -280,7 +279,7 @@
         ),
         grid=(count,),
         in_specs=[pl.BlockSpec(memory_space=pltpu.SMEM)]
-        + [vmem] * (1 + len(halo))
+        + [vmem] * (2 + len(halo))
         + [pl.BlockSpec(memory_space=pltpu.HBM)] * 3
         + [vmem] * len(before)
         + [pl.BlockSpec(memory_space=pl.ANY)] * len(after),
@@ -294,6 +293,7 @@
             pltpu.VMEM((region_tokens, block), BF),
             pltpu.VMEM((block // LANES, total_tokens, LANES), F32),
             pltpu.VMEM((block // LANES, total_tokens, LANES), F32),
+            pltpu.VMEM((band_rows * HALO_COLS, block), BF),
             pltpu.VMEM((count, 4, tokens, block), BF),
             pltpu.VMEM((count, 2, width, block), BF),
             pltpu.SemaphoreType.DMA((count, 4)),
@@ -305,7 +305,7 @@
         cost_estimate=pl.CostEstimate(
             flops=count * 14 * 10**9, bytes_accessed=count * 8 * MIB, transcendentals=count * 10**6
         ),
-    )(place, masks, *halo, qkv, grad_out, w_qkv, *before, *after)
+    )(place, masks, take, *halo, qkv, grad_out, w_qkv, *before, *after)
 
 
 def on_chip(kernel, out_shape, operands, after=(), scratch=(), flops=10**5, place=()):
@@ -477,6 +477,27 @@
 
     out = ((2 * MARGIN * EDGE_R, width), BF)
     return on_chip(kernel, [out, out], [left, right], after=after, place=[place])
+
+
+def selectors(band_rows, band_cols, after):
+    side = MARGIN * band_rows
+
+    def kernel(take_ref, put_ref):
+        sent = lax.broadcasted_iota(jnp.int32, take_ref.shape, 0)
+        held = lax.broadcasted_iota(jnp.int32, take_ref.shape, 1)
+        same_row = (sent & (band_rows - 1)) == (held >> (HALO_COLS.bit_length() - 1))
+        same_col = (sent >> (band_rows.bit_length() - 1)) == (held & (HALO_COLS - 1))
+        take_ref[...] = jnp.where(same_row & same_col, 1.0, 0.0).astype(BF)
+        held = lax.broadcasted_iota(jnp.int32, put_ref.shape, 0)
+        sent = lax.broadcasted_iota(jnp.int32, put_ref.shape, 1)
+        same_row = (sent & (band_rows - 1)) == (held >> (band_cols.bit_length() - 1))
+        col = sent >> (band_rows.bit_length() - 1)
+        col = jnp.where(col < MARGIN, col, col + band_cols - 2 * MARGIN)
+        same_col = col == (held & (band_cols - 1))
+        put_ref[...] = jnp.where(same_row & same_col, 1.0, 0.0).astype(BF)
+
+    out = [((2 * side, band_rows * HALO_COLS), BF), ((band_rows * band_cols, 2 * side), BF)]
+    return on_chip(kernel, out, [], after)
 
 
 def merge_sides(place, lefts, rights, rim_a, rim_b, band_rows, band_cols, after=()):
@@ -510,7 +531,7 @@
     return on_chip(kernel, [out, out], [*lefts, *rights, rim_a, rim_b], after, place=[place])
 
 
-def finish(place, mids, rim_a, rim_b, left, right, parts, band_rows, band_cols, after, flops):
+def finish(place, mids, rim_a, rim_b, left, right, put, parts, band_rows, band_cols, after, flops):
     calls = len(mids)
     slots, _, _, block = rim_a.shape
     each = slots // calls
@@ -518,29 +539,22 @@
     tokens = band_rows * band_cols
 
     def kernel(place_ref, *refs):
-        a_ref, b_ref, left_ref, right_ref, *outs, acc_ref = refs[calls:]
+        a_ref, b_ref, left_ref, right_ref, put_ref, *outs, acc_ref = refs[calls:]
         even = place_ref[1] == 0
         for out_ref, part in zip(outs, parts):
             for slot in range(slots):
-                for lane, at in lanes_of(block):
-                    acc_ref[lane] = refs[slot // each][slot % each, part, :, at].astype(F32)
-                    from_a, from_b = (
-                        r[slot, part, :edge, at].astype(F32) for r in (a_ref, b_ref)
-                    )
-                    acc_ref[lane, :edge, :] += jnp.where(even, from_b, from_a)
-                    acc_ref[lane, tokens - edge :, :] += jnp.where(even, from_a, from_b)
-                    for col in range(MARGIN):
-                        here = slice(col * band_rows, (col + 1) * band_rows)
-                        first = pl.ds(col, band_rows, stride=band_cols)
-                        last = pl.ds(band_cols - MARGIN + col, band_rows, stride=band_cols)
-                        acc_ref[lane, first, :] += left_ref[slot, part, here, at].astype(F32)
-                        acc_ref[lane, last, :] += right_ref[slot, part, here, at].astype(F32)
-                    start = slot * block + lane * LANES
-                    out_ref[:, start : start + LANES] = acc_ref[lane].astype(BF)
+                sides = jnp.concatenate([left_ref[slot, part], right_ref[slot, part]], axis=0)
+                acc_ref[...] = dot(put_ref[...], sides) + refs[slot // each][
+                    slot % each, part
+                ].astype(F32)
+                from_a, from_b = (r[slot, part, :edge, :].astype(F32) for r in (a_ref, b_ref))
+                acc_ref[:edge, :] += jnp.where(even, from_b, from_a)
+                acc_ref[tokens - edge :, :] += jnp.where(even, from_a, from_b)
+                out_ref[:, slot * block : (slot + 1) * block] = acc_ref[...].astype(BF)
 
     out = [((tokens, slots * block), BF)] * len(parts)
-    scratch = [pltpu.VMEM((block // LANES, tokens, LANES), F32)]
-    operands = [*mids, rim_a, rim_b, left, right]
+    scratch = [pltpu.VMEM((tokens, block), F32)]
+    operands = [*mids, rim_a, rim_b, left, right, put]
     return on_chip(kernel, out, operands, after, scratch, flops, [place])
 
 
@@ -669,17 +683,18 @@
     start = jnp.stack([band_start, lax.axis_index("lat") % 2, me])
     rim_rows = swapped(*pack_rows(start, own, band_cols, [last_cols]), "lat")
 
+    take, put = selectors(band_rows, band_cols, [last_cols])
     masks = window_masks(start, band_rows, band_cols, total_rows)
     qkv = project(own, w_qkv, [last_cols])
     first, stages = reduce_stages()
     half = width // 2
     rows_keep, rows_send = row_blocks(start, own, feature_orders(first, stages), [last_cols])
-    corners = pack_corners(start, left, right, band_rows, [masks, qkv, rows_keep, rows_send])
+    corners = pack_corners(start, left, right, band_rows, [masks, take, qkv, rows_keep, rows_send])
     halo = (left, right, *rim_rows, *swapped(*corners, "lat"))
     scale = float(tokens * n_dp * n_lat * n_lon) ** -0.5
 
     attend = lambda first, count, before, after: attention_grads(
-        first, count, start, masks, halo, qkv, flat_grad, w_qkv, shape, before, after
+        first, count, start, masks, take, halo, qkv, flat_grad, w_qkv, shape, before, after
     )
 
     def return_sides(calls, rims, after):
@@ -692,7 +707,7 @@
 
     def finished(calls, rims, sides, parts, after, flops):
         mids = [c[3] for c in calls]
-        return finish(start, mids, *rims, *sides, parts, band_rows, band_cols, after, flops)
+        return finish(start, mids, *rims, *sides, put, parts, band_rows, band_cols, after, flops)
 
     groups = HEADS // GROUP
     one = attend(0, slots, [], [])

time: 148 us -> 149 us (level)
  starting transfers between devices: 34.8 us -> 40 us
  waiting for transfers between devices: 39.7 us -> 34.5 us
    ppermute x6, starting transfers between devices: 4.81 us -> 7.79 us  [exchanged(): lax.ppermute(array, axis, [(i, i ^ flip) for i in range(lax.axis_size(axi...]
    ppermute x6, waiting for transfers between devices: 19.6 us -> 16.8 us  [shifted(): return lax.ppermute(array, axis, route)]
    ppermute x6, waiting for transfers between devices: 14.9 us -> 12.5 us  [exchanged(): lax.ppermute(array, axis, [(i, i ^ flip) for i in range(lax.axis_size(axi...]
    unnamed x16 -> x20, local copies, waits for them, and re-layouts: 5.25 us -> 6.01 us
    pallas_call x22 -> x23, Pallas kernels: 16 us -> 15.8 us  [on_chip(): pl.pallas_call(run, in_specs=[pl.BlockSpec(memory_space=pltpu.SMEM)] * le...]
  transfers between devices with their start and end apart: 24 -> 24, of which waited for: 13 -> 12; matrix products, arithmetic and copies ran while one was open for 0% -> 0% of each run, Pallas kernels for 29% -> 29%
where the time goes in v1:
time: 149 us; the launch traced here: 148 us
  Pallas kernels  66.6 us (45%)
  starting transfers between devices  40 us (27%)
  waiting for transfers between devices  34.5 us (23%)
  local copies, waits for them, and re-layouts  6.01 us (4%)
    pallas_call x3, Pallas kernels, attention_grads(): pl.pallas_call(functools.partial(attention_kernel, band_rows, band_cols,...  35.8 us
    ppermute x6, waiting for transfers between devices, shifted(): return lax.ppermute(array, axis, route)  16.8 us
    pallas_call x23, Pallas kernels, on_chip(): pl.pallas_call(run, in_specs=[pl.BlockSpec(memory_space=pltpu.SMEM)] * le...  15.8 us
    ppermute x8, starting transfers between devices, swapped(): lax.ppermute(array, axis, route(pairs[offset::2]))  13.2 us
    ppermute x6, starting transfers between devices, shifted(): return lax.ppermute(array, axis, route)  12.8 us
    ppermute x6, waiting for transfers between devices, exchanged(): lax.ppermute(array, axis, [(i, i ^ flip) for i in range(lax.axis_size(axi...  12.5 us
    ppermute x6, starting transfers between devices, exchanged(): lax.ppermute(array, axis, [(i, i ^ flip) for i in range(lax.axis_size(axi...  7.79 us
    ppermute x4, starting transfers between devices, exchanged_stage(): return lax.ppermute(array, ('dp', 'lat'), route)  6.14 us
  transfers between devices with their start and end apart: 24, of which 12 were waited for; matrix products, arithmetic and copies ran while one was open for 0% of the time, Pallas kernels for 29%

profile of v1, /device:TPU:0, one launch (start us, length us, event | category | flops | bytes accessed | tf_op | source)
XLA Modules:
  0.0 148.1 jit_solution(14832487760655222077)
XLA Ops:
  3.4 5.0 %collective-permute-start.1 = (bf16[192,1024]{1,0:T(8,128)(2,1)}, bf16[192,1024]{1,0:T(8,128)(2,1)S(1)}, u32[]{:S(2)}, u32[]{:S(2)}) collective-permute-start(bf16[192,1024]{1,0:T(8,128)(2,1)} %get-tuple-element.56), channel_id=1, source_target_pairs={{0,3},{1,0},{2,1},{3,2},{4,7},{5,4},{6,5},{7,6},{8,11},{9,8},{10,9... | collective-permute-start | bytes 1179656 | tf_op jit(solution)/shard_map/ppermute | solution.py:616
  14.4 4.0 %shard_map.50.refs_3_.refs_1_ = bf16[8,512,128]{2,1,0:T(8,128)(2,1)} custom-call(s32[3]{0:T(128)} %copy-done.7), custom_call_target="tpu_custom_call" | custom-call | flops 10000000 | bytes 2097152 | tf_op jit(solution)/shard_map/pallas_call | solution.py:69
  18.5 2.8 %copy-done.3 = bf16[1024,3072]{1,0:T(8,128)(2,1)S(1)} copy-done((bf16[1024,3072]{1,0:T(8,128)(2,1)S(1)}, bf16[1024,3072]{1,0:T(8,128)(2,1)}, u32[]{:S(2)}) %copy-start.3) | copy-done | bytes 6291480
  21.3 4.9 %shard_map.54.refs_5_.refs_9_ = bf16[512,3072]{1,0:T(8,128)(2,1)S(1)} custom-call(bf16[512,1024]{1,0:T(8,128)(2,1)S(1)} %bitcast.9, bf16[1024,3072]{1,0:T(8,128)(2,1)S(1)} %copy-done.3, bf16[192,1024]{1,0:T(8,128)(2,1)S(1)} %get-tuple-element.54.refs_0_.refs_2_), custom_call_target="tpu_custom_call" | custom-call | flops 1000000000 | bytes 1048576 | tf_op jit(solution)/shard_map/pallas_call | solution.py:342
  27.6 2.0 %collective-permute-start.4 = (bf16[96,1024]{1,0:T(8,128)(2,1)S(1)}, bf16[96,1024]{1,0:T(8,128)(2,1)S(1)}, u32[]{:S(2)}, u32[]{:S(2)}) collective-permute-start(bf16[96,1024]{1,0:T(8,128)(2,1)S(1)} %get-tuple-element.61), channel_id=1, source_target_pairs={{0,4},{8,12},{4,0},{12,8},{1,5},{9,13},{5,1},{13,9},{2,6},{10,14},... | collective-permute-start | bytes 589832 | tf_op jit(solution)/shard_map/ppermute | solution.py:624
  30.7 17.2 %shard_map.57 = (bf16[2,512,256]{2,1,0:T(8,128)(2,1)S(1)}, bf16[2,2,192,256]{3,2,1,0:T(8,128)(2,1)S(1)}, bf16[2,2,192,256]{3,2,1,0:T(8,128)(2,1)S(1)}, bf16[2,2,...) custom-call(s32[3]{0:T(128)S(1)} %copy-done.8, ...), custom_call_target="tpu_custom_call" | custom-call | flops 28000000000 | bytes 16777216 | tf_op jit(solution)/shard_map/pallas_call | solution.py:275
  48.0 6.0 %collective-permute-start.6 = (bf16[2,2,192,256]{3,2,1,0:T(8,128)(2,1)S(1)}, bf16[2,2,192,256]{3,2,1,0:T(8,128)(2,1)S(1)}, u32[]{:S(2)}, u32[]{:S(2)}) collective-permute-start(bf16[2,2,192,256]{3,2,1,0:T(8,128)(2,1)S(1)} %get-tuple-element.69), channel_id=1, source_target_pairs={{0,4},{8,12},{4,0},{12,8},{1,5},{9,13},{5,1},{13,9},{2,6},{10,14},... | collective-permute-start | bytes 1179656 | tf_op jit(solution)/shard_map/ppermute | solution.py:624
  54.8 9.3 %shard_map.58 = (bf16[1,512,256]{2,1,0:T(8,128)(2,1)S(1)}, bf16[1,2,192,256]{3,2,1,0:T(8,128)(2,1)S(1)}, bf16[1,2,192,256]{3,2,1,0:T(8,128)(2,1)S(1)}, bf16[1,2,...) custom-call(s32[3]{0:T(128)S(1)} %copy-done.8, ...), custom_call_target="tpu_custom_call" | custom-call | flops 14000000000 | bytes 8388608 | tf_op jit(solution)/shard_map/pallas_call | solution.py:275
  65.0 3.7 %collective-permute-start.9 = (bf16[2,2,192,256]{3,2,1,0:T(8,128)(2,1)S(1)}, bf16[2,2,192,256]{3,2,1,0:T(8,128)(2,1)S(1)}, u32[]{:S(2)}, u32[]{:S(2)}) collective-permute-start(bf16[2,2,192,256]{3,2,1,0:T(8,128)(2,1)S(1)} %get-tuple-element.71.refs_14_), channel_id=1, source_target_pairs={{0,3},{1,0},{2,1},{3,2},{4,7},{5,4},{6,5},{7,6},{8,11},{9,8},{10,9... | collective-permute-start | bytes 1179656 | tf_op jit(solution)/shard_map/ppermute | solution.py:616
  68.7 9.3 %shard_map.60 = (bf16[1,512,256]{2,1,0:T(8,128)(2,1)S(1)}, bf16[2,2,192,256]{3,2,1,0:T(8,128)(2,1)S(1)}, bf16[2,2,192,256]{3,2,1,0:T(8,128)(2,1)S(1)}, bf16[1,2,...) custom-call(s32[3]{0:T(128)S(1)} %copy-done.8, ...), custom_call_target="tpu_custom_call" | custom-call | flops 14000000000 | bytes 8388608 | tf_op jit(solution)/shard_map/pallas_call | solution.py:275
  78.1 1.7 %collective-permute-start.10 = (bf16[2,2,192,256]{3,2,1,0:T(8,128)(2,1)S(1)}, bf16[2,2,192,256]{3,2,1,0:T(8,128)(2,1)S(1)}, u32[]{:S(2)}, u32[]{:S(2)}) collective-permute-start(bf16[2,2,192,256]{3,2,1,0:T(8,128)(2,1)S(1)} %get-tuple-element.79), channel_id=1, source_target_pairs={{0,4},{8,12},{4,0},{12,8},{1,5},{9,13},{5,1},{13,9},{2,6},{10,14},... | collective-permute-start | bytes 1179656 | tf_op jit(solution)/shard_map/ppermute | solution.py:624
  80.4 3.8 %collective-permute-done.9.refs_5_ = bf16[2,2,192,256]{3,2,1,0:T(8,128)(2,1)S(1)} collective-permute-done((bf16[2,2,192,256]{3,2,1,0:T(8,128)(2,1)S(1)}, bf16[2,2,192,256]{3,2,1,0:T(8,128)(2,1)S(1)}, u32[]{:S(2)}, u32[]{:S(2)}) %collective-permute-start.9) | collective-permute-done | bytes 393248 | tf_op jit(solution)/shard_map/ppermute | solution.py:616
  87.5 3.3 %collective-permute-start.14 = (bf16[512,2048]{1,0:T(8,128)(2,1)S(1)}, bf16[512,2048]{1,0:T(8,128)(2,1)S(1)}, u32[]{:S(2)}, u32[]{:S(2)}) collective-permute-start(bf16[512,2048]{1,0:T(8,128)(2,1)S(1)} %shard_map.63.refs_6_), channel_id=1, source_target_pairs={{0,4},{4,0},{8,12},{12,8},{1,5},{5,1},{9,13},{13,9},{2,6},{6,2},{1... | collective-permute-start | bytes 6291464 | tf_op jit(solution)/shard_map/ppermute | solution.py:630
  91.0 3.7 %collective-permute-start.13 = (bf16[2,2,192,256]{3,2,1,0:T(8,128)(2,1)S(1)}, bf16[2,2,192,256]{3,2,1,0:T(8,128)(2,1)S(1)}, u32[]{:S(2)}, u32[]{:S(2)}) collective-permute-start(bf16[2,2,192,256]{3,2,1,0:T(8,128)(2,1)S(1)} %get-tuple-element.86.refs_6_), channel_id=1, source_target_pairs={{0,3},{1,0},{2,1},{3,2},{4,7},{5,4},{6,5},{7,6},{8,11},{9,8},{10,9... | collective-permute-start | bytes 1179656 | tf_op jit(solution)/shard_map/ppermute | solution.py:616
  96.4 1.6 %collective-permute-start.15 = (bf16[256,2048]{1,0:T(8,128)(2,1)S(1)}, bf16[256,2048]{1,0:T(8,128)(2,1)S(1)}, u32[]{:S(2)}, u32[]{:S(2)}) collective-permute-start(bf16[256,2048]{1,0:T(8,128)(2,1)S(1)} %get-tuple-element.89), channel_id=1, source_target_pairs={{0,16},{4,12},{8,24},{12,4},{16,0},{20,28},{24,8},{28,20},{1,17},{... | collective-permute-start | bytes 3145736 | tf_op jit(solution)/shard_map/ppermute | solution.py:665
  98.0 6.7 %collective-permute-done.12.refs_5_ = bf16[2,2,192,256]{3,2,1,0:T(8,128)(2,1)S(1)} collective-permute-done((bf16[2,2,192,256]{3,2,1,0:T(8,128)(2,1)S(1)}, bf16[2,2,192,256]{3,2,1,0:T(8,128)(2,1)S(1)}, u32[]{:S(2)}, u32[]{:S(2)}) %collective-permute-start.12) | collective-permute-done | bytes 393248 | tf_op jit(solution)/shard_map/ppermute | solution.py:616
  104.7 6.0 %collective-permute-done.13.refs_6_ = bf16[2,2,192,256]{3,2,1,0:T(8,128)(2,1)S(1)} collective-permute-done((bf16[2,2,192,256]{3,2,1,0:T(8,128)(2,1)S(1)}, bf16[2,2,192,256]{3,2,1,0:T(8,128)(2,1)S(1)}, u32[]{:S(2)}, u32[]{:S(2)}) %collective-permute-start.13) | collective-permute-done | bytes 393248 | tf_op jit(solution)/shard_map/ppermute | solution.py:616
  116.5 1.6 %collective-permute-start.19 = (bf16[256,1024]{1,0:T(8,128)(2,1)S(1)}, bf16[256,1024]{1,0:T(8,128)(2,1)S(1)}, u32[]{:S(2)}, u32[]{:S(2)}) collective-permute-start(bf16[256,1024]{1,0:T(8,128)(2,1)S(1)} %get-tuple-element.91.refs_8_), channel_id=1, source_target_pairs={{0,16},{4,12},{8,24},{12,4},{16,0},{20,28},{24,8},{28,20},{1,17},{... | collective-permute-start | bytes 1572872 | tf_op jit(solution)/shard_map/ppermute | solution.py:665
  118.1 6.1 %shard_map.72 = (bf16[512,1024]{1,0:T(8,128)(2,1)}, f32[8,128]{1,0:T(8,128)S(1)}) custom-call(bf16[2,512,256]{2,1,0:T(8,128)(2,1)S(1)} %get-tuple-element.63.refs_12_.refs_1_.refs_0_, bf16[1,512,256]{2,1,0:T(8,128)(2,1)S(1)} %get-tuple-element.64.refs_5_.refs_2_.refs_1_, bf16[1,512,256]{2,1,0:T(8,128)(2,1)S(1)} %get-tuple-element.72.refs_7_.refs_3_.refs_2_, ...), custom_call_target="tpu_custom_call" | custom-call | flops 4000000000 | bytes 1048576 | tf_op jit(solution)/shard_map/pallas_call | solution.py:380
  124.2 2.3 %collective-permute-done.17.refs_1_ = bf16[128,2048]{1,0:T(8,128)(2,1)S(1)} collective-permute-done((bf16[128,2048]{1,0:T(8,128)(2,1)S(1)}, bf16[128,2048]{1,0:T(8,128)(2,1)S(1)}, u32[]{:S(2)}, u32[]{:S(2)}) %collective-permute-start.17) | collective-permute-done | bytes 524320 | tf_op jit(solution)/shard_map/ppermute | solution.py:665
  129.6 3.5 %collective-permute-done.18.refs_1_ = bf16[64,2048]{1,0:T(8,128)(2,1)S(1)} collective-permute-done((bf16[64,2048]{1,0:T(8,128)(2,1)S(1)}, bf16[64,2048]{1,0:T(8,128)(2,1)S(1)}, u32[]{:S(2)}, u32[]{:S(2)}) %collective-permute-start.18) | collective-permute-done | bytes 262176 | tf_op jit(solution)/shard_map/ppermute | solution.py:630
  135.3 2.1 %collective-permute-start.20 = (bf16[32,2048]{1,0:T(8,128)(2,1)S(1)}, bf16[32,2048]{1,0:T(8,128)(2,1)S(1)}, u32[]{:S(2)}, u32[]{:S(2)}) collective-permute-start(bf16[32,2048]{1,0:T(8,128)(2,1)S(1)} %get-tuple-element.100), channel_id=1, source_target_pairs={{0,2},{1,3},{2,0},{3,1},{4,6},{5,7},{6,4},{7,5},{8,10},{9,11},{10,... | collective-permute-start | bytes 393224 | tf_op jit(solution)/shard_map/ppermute | solution.py:630
  137.5 4.6 %collective-permute-done.22.refs_1_ = bf16[64,1024]{1,0:T(8,128)(2,1)S(1)} collective-permute-done((bf16[64,1024]{1,0:T(8,128)(2,1)S(1)}, bf16[64,1024]{1,0:T(8,128)(2,1)S(1)}, u32[]{:S(2)}, u32[]{:S(2)}) %collective-permute-start.22) | collective-permute-done | bytes 131104 | tf_op jit(solution)/shard_map/ppermute | solution.py:630
  143.3 4.0 %collective-permute-done.23.refs_3_ = bf16[32,1024]{1,0:T(8,128)(2,1)S(1)} collective-permute-done((bf16[32,1024]{1,0:T(8,128)(2,1)S(1)}, bf16[32,1024]{1,0:T(8,128)(2,1)S(1)}, u32[]{:S(2)}, u32[]{:S(2)}) %collective-permute-start.23) | collective-permute-done | bytes 65568 | tf_op jit(solution)/shard_map/ppermute | solution.py:630
  (74 shorter events, 31.9 us)
Async XLA Ops:
  3.4 22.8 %collective-permute-start.1 = (bf16[192,1024]{1,0:T(8,128)(2,1)}, bf16[192,1024]{1,0:T(8,128)(2,1)S(1)}, u32[]{:S(2)}, u32[]{:S(2)}) collective-permute-start(bf16[192,1024]{1,0:T(8,128)(2,1)} %get-tuple-element.56), channel_id=1, source_target_pairs={{0,3},{1,0},{2,1},{3,2},{4,7},{5,4},{6,5},{7,6},{8,11},{9,8},{10,9... | collective-permute-start | bytes 1179656 | tf_op jit(solution)/shard_map/ppermute | solution.py:616
  8.4 18.0 %collective-permute-start = (bf16[192,1024]{1,0:T(8,128)(2,1)S(1)}, bf16[192,1024]{1,0:T(8,128)(2,1)}, u32[]{:S(2)}, u32[]{:S(2)}) collective-permute-start(bf16[192,1024]{1,0:T(8,128)(2,1)S(1)} %get-tuple-element.54.refs_0_.refs_2_), channel_id=1, source_target_pairs={{0,1},{1,2},{2,3},{3,0},{4,5},{5,6},{6,7},{7,4},{8,9},{9,10},{10,1... | collective-permute-start | bytes 1179656 | tf_op jit(solution)/shard_map/ppermute | solution.py:616
  11.0 19.3 %collective-permute-start.2 = (bf16[96,1024]{1,0:T(8,128)(2,1)}, bf16[96,1024]{1,0:T(8,128)(2,1)S(1)}, u32[]{:S(2)}, u32[]{:S(2)}) collective-permute-start(bf16[96,1024]{1,0:T(8,128)(2,1)} %get-tuple-element.57), channel_id=1, source_target_pairs={{0,4},{8,12},{4,0},{12,8},{1,5},{9,13},{5,1},{13,9},{2,6},{10,14},... | collective-permute-start | bytes 589832 | tf_op jit(solution)/shard_map/ppermute | solution.py:624
  11.1 19.3 %collective-permute-start.3 = (bf16[96,1024]{1,0:T(8,128)(2,1)}, bf16[96,1024]{1,0:T(8,128)(2,1)}, u32[]{:S(2)}, u32[]{:S(2)}) collective-permute-start(bf16[96,1024]{1,0:T(8,128)(2,1)} %get-tuple-element.58), channel_id=1, source_target_pairs={{4,8},{8,4},{5,9},{9,5},{6,10},{10,6},{7,11},{11,7},{20,24},{24,20... | collective-permute-start | bytes 589832 | tf_op jit(solution)/shard_map/ppermute | solution.py:624
  27.6 3.1 %collective-permute-start.4 = (bf16[96,1024]{1,0:T(8,128)(2,1)S(1)}, bf16[96,1024]{1,0:T(8,128)(2,1)S(1)}, u32[]{:S(2)}, u32[]{:S(2)}) collective-permute-start(bf16[96,1024]{1,0:T(8,128)(2,1)S(1)} %get-tuple-element.61), channel_id=1, source_target_pairs={{0,4},{8,12},{4,0},{12,8},{1,5},{9,13},{5,1},{13,9},{2,6},{10,14},... | collective-permute-start | bytes 589832 | tf_op jit(solution)/shard_map/ppermute | solution.py:624
  29.7 1.1 collective-permute-start.5
  48.0 16.1 %collective-permute-start.6 = (bf16[2,2,192,256]{3,2,1,0:T(8,128)(2,1)S(1)}, bf16[2,2,192,256]{3,2,1,0:T(8,128)(2,1)S(1)}, u32[]{:S(2)}, u32[]{:S(2)}) collective-permute-start(bf16[2,2,192,256]{3,2,1,0:T(8,128)(2,1)S(1)} %get-tuple-element.69), channel_id=1, source_target_pairs={{0,4},{8,12},{4,0},{12,8},{1,5},{9,13},{5,1},{13,9},{2,6},{10,14},... | collective-permute-start | bytes 1179656 | tf_op jit(solution)/shard_map/ppermute | solution.py:624
  54.0 10.2 %collective-permute-start.7 = (bf16[2,2,192,256]{3,2,1,0:T(8,128)(2,1)S(1)}, bf16[2,2,192,256]{3,2,1,0:T(8,128)(2,1)S(1)}, u32[]{:S(2)}, u32[]{:S(2)}) collective-permute-start(bf16[2,2,192,256]{3,2,1,0:T(8,128)(2,1)S(1)} %get-tuple-element.70), channel_id=1, source_target_pairs={{4,8},{8,4},{5,9},{9,5},{6,10},{10,6},{7,11},{11,7},{20,24},{24,20... | collective-permute-start | bytes 1179656 | tf_op jit(solution)/shard_map/ppermute | solution.py:624
  64.8 15.6 %collective-permute-start.8 = (bf16[2,2,192,256]{3,2,1,0:T(8,128)(2,1)S(1)}, bf16[2,2,192,256]{3,2,1,0:T(8,128)(2,1)S(1)}, u32[]{:S(2)}, u32[]{:S(2)}) collective-permute-start(bf16[2,2,192,256]{3,2,1,0:T(8,128)(2,1)S(1)} %get-tuple-element.74), channel_id=1, source_target_pairs={{0,1},{1,2},{2,3},{3,0},{4,5},{5,6},{6,7},{7,4},{8,9},{9,10},{10,1... | collective-permute-start | bytes 1179656 | tf_op jit(solution)/shard_map/ppermute | solution.py:616
  65.0 19.3 %collective-permute-start.9 = (bf16[2,2,192,256]{3,2,1,0:T(8,128)(2,1)S(1)}, bf16[2,2,192,256]{3,2,1,0:T(8,128)(2,1)S(1)}, u32[]{:S(2)}, u32[]{:S(2)}) collective-permute-start(bf16[2,2,192,256]{3,2,1,0:T(8,128)(2,1)S(1)} %get-tuple-element.71.refs_14_), channel_id=1, source_target_pairs={{0,3},{1,0},{2,1},{3,2},{4,7},{5,4},{6,5},{7,6},{8,11},{9,8},{10,9... | collective-permute-start | bytes 1179656 | tf_op jit(solution)/shard_map/ppermute | solution.py:616
  78.1 7.5 %collective-permute-start.10 = (bf16[2,2,192,256]{3,2,1,0:T(8,128)(2,1)S(1)}, bf16[2,2,192,256]{3,2,1,0:T(8,128)(2,1)S(1)}, u32[]{:S(2)}, u32[]{:S(2)}) collective-permute-start(bf16[2,2,192,256]{3,2,1,0:T(8,128)(2,1)S(1)} %get-tuple-element.79), channel_id=1, source_target_pairs={{0,4},{8,12},{4,0},{12,8},{1,5},{9,13},{5,1},{13,9},{2,6},{10,14},... | collective-permute-start | bytes 1179656 | tf_op jit(solution)/shard_map/ppermute | solution.py:624
  79.7 5.8 %collective-permute-start.11 = (bf16[2,2,192,256]{3,2,1,0:T(8,128)(2,1)S(1)}, bf16[2,2,192,256]{3,2,1,0:T(8,128)(2,1)S(1)}, u32[]{:S(2)}, u32[]{:S(2)}) collective-permute-start(bf16[2,2,192,256]{3,2,1,0:T(8,128)(2,1)S(1)} %get-tuple-element.80), channel_id=1, source_target_pairs={{4,8},{8,4},{5,9},{9,5},{6,10},{10,6},{7,11},{11,7},{20,24},{24,20... | collective-permute-start | bytes 1179656 | tf_op jit(solution)/shard_map/ppermute | solution.py:624
  87.5 8.4 %collective-permute-start.14 = (bf16[512,2048]{1,0:T(8,128)(2,1)S(1)}, bf16[512,2048]{1,0:T(8,128)(2,1)S(1)}, u32[]{:S(2)}, u32[]{:S(2)}) collective-permute-start(bf16[512,2048]{1,0:T(8,128)(2,1)S(1)} %shard_map.63.refs_6_), channel_id=1, source_target_pairs={{0,4},{4,0},{8,12},{12,8},{1,5},{5,1},{9,13},{13,9},{2,6},{6,2},{1... | collective-permute-start | bytes 6291464 | tf_op jit(solution)/shard_map/ppermute | solution.py:630
  90.8 13.8 %collective-permute-start.12 = (bf16[2,2,192,256]{3,2,1,0:T(8,128)(2,1)S(1)}, bf16[2,2,192,256]{3,2,1,0:T(8,128)(2,1)S(1)}, u32[]{:S(2)}, u32[]{:S(2)}) collective-permute-start(bf16[2,2,192,256]{3,2,1,0:T(8,128)(2,1)S(1)} %get-tuple-element.85), channel_id=1, source_target_pairs={{0,1},{1,2},{2,3},{3,0},{4,5},{5,6},{6,7},{7,4},{8,9},{9,10},{10,1... | collective-permute-start | bytes 1179656 | tf_op jit(solution)/shard_map/ppermute | solution.py:616
  91.0 19.7 %collective-permute-start.13 = (bf16[2,2,192,256]{3,2,1,0:T(8,128)(2,1)S(1)}, bf16[2,2,192,256]{3,2,1,0:T(8,128)(2,1)S(1)}, u32[]{:S(2)}, u32[]{:S(2)}) collective-permute-start(bf16[2,2,192,256]{3,2,1,0:T(8,128)(2,1)S(1)} %get-tuple-element.86.refs_6_), channel_id=1, source_target_pairs={{0,3},{1,0},{2,1},{3,2},{4,7},{5,4},{6,5},{7,6},{8,11},{9,8},{10,9... | collective-permute-start | bytes 1179656 | tf_op jit(solution)/shard_map/ppermute | solution.py:616
  96.4 15.2 %collective-permute-start.15 = (bf16[256,2048]{1,0:T(8,128)(2,1)S(1)}, bf16[256,2048]{1,0:T(8,128)(2,1)S(1)}, u32[]{:S(2)}, u32[]{:S(2)}) collective-permute-start(bf16[256,2048]{1,0:T(8,128)(2,1)S(1)} %get-tuple-element.89), channel_id=1, source_target_pairs={{0,16},{4,12},{8,24},{12,4},{16,0},{20,28},{24,8},{28,20},{1,17},{... | collective-permute-start | bytes 3145736 | tf_op jit(solution)/shard_map/ppermute | solution.py:665
  113.6 2.7 %collective-permute-start.16 = (bf16[512,1024]{1,0:T(8,128)(2,1)S(1)}, bf16[512,1024]{1,0:T(8,128)(2,1)S(1)}, u32[]{:S(2)}, u32[]{:S(2)}) collective-permute-start(bf16[512,1024]{1,0:T(8,128)(2,1)S(1)} %shard_map.69.refs_3_), channel_id=1, source_target_pairs={{0,4},{4,0},{8,12},{12,8},{1,5},{5,1},{9,13},{13,9},{2,6},{6,2},{1... | collective-permute-start | bytes 3145736 | tf_op jit(solution)/shard_map/ppermute | solution.py:630
  113.7 12.8 %collective-permute-start.17 = (bf16[128,2048]{1,0:T(8,128)(2,1)S(1)}, bf16[128,2048]{1,0:T(8,128)(2,1)S(1)}, u32[]{:S(2)}, u32[]{:S(2)}) collective-permute-start(bf16[128,2048]{1,0:T(8,128)(2,1)S(1)} %get-tuple-element.93), channel_id=1, source_target_pairs={{0,8},{4,20},{8,0},{12,28},{16,24},{20,4},{24,16},{28,12},{1,9},{5... | collective-permute-start | bytes 1572872 | tf_op jit(solution)/shard_map/ppermute | solution.py:665
  116.5 11.5 %collective-permute-start.19 = (bf16[256,1024]{1,0:T(8,128)(2,1)S(1)}, bf16[256,1024]{1,0:T(8,128)(2,1)S(1)}, u32[]{:S(2)}, u32[]{:S(2)}) collective-permute-start(bf16[256,1024]{1,0:T(8,128)(2,1)S(1)} %get-tuple-element.91.refs_8_), channel_id=1, source_target_pairs={{0,16},{4,12},{8,24},{12,4},{16,0},{20,28},{24,8},{28,20},{1,17},{... | collective-permute-start | bytes 1572872 | tf_op jit(solution)/shard_map/ppermute | solution.py:665
  126.6 6.5 %collective-permute-start.18 = (bf16[64,2048]{1,0:T(8,128)(2,1)S(1)}, bf16[64,2048]{1,0:T(8,128)(2,1)S(1)}, u32[]{:S(2)}, u32[]{:S(2)}) collective-permute-start(bf16[64,2048]{1,0:T(8,128)(2,1)S(1)} %get-tuple-element.96), channel_id=1, source_target_pairs={{0,1},{1,0},{2,3},{3,2},{4,5},{5,4},{6,7},{7,6},{8,9},{9,8},{10,11... | collective-permute-start | bytes 786440 | tf_op jit(solution)/shard_map/ppermute | solution.py:630
  128.1 6.4 %collective-permute-start.21 = (bf16[128,1024]{1,0:T(8,128)(2,1)S(1)}, bf16[128,1024]{1,0:T(8,128)(2,1)S(1)}, u32[]{:S(2)}, u32[]{:S(2)}) collective-permute-start(bf16[128,1024]{1,0:T(8,128)(2,1)S(1)} %get-tuple-element.101), channel_id=1, source_target_pairs={{0,8},{4,20},{8,0},{12,28},{16,24},{20,4},{24,16},{28,12},{1,9},{5... | collective-permute-start | bytes 786440 | tf_op jit(solution)/shard_map/ppermute | solution.py:665
  134.6 7.5 %collective-permute-start.22 = (bf16[64,1024]{1,0:T(8,128)(2,1)S(1)}, bf16[64,1024]{1,0:T(8,128)(2,1)S(1)}, u32[]{:S(2)}, u32[]{:S(2)}) collective-permute-start(bf16[64,1024]{1,0:T(8,128)(2,1)S(1)} %get-tuple-element.103), channel_id=1, source_target_pairs={{0,1},{1,0},{2,3},{3,2},{4,5},{5,4},{6,7},{7,6},{8,9},{9,8},{10,11... | collective-permute-start | bytes 393224 | tf_op jit(solution)/shard_map/ppermute | solution.py:630
  135.3 8.0 %collective-permute-start.20 = (bf16[32,2048]{1,0:T(8,128)(2,1)S(1)}, bf16[32,2048]{1,0:T(8,128)(2,1)S(1)}, u32[]{:S(2)}, u32[]{:S(2)}) collective-permute-start(bf16[32,2048]{1,0:T(8,128)(2,1)S(1)} %get-tuple-element.100), channel_id=1, source_target_pairs={{0,2},{1,3},{2,0},{3,1},{4,6},{5,7},{6,4},{7,5},{8,10},{9,11},{10,... | collective-permute-start | bytes 393224 | tf_op jit(solution)/shard_map/ppermute | solution.py:630
  142.1 5.2 %collective-permute-start.23 = (bf16[32,1024]{1,0:T(8,128)(2,1)S(1)}, bf16[32,1024]{1,0:T(8,128)(2,1)S(1)}, u32[]{:S(2)}, u32[]{:S(2)}) collective-permute-start(bf16[32,1024]{1,0:T(8,128)(2,1)S(1)} %get-tuple-element.105), channel_id=1, source_target_pairs={{0,2},{1,3},{2,0},{3,1},{4,6},{5,7},{6,4},{7,5},{8,10},{9,11},{10,... | collective-permute-start | bytes 196616 | tf_op jit(solution)/shard_map/ppermute | solution.py:630
  (10 other events, 42.1 us)

commit v2 on v1

--- a/solution.py
+++ b/solution.py
@@ -211,7 +211,7 @@
         dq_ref[mine, :] = (dq * head_width**-0.5).astype(BF)
         return carry
 
-    lax.fori_loop(0, tiles, one_tile, 0, unroll=4)
+    lax.fori_loop(0, tiles, one_tile, 0, unroll=8)
 
     middle = (PAD_R + MARGIN) * KEY_COLS
     below = (PAD_R + MARGIN + band_rows) * KEY_COLS
@@ -337,7 +337,12 @@
     block = 4 * LANES
 
     def kernel(own_ref, w_ref, *refs):
-        refs[-1][...] = dot(own_ref[...], w_ref[...]).astype(BF)
+        def part(n, carry):
+            at = pl.ds(pl.multiple_of(n * 2 * LANES, 2 * LANES), 2 * LANES)
+            refs[-1][:, at] = dot(own_ref[...], w_ref[:, at]).astype(BF)
+            return carry
+
+        lax.fori_loop(0, block // (2 * LANES), part, 0)
 
     return pl.pallas_call(
         kernel,
@@ -368,13 +373,21 @@
             @pl.when(pl.program_id(0) == step)
             def _():
                 both = [piece(refs, *where) for where in pieces[2 * step : 2 * step + 2]]
-                product = dot(jnp.concatenate(both, axis=1), w_ref[...], NT)
-                if step == 0:
-                    acc_ref[...] = product
-                elif step < steps - 1:
-                    acc_ref[...] += product
-                else:
-                    out_ref[...] = (acc_ref[...] + product).astype(BF)
+                chunk = jnp.concatenate(both, axis=1)
+
+                def add(n, carry):
+                    at = pl.ds(pl.multiple_of(n * 2 * LANES, 2 * LANES), 2 * LANES)
+                    product = dot(chunk, w_ref[at, :], NT)
+                    if step == 0:
+                        acc_ref[:, at] = product
+                    elif step < steps - 1:
+                        acc_ref[:, at] += product
+                    else:
+                        out_ref[:, at] = (acc_ref[:, at] + product).astype(BF)
+                    return carry
+
+                lax.fori_loop(0, width // (2 * LANES), add, 0)
+                if step == steps - 1:
                     done_ref[...] = jnp.zeros_like(done_ref)
 
     return pl.pallas_call(
@@ -689,7 +702,7 @@
     first, stages = reduce_stages()
     half = width // 2
     rows_keep, rows_send = row_blocks(start, own, feature_orders(first, stages), [last_cols])
-    corners = pack_corners(start, left, right, band_rows, [masks, take, qkv, rows_keep, rows_send])
+    corners = pack_corners(start, left, right, band_rows, [masks, qkv, rows_keep, rows_send])
     halo = (left, right, *rim_rows, *swapped(*corners, "lat"))
     scale = float(tokens * n_dp * n_lat * n_lon) ** -0.5
 

time: 149 us -> 148 us (level)
  waiting for transfers between devices: 34.5 us -> 31.7 us
  Pallas kernels: 66.6 us -> 69 us
    ppermute x4, waiting for transfers between devices: 4.83 us -> 0.01 us  [exchanged_stage(): return lax.ppermute(array, ('dp', 'lat'), route)]
    pallas_call x1, Pallas kernels: 6.1 us -> 9.8 us  [input_grads(): pl.pallas_call(kernel, grid=(steps,), in_specs=[pl.BlockSpec(memory_space...]
    pallas_call x3, Pallas kernels: 35.8 us -> 33.9 us  [attention_grads(): pl.pallas_call(functools.partial(attention_kernel, band_rows, band_cols,...]
    unnamed x20 -> x16, local copies, waits for them, and re-layouts: 6.01 us -> 5.25 us
  transfers between devices with their start and end apart: 24 -> 24, of which waited for: 12 -> 10; matrix products, arithmetic and copies ran while one was open for 0% -> 0% of each run, Pallas kernels for 29% -> 31%
where the time goes in v2:
time: 148 us; the launch traced here: 147 us
  Pallas kernels  69 us (47%)
  starting transfers between devices  40.5 us (27%)
  waiting for transfers between devices  31.7 us (21%)
  local copies, waits for them, and re-layouts  5.25 us (4%)
    pallas_call x3, Pallas kernels, attention_grads(): pl.pallas_call(functools.partial(attention_kernel, band_rows, band_cols,...  33.9 us
    ppermute x6, waiting for transfers between devices, shifted(): return lax.ppermute(array, axis, route)  17.7 us
    pallas_call x23, Pallas kernels, on_chip(): pl.pallas_call(run, in_specs=[pl.BlockSpec(memory_space=pltpu.SMEM)] * le...  15.2 us
    ppermute x6, waiting for transfers between devices, exchanged(): lax.ppermute(array, axis, [(i, i ^ flip) for i in range(lax.axis_size(axi...  13.9 us
    ppermute x8, starting transfers between devices, swapped(): lax.ppermute(array, axis, route(pairs[offset::2]))  13.4 us
    ppermute x6, starting transfers between devices, shifted(): return lax.ppermute(array, axis, route)  13 us
    pallas_call x1, Pallas kernels, input_grads(): pl.pallas_call(kernel, grid=(steps,), in_specs=[pl.BlockSpec(memory_space...  9.8 us
    ppermute x6, starting transfers between devices, exchanged(): lax.ppermute(array, axis, [(i, i ^ flip) for i in range(lax.axis_size(axi...  8 us
  transfers between devices with their start and end apart: 24, of which 10 were waited for; matrix products, arithmetic and copies ran while one was open for 0% of the time, Pallas kernels for 31%

profile of v2, /device:TPU:0, one launch (start us, length us, event | category | flops | bytes accessed | tf_op | source)
XLA Modules:
  0.0 147.4 jit_solution(15442514424474784153)
XLA Ops:
  3.4 5.0 %collective-permute-start.1 = (bf16[192,1024]{1,0:T(8,128)(2,1)}, bf16[192,1024]{1,0:T(8,128)(2,1)S(1)}, u32[]{:S(2)}, u32[]{:S(2)}) collective-permute-start(bf16[192,1024]{1,0:T(8,128)(2,1)} %get-tuple-element.56), channel_id=1, source_target_pairs={{0,3},{1,0},{2,1},{3,2},{4,7},{5,4},{6,5},{7,6},{8,11},{9,8},{10,9... | collective-permute-start | bytes 1179656 | tf_op jit(solution)/shard_map/ppermute | solution.py:629
  13.4 4.0 %shard_map.50.refs_3_.refs_1_ = bf16[8,512,128]{2,1,0:T(8,128)(2,1)} custom-call(s32[3]{0:T(128)} %copy-done.5), custom_call_target="tpu_custom_call" | custom-call | flops 10000000 | bytes 2097152 | tf_op jit(solution)/shard_map/pallas_call | solution.py:69
  17.4 2.8 %copy-done.3 = bf16[1024,3072]{1,0:T(8,128)(2,1)S(1)} copy-done((bf16[1024,3072]{1,0:T(8,128)(2,1)S(1)}, bf16[1024,3072]{1,0:T(8,128)(2,1)}, u32[]{:S(2)}) %copy-start.3) | copy-done | bytes 6291480
  20.2 6.0 %shard_map.54.refs_4_.refs_9_ = bf16[512,3072]{1,0:T(8,128)(2,1)S(1)} custom-call(bf16[512,1024]{1,0:T(8,128)(2,1)S(1)} %bitcast.9, bf16[1024,3072]{1,0:T(8,128)(2,1)S(1)} %copy-done.3, bf16[192,1024]{1,0:T(8,128)(2,1)S(1)} %get-tuple-element.54.refs_0_.refs_2_), custom_call_target="tpu_custom_call" | custom-call | flops 1000000000 | bytes 1048576 | tf_op jit(solution)/shard_map/pallas_call | solution.py:347
  27.0 2.2 %collective-permute-start.4 = (bf16[96,1024]{1,0:T(8,128)(2,1)S(1)}, bf16[96,1024]{1,0:T(8,128)(2,1)S(1)}, u32[]{:S(2)}, u32[]{:S(2)}) collective-permute-start(bf16[96,1024]{1,0:T(8,128)(2,1)S(1)} %get-tuple-element.61), channel_id=1, source_target_pairs={{0,4},{8,12},{4,0},{12,8},{1,5},{9,13},{5,1},{13,9},{2,6},{10,14},... | collective-permute-start | bytes 589832 | tf_op jit(solution)/shard_map/ppermute | solution.py:637
  30.3 16.4 %shard_map.57 = (bf16[2,512,256]{2,1,0:T(8,128)(2,1)S(1)}, bf16[2,2,192,256]{3,2,1,0:T(8,128)(2,1)S(1)}, bf16[2,2,192,256]{3,2,1,0:T(8,128)(2,1)S(1)}, bf16[2,2,...) custom-call(s32[3]{0:T(128)S(1)} %copy-done.6, ...), custom_call_target="tpu_custom_call" | custom-call | flops 28000000000 | bytes 16777216 | tf_op jit(solution)/shard_map/pallas_call | solution.py:275
  46.7 6.0 %collective-permute-start.6 = (bf16[2,2,192,256]{3,2,1,0:T(8,128)(2,1)S(1)}, bf16[2,2,192,256]{3,2,1,0:T(8,128)(2,1)S(1)}, u32[]{:S(2)}, u32[]{:S(2)}) collective-permute-start(bf16[2,2,192,256]{3,2,1,0:T(8,128)(2,1)S(1)} %get-tuple-element.69), channel_id=1, source_target_pairs={{0,4},{8,12},{4,0},{12,8},{1,5},{9,13},{5,1},{13,9},{2,6},{10,14},... | collective-permute-start | bytes 1179656 | tf_op jit(solution)/shard_map/ppermute | solution.py:637
  53.6 8.7 %shard_map.58 = (bf16[1,512,256]{2,1,0:T(8,128)(2,1)S(1)}, bf16[1,2,192,256]{3,2,1,0:T(8,128)(2,1)S(1)}, bf16[1,2,192,256]{3,2,1,0:T(8,128)(2,1)S(1)}, bf16[1,2,...) custom-call(s32[3]{0:T(128)S(1)} %copy-done.6, ...), custom_call_target="tpu_custom_call" | custom-call | flops 14000000000 | bytes 8388608 | tf_op jit(solution)/shard_map/pallas_call | solution.py:275
  63.1 4.1 %collective-permute-start.9 = (bf16[2,2,192,256]{3,2,1,0:T(8,128)(2,1)S(1)}, bf16[2,2,192,256]{3,2,1,0:T(8,128)(2,1)S(1)}, u32[]{:S(2)}, u32[]{:S(2)}) collective-permute-start(bf16[2,2,192,256]{3,2,1,0:T(8,128)(2,1)S(1)} %get-tuple-element.71.refs_14_), channel_id=1, source_target_pairs={{0,3},{1,0},{2,1},{3,2},{4,7},{5,4},{6,5},{7,6},{8,11},{9,8},{10,9... | collective-permute-start | bytes 1179656 | tf_op jit(solution)/shard_map/ppermute | solution.py:629
  67.1 8.7 %shard_map.60 = (bf16[1,512,256]{2,1,0:T(8,128)(2,1)S(1)}, bf16[2,2,192,256]{3,2,1,0:T(8,128)(2,1)S(1)}, bf16[2,2,192,256]{3,2,1,0:T(8,128)(2,1)S(1)}, bf16[1,2,...) custom-call(s32[3]{0:T(128)S(1)} %copy-done.6, ...), custom_call_target="tpu_custom_call" | custom-call | flops 14000000000 | bytes 8388608 | tf_op jit(solution)/shard_map/pallas_call | solution.py:275
  75.9 1.7 %collective-permute-start.10 = (bf16[2,2,192,256]{3,2,1,0:T(8,128)(2,1)S(1)}, bf16[2,2,192,256]{3,2,1,0:T(8,128)(2,1)S(1)}, u32[]{:S(2)}, u32[]{:S(2)}) collective-permute-start(bf16[2,2,192,256]{3,2,1,0:T(8,128)(2,1)S(1)} %get-tuple-element.79), channel_id=1, source_target_pairs={{0,4},{8,12},{4,0},{12,8},{1,5},{9,13},{5,1},{13,9},{2,6},{10,14},... | collective-permute-start | bytes 1179656 | tf_op jit(solution)/shard_map/ppermute | solution.py:637
  78.3 4.6 %collective-permute-done.9.refs_5_ = bf16[2,2,192,256]{3,2,1,0:T(8,128)(2,1)S(1)} collective-permute-done((bf16[2,2,192,256]{3,2,1,0:T(8,128)(2,1)S(1)}, bf16[2,2,192,256]{3,2,1,0:T(8,128)(2,1)S(1)}, u32[]{:S(2)}, u32[]{:S(2)}) %collective-permute-start.9) | collective-permute-done | bytes 393248 | tf_op jit(solution)/shard_map/ppermute | solution.py:629
  86.1 2.6 %collective-permute-start.14 = (bf16[512,2048]{1,0:T(8,128)(2,1)S(1)}, bf16[512,2048]{1,0:T(8,128)(2,1)S(1)}, u32[]{:S(2)}, u32[]{:S(2)}) collective-permute-start(bf16[512,2048]{1,0:T(8,128)(2,1)S(1)} %shard_map.63.refs_6_), channel_id=1, source_target_pairs={{0,4},{4,0},{8,12},{12,8},{1,5},{5,1},{9,13},{13,9},{2,6},{6,2},{1... | collective-permute-start | bytes 6291464 | tf_op jit(solution)/shard_map/ppermute | solution.py:643
  89.2 3.3 %collective-permute-start.13 = (bf16[2,2,192,256]{3,2,1,0:T(8,128)(2,1)S(1)}, bf16[2,2,192,256]{3,2,1,0:T(8,128)(2,1)S(1)}, u32[]{:S(2)}, u32[]{:S(2)}) collective-permute-start(bf16[2,2,192,256]{3,2,1,0:T(8,128)(2,1)S(1)} %get-tuple-element.86.refs_6_), channel_id=1, source_target_pairs={{0,3},{1,0},{2,1},{3,2},{4,7},{5,4},{6,5},{7,6},{8,11},{9,8},{10,9... | collective-permute-start | bytes 1179656 | tf_op jit(solution)/shard_map/ppermute | solution.py:629
  95.8 6.7 %collective-permute-done.12.refs_5_ = bf16[2,2,192,256]{3,2,1,0:T(8,128)(2,1)S(1)} collective-permute-done((bf16[2,2,192,256]{3,2,1,0:T(8,128)(2,1)S(1)}, bf16[2,2,192,256]{3,2,1,0:T(8,128)(2,1)S(1)}, u32[]{:S(2)}, u32[]{:S(2)}) %collective-permute-start.12) | collective-permute-done | bytes 393248 | tf_op jit(solution)/shard_map/ppermute | solution.py:629
  102.5 6.3 %collective-permute-done.13.refs_6_ = bf16[2,2,192,256]{3,2,1,0:T(8,128)(2,1)S(1)} collective-permute-done((bf16[2,2,192,256]{3,2,1,0:T(8,128)(2,1)S(1)}, bf16[2,2,192,256]{3,2,1,0:T(8,128)(2,1)S(1)}, u32[]{:S(2)}, u32[]{:S(2)}) %collective-permute-start.13) | collective-permute-done | bytes 393248 | tf_op jit(solution)/shard_map/ppermute | solution.py:629
  116.1 9.8 %shard_map.72 = (bf16[512,1024]{1,0:T(8,128)(2,1)}, f32[8,128]{1,0:T(8,128)S(1)}) custom-call(bf16[2,512,256]{2,1,0:T(8,128)(2,1)S(1)} %get-tuple-element.63.refs_12_.refs_1_.refs_0_, bf16[1,512,256]{2,1,0:T(8,128)(2,1)S(1)} %get-tuple-element.64.refs_5_.refs_2_.refs_1_, bf16[1,512,256]{2,1,0:T(8,128)(2,1)S(1)} %get-tuple-element.72.refs_7_.refs_3_.refs_2_, ...), custom_call_target="tpu_custom_call" | custom-call | flops 4000000000 | bytes 1048576 | tf_op jit(solution)/shard_map/pallas_call | solution.py:393
  126.5 1.8 %collective-permute-start.21 = (bf16[128,1024]{1,0:T(8,128)(2,1)S(1)}, bf16[128,1024]{1,0:T(8,128)(2,1)S(1)}, u32[]{:S(2)}, u32[]{:S(2)}) collective-permute-start(bf16[128,1024]{1,0:T(8,128)(2,1)S(1)} %get-tuple-element.101), channel_id=1, source_target_pairs={{0,8},{4,20},{8,0},{12,28},{16,24},{20,4},{24,16},{28,12},{1,9},{5... | collective-permute-start | bytes 786440 | tf_op jit(solution)/shard_map/ppermute | solution.py:678
  128.3 5.6 %collective-permute-done.18.refs_1_ = bf16[64,2048]{1,0:T(8,128)(2,1)S(1)} collective-permute-done((bf16[64,2048]{1,0:T(8,128)(2,1)S(1)}, bf16[64,2048]{1,0:T(8,128)(2,1)S(1)}, u32[]{:S(2)}, u32[]{:S(2)}) %collective-permute-start.18) | collective-permute-done | bytes 262176 | tf_op jit(solution)/shard_map/ppermute | solution.py:643
  134.9 1.9 %collective-permute-start.20 = (bf16[32,2048]{1,0:T(8,128)(2,1)S(1)}, bf16[32,2048]{1,0:T(8,128)(2,1)S(1)}, u32[]{:S(2)}, u32[]{:S(2)}) collective-permute-start(bf16[32,2048]{1,0:T(8,128)(2,1)S(1)} %get-tuple-element.100), channel_id=1, source_target_pairs={{0,2},{1,3},{2,0},{3,1},{4,6},{5,7},{6,4},{7,5},{8,10},{9,11},{10,... | collective-permute-start | bytes 393224 | tf_op jit(solution)/shard_map/ppermute | solution.py:643
  136.8 3.9 %collective-permute-done.22.refs_1_ = bf16[64,1024]{1,0:T(8,128)(2,1)S(1)} collective-permute-done((bf16[64,1024]{1,0:T(8,128)(2,1)S(1)}, bf16[64,1024]{1,0:T(8,128)(2,1)S(1)}, u32[]{:S(2)}, u32[]{:S(2)}) %collective-permute-start.22) | collective-permute-done | bytes 131104 | tf_op jit(solution)/shard_map/ppermute | solution.py:643
  140.7 2.3 %collective-permute-start.23 = (bf16[32,1024]{1,0:T(8,128)(2,1)S(1)}, bf16[32,1024]{1,0:T(8,128)(2,1)S(1)}, u32[]{:S(2)}, u32[]{:S(2)}) collective-permute-start(bf16[32,1024]{1,0:T(8,128)(2,1)S(1)} %get-tuple-element.105), channel_id=1, source_target_pairs={{0,2},{1,3},{2,0},{3,1},{4,6},{5,7},{6,4},{7,5},{8,10},{9,11},{10,... | collective-permute-start | bytes 196616 | tf_op jit(solution)/shard_map/ppermute | solution.py:643
  143.0 1.8 %collective-permute-done.20.refs_1_ = bf16[32,2048]{1,0:T(8,128)(2,1)S(1)} collective-permute-done((bf16[32,2048]{1,0:T(8,128)(2,1)S(1)}, bf16[32,2048]{1,0:T(8,128)(2,1)S(1)}, u32[]{:S(2)}, u32[]{:S(2)}) %collective-permute-start.20) | collective-permute-done | bytes 131104 | tf_op jit(solution)/shard_map/ppermute | solution.py:643
  144.8 1.8 %collective-permute-done.23.refs_3_ = bf16[32,1024]{1,0:T(8,128)(2,1)S(1)} collective-permute-done((bf16[32,1024]{1,0:T(8,128)(2,1)S(1)}, bf16[32,1024]{1,0:T(8,128)(2,1)S(1)}, u32[]{:S(2)}, u32[]{:S(2)}) %collective-permute-start.23) | collective-permute-done | bytes 65568 | tf_op jit(solution)/shard_map/ppermute | solution.py:643
  (70 shorter events, 28.3 us)
Async XLA Ops:
  3.4 22.9 %collective-permute-start.1 = (bf16[192,1024]{1,0:T(8,128)(2,1)}, bf16[192,1024]{1,0:T(8,128)(2,1)S(1)}, u32[]{:S(2)}, u32[]{:S(2)}) collective-permute-start(bf16[192,1024]{1,0:T(8,128)(2,1)} %get-tuple-element.56), channel_id=1, source_target_pairs={{0,3},{1,0},{2,1},{3,2},{4,7},{5,4},{6,5},{7,6},{8,11},{9,8},{10,9... | collective-permute-start | bytes 1179656 | tf_op jit(solution)/shard_map/ppermute | solution.py:629
  8.4 17.9 %collective-permute-start = (bf16[192,1024]{1,0:T(8,128)(2,1)S(1)}, bf16[192,1024]{1,0:T(8,128)(2,1)S(1)}, u32[]{:S(2)}, u32[]{:S(2)}) collective-permute-start(bf16[192,1024]{1,0:T(8,128)(2,1)S(1)} %get-tuple-element.54.refs_0_.refs_2_), channel_id=1, source_target_pairs={{0,1},{1,2},{2,3},{3,0},{4,5},{5,6},{6,7},{7,4},{8,9},{9,10},{10,1... | collective-permute-start | bytes 1179656 | tf_op jit(solution)/shard_map/ppermute | solution.py:629
  11.0 19.1 %collective-permute-start.2 = (bf16[96,1024]{1,0:T(8,128)(2,1)}, bf16[96,1024]{1,0:T(8,128)(2,1)S(1)}, u32[]{:S(2)}, u32[]{:S(2)}) collective-permute-start(bf16[96,1024]{1,0:T(8,128)(2,1)} %get-tuple-element.57), channel_id=1, source_target_pairs={{0,4},{8,12},{4,0},{12,8},{1,5},{9,13},{5,1},{13,9},{2,6},{10,14},... | collective-permute-start | bytes 589832 | tf_op jit(solution)/shard_map/ppermute | solution.py:637
  11.0 19.1 %collective-permute-start.3 = (bf16[96,1024]{1,0:T(8,128)(2,1)}, bf16[96,1024]{1,0:T(8,128)(2,1)}, u32[]{:S(2)}, u32[]{:S(2)}) collective-permute-start(bf16[96,1024]{1,0:T(8,128)(2,1)} %get-tuple-element.58), channel_id=1, source_target_pairs={{4,8},{8,4},{5,9},{9,5},{6,10},{10,6},{7,11},{11,7},{20,24},{24,20... | collective-permute-start | bytes 589832 | tf_op jit(solution)/shard_map/ppermute | solution.py:637
  27.0 3.3 %collective-permute-start.4 = (bf16[96,1024]{1,0:T(8,128)(2,1)S(1)}, bf16[96,1024]{1,0:T(8,128)(2,1)S(1)}, u32[]{:S(2)}, u32[]{:S(2)}) collective-permute-start(bf16[96,1024]{1,0:T(8,128)(2,1)S(1)} %get-tuple-element.61), channel_id=1, source_target_pairs={{0,4},{8,12},{4,0},{12,8},{1,5},{9,13},{5,1},{13,9},{2,6},{10,14},... | collective-permute-start | bytes 589832 | tf_op jit(solution)/shard_map/ppermute | solution.py:637
  29.2 1.1 collective-permute-start.5
  46.7 15.6 %collective-permute-start.6 = (bf16[2,2,192,256]{3,2,1,0:T(8,128)(2,1)S(1)}, bf16[2,2,192,256]{3,2,1,0:T(8,128)(2,1)S(1)}, u32[]{:S(2)}, u32[]{:S(2)}) collective-permute-start(bf16[2,2,192,256]{3,2,1,0:T(8,128)(2,1)S(1)} %get-tuple-element.69), channel_id=1, source_target_pairs={{0,4},{8,12},{4,0},{12,8},{1,5},{9,13},{5,1},{13,9},{2,6},{10,14},... | collective-permute-start | bytes 1179656 | tf_op jit(solution)/shard_map/ppermute | solution.py:637
  52.7 9.6 %collective-permute-start.7 = (bf16[2,2,192,256]{3,2,1,0:T(8,128)(2,1)S(1)}, bf16[2,2,192,256]{3,2,1,0:T(8,128)(2,1)S(1)}, u32[]{:S(2)}, u32[]{:S(2)}) collective-permute-start(bf16[2,2,192,256]{3,2,1,0:T(8,128)(2,1)S(1)} %get-tuple-element.70), channel_id=1, source_target_pairs={{4,8},{8,4},{5,9},{9,5},{6,10},{10,6},{7,11},{11,7},{20,24},{24,20... | collective-permute-start | bytes 1179656 | tf_op jit(solution)/shard_map/ppermute | solution.py:637
  63.0 15.2 %collective-permute-start.8 = (bf16[2,2,192,256]{3,2,1,0:T(8,128)(2,1)S(1)}, bf16[2,2,192,256]{3,2,1,0:T(8,128)(2,1)S(1)}, u32[]{:S(2)}, u32[]{:S(2)}) collective-permute-start(bf16[2,2,192,256]{3,2,1,0:T(8,128)(2,1)S(1)} %get-tuple-element.74), channel_id=1, source_target_pairs={{0,1},{1,2},{2,3},{3,0},{4,5},{5,6},{6,7},{7,4},{8,9},{9,10},{10,1... | collective-permute-start | bytes 1179656 | tf_op jit(solution)/shard_map/ppermute | solution.py:629
  63.1 19.8 %collective-permute-start.9 = (bf16[2,2,192,256]{3,2,1,0:T(8,128)(2,1)S(1)}, bf16[2,2,192,256]{3,2,1,0:T(8,128)(2,1)S(1)}, u32[]{:S(2)}, u32[]{:S(2)}) collective-permute-start(bf16[2,2,192,256]{3,2,1,0:T(8,128)(2,1)S(1)} %get-tuple-element.71.refs_14_), channel_id=1, source_target_pairs={{0,3},{1,0},{2,1},{3,2},{4,7},{5,4},{6,5},{7,6},{8,11},{9,8},{10,9... | collective-permute-start | bytes 1179656 | tf_op jit(solution)/shard_map/ppermute | solution.py:629
  75.9 8.3 %collective-permute-start.10 = (bf16[2,2,192,256]{3,2,1,0:T(8,128)(2,1)S(1)}, bf16[2,2,192,256]{3,2,1,0:T(8,128)(2,1)S(1)}, u32[]{:S(2)}, u32[]{:S(2)}) collective-permute-start(bf16[2,2,192,256]{3,2,1,0:T(8,128)(2,1)S(1)} %get-tuple-element.79), channel_id=1, source_target_pairs={{0,4},{8,12},{4,0},{12,8},{1,5},{9,13},{5,1},{13,9},{2,6},{10,14},... | collective-permute-start | bytes 1179656 | tf_op jit(solution)/shard_map/ppermute | solution.py:637
  77.6 6.6 %collective-permute-start.11 = (bf16[2,2,192,256]{3,2,1,0:T(8,128)(2,1)S(1)}, bf16[2,2,192,256]{3,2,1,0:T(8,128)(2,1)S(1)}, u32[]{:S(2)}, u32[]{:S(2)}) collective-permute-start(bf16[2,2,192,256]{3,2,1,0:T(8,128)(2,1)S(1)} %get-tuple-element.80), channel_id=1, source_target_pairs={{4,8},{8,4},{5,9},{9,5},{6,10},{10,6},{7,11},{11,7},{20,24},{24,20... | collective-permute-start | bytes 1179656 | tf_op jit(solution)/shard_map/ppermute | solution.py:637
  86.1 7.6 %collective-permute-start.14 = (bf16[512,2048]{1,0:T(8,128)(2,1)S(1)}, bf16[512,2048]{1,0:T(8,128)(2,1)S(1)}, u32[]{:S(2)}, u32[]{:S(2)}) collective-permute-start(bf16[512,2048]{1,0:T(8,128)(2,1)S(1)} %shard_map.63.refs_6_), channel_id=1, source_target_pairs={{0,4},{4,0},{8,12},{12,8},{1,5},{5,1},{9,13},{13,9},{2,6},{6,2},{1... | collective-permute-start | bytes 6291464 | tf_op jit(solution)/shard_map/ppermute | solution.py:643
  88.7 13.8 %collective-permute-start.12 = (bf16[2,2,192,256]{3,2,1,0:T(8,128)(2,1)S(1)}, bf16[2,2,192,256]{3,2,1,0:T(8,128)(2,1)S(1)}, u32[]{:S(2)}, u32[]{:S(2)}) collective-permute-start(bf16[2,2,192,256]{3,2,1,0:T(8,128)(2,1)S(1)} %get-tuple-element.85), channel_id=1, source_target_pairs={{0,1},{1,2},{2,3},{3,0},{4,5},{5,6},{6,7},{7,4},{8,9},{9,10},{10,1... | collective-permute-start | bytes 1179656 | tf_op jit(solution)/shard_map/ppermute | solution.py:629
  89.2 19.6 %collective-permute-start.13 = (bf16[2,2,192,256]{3,2,1,0:T(8,128)(2,1)S(1)}, bf16[2,2,192,256]{3,2,1,0:T(8,128)(2,1)S(1)}, u32[]{:S(2)}, u32[]{:S(2)}) collective-permute-start(bf16[2,2,192,256]{3,2,1,0:T(8,128)(2,1)S(1)} %get-tuple-element.86.refs_6_), channel_id=1, source_target_pairs={{0,3},{1,0},{2,1},{3,2},{4,7},{5,4},{6,5},{7,6},{8,11},{9,8},{10,9... | collective-permute-start | bytes 1179656 | tf_op jit(solution)/shard_map/ppermute | solution.py:629
  94.2 15.5 %collective-permute-start.15 = (bf16[256,2048]{1,0:T(8,128)(2,1)S(1)}, bf16[256,2048]{1,0:T(8,128)(2,1)S(1)}, u32[]{:S(2)}, u32[]{:S(2)}) collective-permute-start(bf16[256,2048]{1,0:T(8,128)(2,1)S(1)} %get-tuple-element.89), channel_id=1, source_target_pairs={{0,16},{4,12},{8,24},{12,4},{16,0},{20,28},{24,8},{28,20},{1,17},{... | collective-permute-start | bytes 3145736 | tf_op jit(solution)/shard_map/ppermute | solution.py:678
  111.7 2.7 %collective-permute-start.16 = (bf16[512,1024]{1,0:T(8,128)(2,1)S(1)}, bf16[512,1024]{1,0:T(8,128)(2,1)S(1)}, u32[]{:S(2)}, u32[]{:S(2)}) collective-permute-start(bf16[512,1024]{1,0:T(8,128)(2,1)S(1)} %shard_map.69.refs_3_), channel_id=1, source_target_pairs={{0,4},{4,0},{8,12},{12,8},{1,5},{5,1},{9,13},{13,9},{2,6},{6,2},{1... | collective-permute-start | bytes 3145736 | tf_op jit(solution)/shard_map/ppermute | solution.py:643
  111.8 14.2 %collective-permute-start.17 = (bf16[128,2048]{1,0:T(8,128)(2,1)S(1)}, bf16[128,2048]{1,0:T(8,128)(2,1)S(1)}, u32[]{:S(2)}, u32[]{:S(2)}) collective-permute-start(bf16[128,2048]{1,0:T(8,128)(2,1)S(1)} %get-tuple-element.93), channel_id=1, source_target_pairs={{0,8},{4,20},{8,0},{12,28},{16,24},{20,4},{24,16},{28,12},{1,9},{5... | collective-permute-start | bytes 1572872 | tf_op jit(solution)/shard_map/ppermute | solution.py:678
  114.6 11.8 %collective-permute-start.19 = (bf16[256,1024]{1,0:T(8,128)(2,1)S(1)}, bf16[256,1024]{1,0:T(8,128)(2,1)S(1)}, u32[]{:S(2)}, u32[]{:S(2)}) collective-permute-start(bf16[256,1024]{1,0:T(8,128)(2,1)S(1)} %get-tuple-element.91.refs_8_), channel_id=1, source_target_pairs={{0,16},{4,12},{8,24},{12,4},{16,0},{20,28},{24,8},{28,20},{1,17},{... | collective-permute-start | bytes 1572872 | tf_op jit(solution)/shard_map/ppermute | solution.py:678
  126.1 7.8 %collective-permute-start.18 = (bf16[64,2048]{1,0:T(8,128)(2,1)S(1)}, bf16[64,2048]{1,0:T(8,128)(2,1)S(1)}, u32[]{:S(2)}, u32[]{:S(2)}) collective-permute-start(bf16[64,2048]{1,0:T(8,128)(2,1)S(1)} %get-tuple-element.96), channel_id=1, source_target_pairs={{0,1},{1,0},{2,3},{3,2},{4,5},{5,4},{6,7},{7,6},{8,9},{9,8},{10,11... | collective-permute-start | bytes 786440 | tf_op jit(solution)/shard_map/ppermute | solution.py:643
  126.5 7.4 %collective-permute-start.21 = (bf16[128,1024]{1,0:T(8,128)(2,1)S(1)}, bf16[128,1024]{1,0:T(8,128)(2,1)S(1)}, u32[]{:S(2)}, u32[]{:S(2)}) collective-permute-start(bf16[128,1024]{1,0:T(8,128)(2,1)S(1)} %get-tuple-element.101), channel_id=1, source_target_pairs={{0,8},{4,20},{8,0},{12,28},{16,24},{20,4},{24,16},{28,12},{1,9},{5... | collective-permute-start | bytes 786440 | tf_op jit(solution)/shard_map/ppermute | solution.py:678
  134.0 6.7 %collective-permute-start.22 = (bf16[64,1024]{1,0:T(8,128)(2,1)S(1)}, bf16[64,1024]{1,0:T(8,128)(2,1)S(1)}, u32[]{:S(2)}, u32[]{:S(2)}) collective-permute-start(bf16[64,1024]{1,0:T(8,128)(2,1)S(1)} %get-tuple-element.103), channel_id=1, source_target_pairs={{0,1},{1,0},{2,3},{3,2},{4,5},{5,4},{6,7},{7,6},{8,9},{9,8},{10,11... | collective-permute-start | bytes 393224 | tf_op jit(solution)/shard_map/ppermute | solution.py:643
  134.9 10.0 %collective-permute-start.20 = (bf16[32,2048]{1,0:T(8,128)(2,1)S(1)}, bf16[32,2048]{1,0:T(8,128)(2,1)S(1)}, u32[]{:S(2)}, u32[]{:S(2)}) collective-permute-start(bf16[32,2048]{1,0:T(8,128)(2,1)S(1)} %get-tuple-element.100), channel_id=1, source_target_pairs={{0,2},{1,3},{2,0},{3,1},{4,6},{5,7},{6,4},{7,5},{8,10},{9,11},{10,... | collective-permute-start | bytes 393224 | tf_op jit(solution)/shard_map/ppermute | solution.py:643
  140.7 5.9 %collective-permute-start.23 = (bf16[32,1024]{1,0:T(8,128)(2,1)S(1)}, bf16[32,1024]{1,0:T(8,128)(2,1)S(1)}, u32[]{:S(2)}, u32[]{:S(2)}) collective-permute-start(bf16[32,1024]{1,0:T(8,128)(2,1)S(1)} %get-tuple-element.105), channel_id=1, source_target_pairs={{0,2},{1,3},{2,0},{3,1},{4,6},{5,7},{6,4},{7,5},{8,10},{9,11},{10,... | collective-permute-start | bytes 196616 | tf_op jit(solution)/shard_map/ppermute | solution.py:643
  (8 other events, 40.6 us)

commit v3 on v1

--- a/solution.py
+++ b/solution.py
@@ -211,7 +211,7 @@
         dq_ref[mine, :] = (dq * head_width**-0.5).astype(BF)
         return carry
 
-    lax.fori_loop(0, tiles, one_tile, 0, unroll=4)
+    lax.fori_loop(0, tiles, one_tile, 0, unroll=8)
 
     middle = (PAD_R + MARGIN) * KEY_COLS
     below = (PAD_R + MARGIN + band_rows) * KEY_COLS
@@ -362,20 +362,25 @@
     steps = len(pieces) // 2
 
     def kernel(*refs):
-        w_ref, (out_ref, done_ref, acc_ref) = refs[count], refs[-3:]
+        w_ref, (out_ref, done_ref, acc_ref, chunk_ref) = refs[count], refs[-4:]
+        now = pl.program_id(0)
         for step in range(steps):
 
-            @pl.when(pl.program_id(0) == step)
+            @pl.when(now == step)
             def _():
-                both = [piece(refs, *where) for where in pieces[2 * step : 2 * step + 2]]
-                product = dot(jnp.concatenate(both, axis=1), w_ref[...], NT)
-                if step == 0:
-                    acc_ref[...] = product
-                elif step < steps - 1:
-                    acc_ref[...] += product
-                else:
-                    out_ref[...] = (acc_ref[...] + product).astype(BF)
-                    done_ref[...] = jnp.zeros_like(done_ref)
+                for half, where in enumerate(pieces[2 * step : 2 * step + 2]):
+                    chunk_ref[:, half * 2 * LANES : (half + 1) * 2 * LANES] = piece(refs, *where)
+
+        @pl.when(now == 0)
+        def _():
+            acc_ref[...] = jnp.zeros_like(acc_ref)
+
+        acc_ref[...] += dot(chunk_ref[...], w_ref[...], NT)
+
+        @pl.when(now == steps - 1)
+        def _():
+            out_ref[...] = acc_ref[...].astype(BF)
+            done_ref[...] = jnp.zeros_like(done_ref)
 
     return pl.pallas_call(
         kernel,
@@ -391,7 +396,7 @@
             jax.ShapeDtypeStruct((tokens, width), BF),
             jax.ShapeDtypeStruct((8, LANES), F32),
         ],
-        scratch_shapes=[pltpu.VMEM((tokens, width), F32)],
+        scratch_shapes=[pltpu.VMEM((tokens, width), F32), pltpu.VMEM((tokens, 4 * LANES), BF)],
         compiler_params=pltpu.CompilerParams(vmem_limit_bytes=24 * MIB),
         cost_estimate=pl.CostEstimate(flops=4 * 10**9, bytes_accessed=MIB, transcendentals=0),
     )(*columns, w_qkv, *after)
@@ -689,7 +694,7 @@
     first, stages = reduce_stages()
     half = width // 2
     rows_keep, rows_send = row_blocks(start, own, feature_orders(first, stages), [last_cols])
-    corners = pack_corners(start, left, right, band_rows, [masks, take, qkv, rows_keep, rows_send])
+    corners = pack_corners(start, left, right, band_rows, [masks, qkv, rows_keep, rows_send])
     halo = (left, right, *rim_rows, *swapped(*corners, "lat"))
     scale = float(tokens * n_dp * n_lat * n_lon) ** -0.5
 

time: 149 us -> 145 us (0.973)
  starting transfers between devices: 40 us -> 36.5 us
  waiting for transfers between devices: 34.5 us -> 37.8 us
  Pallas kernels: 66.6 us -> 64.5 us
    ppermute x6, waiting for transfers between devices: 16.8 us -> 19.7 us  [shifted(): return lax.ppermute(array, axis, route)]
    ppermute x6, starting transfers between devices: 7.79 us -> 5.61 us  [exchanged(): lax.ppermute(array, axis, [(i, i ^ flip) for i in range(lax.axis_size(axi...]
    pallas_call x3, Pallas kernels: 35.8 us -> 33.9 us  [attention_grads(): pl.pallas_call(functools.partial(attention_kernel, band_rows, band_cols,...]
    unnamed x20 -> x16, local copies, waits for them, and re-layouts: 6.01 us -> 5.25 us
  transfers between devices with their start and end apart: 24 -> 24, of which waited for: 12 -> 13; matrix products, arithmetic and copies ran while one was open for 0% -> 0% of each run, Pallas kernels for 29% -> 28%
where the time goes in v3:
time: 145 us
  Pallas kernels  64.5 us (44%)
  waiting for transfers between devices  37.8 us (26%)
  starting transfers between devices  36.5 us (25%)
  local copies, waits for them, and re-layouts  5.25 us (4%)
    pallas_call x3, Pallas kernels, attention_grads(): pl.pallas_call(functools.partial(attention_kernel, band_rows, band_cols,...  33.9 us
    ppermute x6, waiting for transfers between devices, shifted(): return lax.ppermute(array, axis, route)  19.7 us
    pallas_call x23, Pallas kernels, on_chip(): pl.pallas_call(run, in_specs=[pl.BlockSpec(memory_space=pltpu.SMEM)] * le...  15.2 us
    ppermute x6, waiting for transfers between devices, exchanged(): lax.ppermute(array, axis, [(i, i ^ flip) for i in range(lax.axis_size(axi...  13.7 us
    ppermute x6, starting transfers between devices, shifted(): return lax.ppermute(array, axis, route)  13 us
    ppermute x8, starting transfers between devices, swapped(): lax.ppermute(array, axis, route(pairs[offset::2]))  12.2 us
    pallas_call x1, Pallas kernels, input_grads(): pl.pallas_call(kernel, grid=(steps,), in_specs=[pl.BlockSpec(memory_space...  6.5 us
    ppermute x4, starting transfers between devices, exchanged_stage(): return lax.ppermute(array, ('dp', 'lat'), route)  5.66 us
  transfers between devices with their start and end apart: 24, of which 13 were waited for; matrix products, arithmetic and copies ran while one was open for 0% of the time, Pallas kernels for 28%

profile of v3, /device:TPU:0, one launch (start us, length us, event | category | flops | bytes accessed | tf_op | source)
XLA Modules:
  0.0 145.1 jit_solution(5099245996355414588)
XLA Ops:
  3.4 5.0 %collective-permute-start.1 = (bf16[192,1024]{1,0:T(8,128)(2,1)}, bf16[192,1024]{1,0:T(8,128)(2,1)S(1)}, u32[]{:S(2)}, u32[]{:S(2)}) collective-permute-start(bf16[192,1024]{1,0:T(8,128)(2,1)} %get-tuple-element.56), channel_id=1, source_target_pairs={{0,3},{1,0},{2,1},{3,2},{4,7},{5,4},{6,5},{7,6},{8,11},{9,8},{10,9... | collective-permute-start | bytes 1179656 | tf_op jit(solution)/shard_map/ppermute | solution.py:621
  13.4 4.0 %shard_map.50.refs_3_.refs_1_ = bf16[8,512,128]{2,1,0:T(8,128)(2,1)} custom-call(s32[3]{0:T(128)} %copy-done.5), custom_call_target="tpu_custom_call" | custom-call | flops 10000000 | bytes 2097152 | tf_op jit(solution)/shard_map/pallas_call | solution.py:69
  17.4 2.8 %copy-done.3 = bf16[1024,3072]{1,0:T(8,128)(2,1)S(1)} copy-done((bf16[1024,3072]{1,0:T(8,128)(2,1)S(1)}, bf16[1024,3072]{1,0:T(8,128)(2,1)}, u32[]{:S(2)}) %copy-start.3) | copy-done | bytes 6291480
  20.2 4.9 %shard_map.54.refs_4_.refs_9_ = bf16[512,3072]{1,0:T(8,128)(2,1)S(1)} custom-call(bf16[512,1024]{1,0:T(8,128)(2,1)S(1)} %bitcast.9, bf16[1024,3072]{1,0:T(8,128)(2,1)S(1)} %copy-done.3, bf16[192,1024]{1,0:T(8,128)(2,1)S(1)} %get-tuple-element.54.refs_0_.refs_2_), custom_call_target="tpu_custom_call" | custom-call | flops 1000000000 | bytes 1048576 | tf_op jit(solution)/shard_map/pallas_call | solution.py:342
  29.1 16.4 %shard_map.57 = (bf16[2,512,256]{2,1,0:T(8,128)(2,1)S(1)}, bf16[2,2,192,256]{3,2,1,0:T(8,128)(2,1)S(1)}, bf16[2,2,192,256]{3,2,1,0:T(8,128)(2,1)S(1)}, bf16[2,2,...) custom-call(s32[3]{0:T(128)S(1)} %copy-done.6, ...), custom_call_target="tpu_custom_call" | custom-call | flops 28000000000 | bytes 16777216 | tf_op jit(solution)/shard_map/pallas_call | solution.py:275
  45.6 6.0 %collective-permute-start.6 = (bf16[2,2,192,256]{3,2,1,0:T(8,128)(2,1)S(1)}, bf16[2,2,192,256]{3,2,1,0:T(8,128)(2,1)S(1)}, u32[]{:S(2)}, u32[]{:S(2)}) collective-permute-start(bf16[2,2,192,256]{3,2,1,0:T(8,128)(2,1)S(1)} %get-tuple-element.69), channel_id=1, source_target_pairs={{0,4},{8,12},{4,0},{12,8},{1,5},{9,13},{5,1},{13,9},{2,6},{10,14},... | collective-permute-start | bytes 1179656 | tf_op jit(solution)/shard_map/ppermute | solution.py:629
  52.4 8.7 %shard_map.58 = (bf16[1,512,256]{2,1,0:T(8,128)(2,1)S(1)}, bf16[1,2,192,256]{3,2,1,0:T(8,128)(2,1)S(1)}, bf16[1,2,192,256]{3,2,1,0:T(8,128)(2,1)S(1)}, bf16[1,2,...) custom-call(s32[3]{0:T(128)S(1)} %copy-done.6, ...), custom_call_target="tpu_custom_call" | custom-call | flops 14000000000 | bytes 8388608 | tf_op jit(solution)/shard_map/pallas_call | solution.py:275
  63.0 3.0 %collective-permute-start.9 = (bf16[2,2,192,256]{3,2,1,0:T(8,128)(2,1)S(1)}, bf16[2,2,192,256]{3,2,1,0:T(8,128)(2,1)S(1)}, u32[]{:S(2)}, u32[]{:S(2)}) collective-permute-start(bf16[2,2,192,256]{3,2,1,0:T(8,128)(2,1)S(1)} %get-tuple-element.71.refs_14_), channel_id=1, source_target_pairs={{0,3},{1,0},{2,1},{3,2},{4,7},{5,4},{6,5},{7,6},{8,11},{9,8},{10,9... | collective-permute-start | bytes 1179656 | tf_op jit(solution)/shard_map/ppermute | solution.py:621
  66.0 8.7 %shard_map.60 = (bf16[1,512,256]{2,1,0:T(8,128)(2,1)S(1)}, bf16[2,2,192,256]{3,2,1,0:T(8,128)(2,1)S(1)}, bf16[2,2,192,256]{3,2,1,0:T(8,128)(2,1)S(1)}, bf16[1,2,...) custom-call(s32[3]{0:T(128)S(1)} %copy-done.6, ...), custom_call_target="tpu_custom_call" | custom-call | flops 14000000000 | bytes 8388608 | tf_op jit(solution)/shard_map/pallas_call | solution.py:275
  74.7 1.7 %collective-permute-start.10 = (bf16[2,2,192,256]{3,2,1,0:T(8,128)(2,1)S(1)}, bf16[2,2,192,256]{3,2,1,0:T(8,128)(2,1)S(1)}, u32[]{:S(2)}, u32[]{:S(2)}) collective-permute-start(bf16[2,2,192,256]{3,2,1,0:T(8,128)(2,1)S(1)} %get-tuple-element.79), channel_id=1, source_target_pairs={{0,4},{8,12},{4,0},{12,8},{1,5},{9,13},{5,1},{13,9},{2,6},{10,14},... | collective-permute-start | bytes 1179656 | tf_op jit(solution)/shard_map/ppermute | solution.py:629
  77.1 5.5 %collective-permute-done.9.refs_5_ = bf16[2,2,192,256]{3,2,1,0:T(8,128)(2,1)S(1)} collective-permute-done((bf16[2,2,192,256]{3,2,1,0:T(8,128)(2,1)S(1)}, bf16[2,2,192,256]{3,2,1,0:T(8,128)(2,1)S(1)}, u32[]{:S(2)}, u32[]{:S(2)}) %collective-permute-start.9) | collective-permute-done | bytes 393248 | tf_op jit(solution)/shard_map/ppermute | solution.py:621
  85.8 1.7 %collective-permute-start.14 = (bf16[512,2048]{1,0:T(8,128)(2,1)S(1)}, bf16[512,2048]{1,0:T(8,128)(2,1)S(1)}, u32[]{:S(2)}, u32[]{:S(2)}) collective-permute-start(bf16[512,2048]{1,0:T(8,128)(2,1)S(1)} %shard_map.63.refs_6_), channel_id=1, source_target_pairs={{0,4},{4,0},{8,12},{12,8},{1,5},{5,1},{9,13},{13,9},{2,6},{6,2},{1... | collective-permute-start | bytes 6291464 | tf_op jit(solution)/shard_map/ppermute | solution.py:635
  88.0 3.3 %collective-permute-start.13 = (bf16[2,2,192,256]{3,2,1,0:T(8,128)(2,1)S(1)}, bf16[2,2,192,256]{3,2,1,0:T(8,128)(2,1)S(1)}, u32[]{:S(2)}, u32[]{:S(2)}) collective-permute-start(bf16[2,2,192,256]{3,2,1,0:T(8,128)(2,1)S(1)} %get-tuple-element.86.refs_6_), channel_id=1, source_target_pairs={{0,3},{1,0},{2,1},{3,2},{4,7},{5,4},{6,5},{7,6},{8,11},{9,8},{10,9... | collective-permute-start | bytes 1179656 | tf_op jit(solution)/shard_map/ppermute | solution.py:621
  93.1 1.6 %collective-permute-start.15 = (bf16[256,2048]{1,0:T(8,128)(2,1)S(1)}, bf16[256,2048]{1,0:T(8,128)(2,1)S(1)}, u32[]{:S(2)}, u32[]{:S(2)}) collective-permute-start(bf16[256,2048]{1,0:T(8,128)(2,1)S(1)} %get-tuple-element.89), channel_id=1, source_target_pairs={{0,16},{4,12},{8,24},{12,4},{16,0},{20,28},{24,8},{28,20},{1,17},{... | collective-permute-start | bytes 3145736 | tf_op jit(solution)/shard_map/ppermute | solution.py:670
  94.6 6.7 %collective-permute-done.12.refs_5_ = bf16[2,2,192,256]{3,2,1,0:T(8,128)(2,1)S(1)} collective-permute-done((bf16[2,2,192,256]{3,2,1,0:T(8,128)(2,1)S(1)}, bf16[2,2,192,256]{3,2,1,0:T(8,128)(2,1)S(1)}, u32[]{:S(2)}, u32[]{:S(2)}) %collective-permute-start.12) | collective-permute-done | bytes 393248 | tf_op jit(solution)/shard_map/ppermute | solution.py:621
  101.3 6.2 %collective-permute-done.13.refs_6_ = bf16[2,2,192,256]{3,2,1,0:T(8,128)(2,1)S(1)} collective-permute-done((bf16[2,2,192,256]{3,2,1,0:T(8,128)(2,1)S(1)}, bf16[2,2,192,256]{3,2,1,0:T(8,128)(2,1)S(1)}, u32[]{:S(2)}, u32[]{:S(2)}) %collective-permute-start.13) | collective-permute-done | bytes 393248 | tf_op jit(solution)/shard_map/ppermute | solution.py:621
  113.4 1.6 %collective-permute-start.19 = (bf16[256,1024]{1,0:T(8,128)(2,1)S(1)}, bf16[256,1024]{1,0:T(8,128)(2,1)S(1)}, u32[]{:S(2)}, u32[]{:S(2)}) collective-permute-start(bf16[256,1024]{1,0:T(8,128)(2,1)S(1)} %get-tuple-element.91.refs_8_), channel_id=1, source_target_pairs={{0,16},{4,12},{8,24},{12,4},{16,0},{20,28},{24,8},{28,20},{1,17},{... | collective-permute-start | bytes 1572872 | tf_op jit(solution)/shard_map/ppermute | solution.py:670
  115.0 6.5 %shard_map.72 = (bf16[512,1024]{1,0:T(8,128)(2,1)}, f32[8,128]{1,0:T(8,128)S(1)}) custom-call(bf16[2,512,256]{2,1,0:T(8,128)(2,1)S(1)} %get-tuple-element.63.refs_12_.refs_1_.refs_0_, bf16[1,512,256]{2,1,0:T(8,128)(2,1)S(1)} %get-tuple-element.64.refs_5_.refs_2_.refs_1_, bf16[1,512,256]{2,1,0:T(8,128)(2,1)S(1)} %get-tuple-element.72.refs_7_.refs_3_.refs_2_, ...), custom_call_target="tpu_custom_call" | custom-call | flops 4000000000 | bytes 1048576 | tf_op jit(solution)/shard_map/pallas_call | solution.py:385
  121.5 1.9 %collective-permute-done.17.refs_1_ = bf16[128,2048]{1,0:T(8,128)(2,1)S(1)} collective-permute-done((bf16[128,2048]{1,0:T(8,128)(2,1)S(1)}, bf16[128,2048]{1,0:T(8,128)(2,1)S(1)}, u32[]{:S(2)}, u32[]{:S(2)}) %collective-permute-start.17) | collective-permute-done | bytes 524320 | tf_op jit(solution)/shard_map/ppermute | solution.py:670
  126.3 3.7 %collective-permute-done.18.refs_1_ = bf16[64,2048]{1,0:T(8,128)(2,1)S(1)} collective-permute-done((bf16[64,2048]{1,0:T(8,128)(2,1)S(1)}, bf16[64,2048]{1,0:T(8,128)(2,1)S(1)}, u32[]{:S(2)}, u32[]{:S(2)}) %collective-permute-start.18) | collective-permute-done | bytes 262176 | tf_op jit(solution)/shard_map/ppermute | solution.py:635
  132.3 1.9 %collective-permute-start.20 = (bf16[32,2048]{1,0:T(8,128)(2,1)S(1)}, bf16[32,2048]{1,0:T(8,128)(2,1)S(1)}, u32[]{:S(2)}, u32[]{:S(2)}) collective-permute-start(bf16[32,2048]{1,0:T(8,128)(2,1)S(1)} %get-tuple-element.100), channel_id=1, source_target_pairs={{0,2},{1,3},{2,0},{3,1},{4,6},{5,7},{6,4},{7,5},{8,10},{9,11},{10,... | collective-permute-start | bytes 393224 | tf_op jit(solution)/shard_map/ppermute | solution.py:635
  134.2 4.8 %collective-permute-done.22.refs_1_ = bf16[64,1024]{1,0:T(8,128)(2,1)S(1)} collective-permute-done((bf16[64,1024]{1,0:T(8,128)(2,1)S(1)}, bf16[64,1024]{1,0:T(8,128)(2,1)S(1)}, u32[]{:S(2)}, u32[]{:S(2)}) %collective-permute-start.22) | collective-permute-done | bytes 131104 | tf_op jit(solution)/shard_map/ppermute | solution.py:635
  139.8 1.6 %collective-permute-done.20.refs_1_ = bf16[32,2048]{1,0:T(8,128)(2,1)S(1)} collective-permute-done((bf16[32,2048]{1,0:T(8,128)(2,1)S(1)}, bf16[32,2048]{1,0:T(8,128)(2,1)S(1)}, u32[]{:S(2)}, u32[]{:S(2)}) %collective-permute-start.20) | collective-permute-done | bytes 131104 | tf_op jit(solution)/shard_map/ppermute | solution.py:635
  141.4 2.9 %collective-permute-done.23.refs_3_ = bf16[32,1024]{1,0:T(8,128)(2,1)S(1)} collective-permute-done((bf16[32,1024]{1,0:T(8,128)(2,1)S(1)}, bf16[32,1024]{1,0:T(8,128)(2,1)S(1)}, u32[]{:S(2)}, u32[]{:S(2)}) %collective-permute-start.23) | collective-permute-done | bytes 65568 | tf_op jit(solution)/shard_map/ppermute | solution.py:635
  (70 shorter events, 33.0 us)
Async XLA Ops:
  3.4 21.7 %collective-permute-start.1 = (bf16[192,1024]{1,0:T(8,128)(2,1)}, bf16[192,1024]{1,0:T(8,128)(2,1)S(1)}, u32[]{:S(2)}, u32[]{:S(2)}) collective-permute-start(bf16[192,1024]{1,0:T(8,128)(2,1)} %get-tuple-element.56), channel_id=1, source_target_pairs={{0,3},{1,0},{2,1},{3,2},{4,7},{5,4},{6,5},{7,6},{8,11},{9,8},{10,9... | collective-permute-start | bytes 1179656 | tf_op jit(solution)/shard_map/ppermute | solution.py:621
  8.4 17.9 %collective-permute-start = (bf16[192,1024]{1,0:T(8,128)(2,1)S(1)}, bf16[192,1024]{1,0:T(8,128)(2,1)S(1)}, u32[]{:S(2)}, u32[]{:S(2)}) collective-permute-start(bf16[192,1024]{1,0:T(8,128)(2,1)S(1)} %get-tuple-element.54.refs_0_.refs_2_), channel_id=1, source_target_pairs={{0,1},{1,2},{2,3},{3,0},{4,5},{5,6},{6,7},{7,4},{8,9},{9,10},{10,1... | collective-permute-start | bytes 1179656 | tf_op jit(solution)/shard_map/ppermute | solution.py:621
  11.0 18.0 %collective-permute-start.2 = (bf16[96,1024]{1,0:T(8,128)(2,1)}, bf16[96,1024]{1,0:T(8,128)(2,1)S(1)}, u32[]{:S(2)}, u32[]{:S(2)}) collective-permute-start(bf16[96,1024]{1,0:T(8,128)(2,1)} %get-tuple-element.57), channel_id=1, source_target_pairs={{0,4},{8,12},{4,0},{12,8},{1,5},{9,13},{5,1},{13,9},{2,6},{10,14},... | collective-permute-start | bytes 589832 | tf_op jit(solution)/shard_map/ppermute | solution.py:629
  11.0 18.0 %collective-permute-start.3 = (bf16[96,1024]{1,0:T(8,128)(2,1)}, bf16[96,1024]{1,0:T(8,128)(2,1)}, u32[]{:S(2)}, u32[]{:S(2)}) collective-permute-start(bf16[96,1024]{1,0:T(8,128)(2,1)} %get-tuple-element.58), channel_id=1, source_target_pairs={{4,8},{8,4},{5,9},{9,5},{6,10},{10,6},{7,11},{11,7},{20,24},{24,20... | collective-permute-start | bytes 589832 | tf_op jit(solution)/shard_map/ppermute | solution.py:629
  27.0 2.2 %collective-permute-start.4 = (bf16[96,1024]{1,0:T(8,128)(2,1)S(1)}, bf16[96,1024]{1,0:T(8,128)(2,1)S(1)}, u32[]{:S(2)}, u32[]{:S(2)}) collective-permute-start(bf16[96,1024]{1,0:T(8,128)(2,1)S(1)} %get-tuple-element.61), channel_id=1, source_target_pairs={{0,4},{8,12},{4,0},{12,8},{1,5},{9,13},{5,1},{13,9},{2,6},{10,14},... | collective-permute-start | bytes 589832 | tf_op jit(solution)/shard_map/ppermute | solution.py:629
  28.0 1.1 collective-permute-start.5
  45.6 15.6 %collective-permute-start.6 = (bf16[2,2,192,256]{3,2,1,0:T(8,128)(2,1)S(1)}, bf16[2,2,192,256]{3,2,1,0:T(8,128)(2,1)S(1)}, u32[]{:S(2)}, u32[]{:S(2)}) collective-permute-start(bf16[2,2,192,256]{3,2,1,0:T(8,128)(2,1)S(1)} %get-tuple-element.69), channel_id=1, source_target_pairs={{0,4},{8,12},{4,0},{12,8},{1,5},{9,13},{5,1},{13,9},{2,6},{10,14},... | collective-permute-start | bytes 1179656 | tf_op jit(solution)/shard_map/ppermute | solution.py:629
  51.5 9.6 %collective-permute-start.7 = (bf16[2,2,192,256]{3,2,1,0:T(8,128)(2,1)S(1)}, bf16[2,2,192,256]{3,2,1,0:T(8,128)(2,1)S(1)}, u32[]{:S(2)}, u32[]{:S(2)}) collective-permute-start(bf16[2,2,192,256]{3,2,1,0:T(8,128)(2,1)S(1)} %get-tuple-element.70), channel_id=1, source_target_pairs={{4,8},{8,4},{5,9},{9,5},{6,10},{10,6},{7,11},{11,7},{20,24},{24,20... | collective-permute-start | bytes 1179656 | tf_op jit(solution)/shard_map/ppermute | solution.py:629
  61.8 15.3 %collective-permute-start.8 = (bf16[2,2,192,256]{3,2,1,0:T(8,128)(2,1)S(1)}, bf16[2,2,192,256]{3,2,1,0:T(8,128)(2,1)S(1)}, u32[]{:S(2)}, u32[]{:S(2)}) collective-permute-start(bf16[2,2,192,256]{3,2,1,0:T(8,128)(2,1)S(1)} %get-tuple-element.74), channel_id=1, source_target_pairs={{0,1},{1,2},{2,3},{3,0},{4,5},{5,6},{6,7},{7,4},{8,9},{9,10},{10,1... | collective-permute-start | bytes 1179656 | tf_op jit(solution)/shard_map/ppermute | solution.py:621
  63.0 19.6 %collective-permute-start.9 = (bf16[2,2,192,256]{3,2,1,0:T(8,128)(2,1)S(1)}, bf16[2,2,192,256]{3,2,1,0:T(8,128)(2,1)S(1)}, u32[]{:S(2)}, u32[]{:S(2)}) collective-permute-start(bf16[2,2,192,256]{3,2,1,0:T(8,128)(2,1)S(1)} %get-tuple-element.71.refs_14_), channel_id=1, source_target_pairs={{0,3},{1,0},{2,1},{3,2},{4,7},{5,4},{6,5},{7,6},{8,11},{9,8},{10,9... | collective-permute-start | bytes 1179656 | tf_op jit(solution)/shard_map/ppermute | solution.py:621
  74.7 9.1 %collective-permute-start.10 = (bf16[2,2,192,256]{3,2,1,0:T(8,128)(2,1)S(1)}, bf16[2,2,192,256]{3,2,1,0:T(8,128)(2,1)S(1)}, u32[]{:S(2)}, u32[]{:S(2)}) collective-permute-start(bf16[2,2,192,256]{3,2,1,0:T(8,128)(2,1)S(1)} %get-tuple-element.79), channel_id=1, source_target_pairs={{0,4},{8,12},{4,0},{12,8},{1,5},{9,13},{5,1},{13,9},{2,6},{10,14},... | collective-permute-start | bytes 1179656 | tf_op jit(solution)/shard_map/ppermute | solution.py:629
  76.4 7.5 %collective-permute-start.11 = (bf16[2,2,192,256]{3,2,1,0:T(8,128)(2,1)S(1)}, bf16[2,2,192,256]{3,2,1,0:T(8,128)(2,1)S(1)}, u32[]{:S(2)}, u32[]{:S(2)}) collective-permute-start(bf16[2,2,192,256]{3,2,1,0:T(8,128)(2,1)S(1)} %get-tuple-element.80), channel_id=1, source_target_pairs={{4,8},{8,4},{5,9},{9,5},{6,10},{10,6},{7,11},{11,7},{20,24},{24,20... | collective-permute-start | bytes 1179656 | tf_op jit(solution)/shard_map/ppermute | solution.py:629
  85.8 6.8 %collective-permute-start.14 = (bf16[512,2048]{1,0:T(8,128)(2,1)S(1)}, bf16[512,2048]{1,0:T(8,128)(2,1)S(1)}, u32[]{:S(2)}, u32[]{:S(2)}) collective-permute-start(bf16[512,2048]{1,0:T(8,128)(2,1)S(1)} %shard_map.63.refs_6_), channel_id=1, source_target_pairs={{0,4},{4,0},{8,12},{12,8},{1,5},{5,1},{9,13},{13,9},{2,6},{6,2},{1... | collective-permute-start | bytes 6291464 | tf_op jit(solution)/shard_map/ppermute | solution.py:635
  87.5 13.8 %collective-permute-start.12 = (bf16[2,2,192,256]{3,2,1,0:T(8,128)(2,1)S(1)}, bf16[2,2,192,256]{3,2,1,0:T(8,128)(2,1)S(1)}, u32[]{:S(2)}, u32[]{:S(2)}) collective-permute-start(bf16[2,2,192,256]{3,2,1,0:T(8,128)(2,1)S(1)} %get-tuple-element.85), channel_id=1, source_target_pairs={{0,1},{1,2},{2,3},{3,0},{4,5},{5,6},{6,7},{7,4},{8,9},{9,10},{10,1... | collective-permute-start | bytes 1179656 | tf_op jit(solution)/shard_map/ppermute | solution.py:621
  88.0 19.5 %collective-permute-start.13 = (bf16[2,2,192,256]{3,2,1,0:T(8,128)(2,1)S(1)}, bf16[2,2,192,256]{3,2,1,0:T(8,128)(2,1)S(1)}, u32[]{:S(2)}, u32[]{:S(2)}) collective-permute-start(bf16[2,2,192,256]{3,2,1,0:T(8,128)(2,1)S(1)} %get-tuple-element.86.refs_6_), channel_id=1, source_target_pairs={{0,3},{1,0},{2,1},{3,2},{4,7},{5,4},{6,5},{7,6},{8,11},{9,8},{10,9... | collective-permute-start | bytes 1179656 | tf_op jit(solution)/shard_map/ppermute | solution.py:621
  93.1 15.5 %collective-permute-start.15 = (bf16[256,2048]{1,0:T(8,128)(2,1)S(1)}, bf16[256,2048]{1,0:T(8,128)(2,1)S(1)}, u32[]{:S(2)}, u32[]{:S(2)}) collective-permute-start(bf16[256,2048]{1,0:T(8,128)(2,1)S(1)} %get-tuple-element.89), channel_id=1, source_target_pairs={{0,16},{4,12},{8,24},{12,4},{16,0},{20,28},{24,8},{28,20},{1,17},{... | collective-permute-start | bytes 3145736 | tf_op jit(solution)/shard_map/ppermute | solution.py:670
  110.5 2.7 %collective-permute-start.16 = (bf16[512,1024]{1,0:T(8,128)(2,1)S(1)}, bf16[512,1024]{1,0:T(8,128)(2,1)S(1)}, u32[]{:S(2)}, u32[]{:S(2)}) collective-permute-start(bf16[512,1024]{1,0:T(8,128)(2,1)S(1)} %shard_map.69.refs_3_), channel_id=1, source_target_pairs={{0,4},{4,0},{8,12},{12,8},{1,5},{5,1},{9,13},{13,9},{2,6},{6,2},{1... | collective-permute-start | bytes 3145736 | tf_op jit(solution)/shard_map/ppermute | solution.py:635
  110.6 12.8 %collective-permute-start.17 = (bf16[128,2048]{1,0:T(8,128)(2,1)S(1)}, bf16[128,2048]{1,0:T(8,128)(2,1)S(1)}, u32[]{:S(2)}, u32[]{:S(2)}) collective-permute-start(bf16[128,2048]{1,0:T(8,128)(2,1)S(1)} %get-tuple-element.93), channel_id=1, source_target_pairs={{0,8},{4,20},{8,0},{12,28},{16,24},{20,4},{24,16},{28,12},{1,9},{5... | collective-permute-start | bytes 1572872 | tf_op jit(solution)/shard_map/ppermute | solution.py:670
  113.4 11.5 %collective-permute-start.19 = (bf16[256,1024]{1,0:T(8,128)(2,1)S(1)}, bf16[256,1024]{1,0:T(8,128)(2,1)S(1)}, u32[]{:S(2)}, u32[]{:S(2)}) collective-permute-start(bf16[256,1024]{1,0:T(8,128)(2,1)S(1)} %get-tuple-element.91.refs_8_), channel_id=1, source_target_pairs={{0,16},{4,12},{8,24},{12,4},{16,0},{20,28},{24,8},{28,20},{1,17},{... | collective-permute-start | bytes 1572872 | tf_op jit(solution)/shard_map/ppermute | solution.py:670
  123.5 6.5 %collective-permute-start.18 = (bf16[64,2048]{1,0:T(8,128)(2,1)S(1)}, bf16[64,2048]{1,0:T(8,128)(2,1)S(1)}, u32[]{:S(2)}, u32[]{:S(2)}) collective-permute-start(bf16[64,2048]{1,0:T(8,128)(2,1)S(1)} %get-tuple-element.96), channel_id=1, source_target_pairs={{0,1},{1,0},{2,3},{3,2},{4,5},{5,4},{6,7},{7,6},{8,9},{9,8},{10,11... | collective-permute-start | bytes 786440 | tf_op jit(solution)/shard_map/ppermute | solution.py:635
  125.0 6.4 %collective-permute-start.21 = (bf16[128,1024]{1,0:T(8,128)(2,1)S(1)}, bf16[128,1024]{1,0:T(8,128)(2,1)S(1)}, u32[]{:S(2)}, u32[]{:S(2)}) collective-permute-start(bf16[128,1024]{1,0:T(8,128)(2,1)S(1)} %get-tuple-element.101), channel_id=1, source_target_pairs={{0,8},{4,20},{8,0},{12,28},{16,24},{20,4},{24,16},{28,12},{1,9},{5... | collective-permute-start | bytes 786440 | tf_op jit(solution)/shard_map/ppermute | solution.py:670
  131.5 7.5 %collective-permute-start.22 = (bf16[64,1024]{1,0:T(8,128)(2,1)S(1)}, bf16[64,1024]{1,0:T(8,128)(2,1)S(1)}, u32[]{:S(2)}, u32[]{:S(2)}) collective-permute-start(bf16[64,1024]{1,0:T(8,128)(2,1)S(1)} %get-tuple-element.103), channel_id=1, source_target_pairs={{0,1},{1,0},{2,3},{3,2},{4,5},{5,4},{6,7},{7,6},{8,9},{9,8},{10,11... | collective-permute-start | bytes 393224 | tf_op jit(solution)/shard_map/ppermute | solution.py:635
  132.3 9.1 %collective-permute-start.20 = (bf16[32,2048]{1,0:T(8,128)(2,1)S(1)}, bf16[32,2048]{1,0:T(8,128)(2,1)S(1)}, u32[]{:S(2)}, u32[]{:S(2)}) collective-permute-start(bf16[32,2048]{1,0:T(8,128)(2,1)S(1)} %get-tuple-element.100), channel_id=1, source_target_pairs={{0,2},{1,3},{2,0},{3,1},{4,6},{5,7},{6,4},{7,5},{8,10},{9,11},{10,... | collective-permute-start | bytes 393224 | tf_op jit(solution)/shard_map/ppermute | solution.py:635
  139.1 5.2 %collective-permute-start.23 = (bf16[32,1024]{1,0:T(8,128)(2,1)S(1)}, bf16[32,1024]{1,0:T(8,128)(2,1)S(1)}, u32[]{:S(2)}, u32[]{:S(2)}) collective-permute-start(bf16[32,1024]{1,0:T(8,128)(2,1)S(1)} %get-tuple-element.105), channel_id=1, source_target_pairs={{0,2},{1,3},{2,0},{3,1},{4,6},{5,7},{6,4},{7,5},{8,10},{9,11},{10,... | collective-permute-start | bytes 196616 | tf_op jit(solution)/shard_map/ppermute | solution.py:635
  (8 other events, 39.5 us)

commit v4 on v3

--- a/solution.py
+++ b/solution.py
@@ -694,7 +694,7 @@
     first, stages = reduce_stages()
     half = width // 2
     rows_keep, rows_send = row_blocks(start, own, feature_orders(first, stages), [last_cols])
-    corners = pack_corners(start, left, right, band_rows, [masks, qkv, rows_keep, rows_send])
+    corners = pack_corners(start, left, right, band_rows, [masks, qkv])
     halo = (left, right, *rim_rows, *swapped(*corners, "lat"))
     scale = float(tokens * n_dp * n_lat * n_lon) ** -0.5
 
@@ -715,7 +715,7 @@
         return finish(start, mids, *rims, *sides, put, parts, band_rows, band_cols, after, flops)
 
     groups = HEADS // GROUP
-    one = attend(0, slots, [], [])
+    one = attend(0, slots, [], [rows_keep])
     rims_1 = swapped(one[1], one[2], "lat")
     two = attend(slots, groups - slots - 1, [], [one[0]])
     sent, *sides_1 = return_sides([one], rims_1, [two[0]])

time: 145 us -> 142 us (0.979)
  Pallas kernels: 64.5 us -> 61.8 us
  starting transfers between devices: 36.5 us -> 34.4 us
  waiting for transfers between devices: 37.8 us -> 39.6 us
    ppermute x6, waiting for transfers between devices: 19.7 us -> 23 us  [shifted(): return lax.ppermute(array, axis, route)]
    ppermute x8, starting transfers between devices: 12.2 us -> 10.4 us  [swapped(): lax.ppermute(array, axis, route(pairs[offset::2]))]
    pallas_call x23, Pallas kernels: 15.2 us -> 13.7 us  [on_chip(): pl.pallas_call(run, in_specs=[pl.BlockSpec(memory_space=pltpu.SMEM)] * le...]
  transfers between devices with their start and end apart: 24 -> 24, of which waited for: 13 -> 12; matrix products, arithmetic and copies ran while one was open for 0% -> 0% of each run, Pallas kernels for 28% -> 28%
where the time goes in v4:
time: 142 us
  Pallas kernels  61.8 us (44%)
  waiting for transfers between devices  39.6 us (28%)
  starting transfers between devices  34.4 us (24%)
  local copies, waits for them, and re-layouts  5.25 us (4%)
    pallas_call x3, Pallas kernels, attention_grads(): pl.pallas_call(functools.partial(attention_kernel, band_rows, band_cols,...  32.7 us
    ppermute x6, waiting for transfers between devices, shifted(): return lax.ppermute(array, axis, route)  23 us
    pallas_call x23, Pallas kernels, on_chip(): pl.pallas_call(run, in_specs=[pl.BlockSpec(memory_space=pltpu.SMEM)] * le...  13.7 us
    ppermute x6, starting transfers between devices, shifted(): return lax.ppermute(array, axis, route)  12.8 us
    ppermute x6, waiting for transfers between devices, exchanged(): lax.ppermute(array, axis, [(i, i ^ flip) for i in range(lax.axis_size(axi...  12.6 us
    ppermute x8, starting transfers between devices, swapped(): lax.ppermute(array, axis, route(pairs[offset::2]))  10.4 us
    pallas_call x1, Pallas kernels, input_grads(): pl.pallas_call(kernel, grid=(steps,), in_specs=[pl.BlockSpec(memory_space...  6.5 us
    ppermute x6, starting transfers between devices, exchanged(): lax.ppermute(array, axis, [(i, i ^ flip) for i in range(lax.axis_size(axi...  5.63 us
  transfers between devices with their start and end apart: 24, of which 12 were waited for; matrix products, arithmetic and copies ran while one was open for 0% of the time, Pallas kernels for 28%

profile of v4, /device:TPU:0, one launch (start us, length us, event | category | flops | bytes accessed | tf_op | source)
XLA Modules:
  0.0 142.1 jit_solution(11415983064821811032)
XLA Ops:
  2.6 5.1 %collective-permute-start.1 = (bf16[192,1024]{1,0:T(8,128)(2,1)S(1)}, bf16[192,1024]{1,0:T(8,128)(2,1)S(1)}, u32[]{:S(2)}, u32[]{:S(2)}) collective-permute-start(bf16[192,1024]{1,0:T(8,128)(2,1)S(1)} %get-tuple-element.56), channel_id=1, source_target_pairs={{0,3},{1,0},{2,1},{3,2},{4,7},{5,4},{6,5},{7,6},{8,11},{9,8},{10,9... | collective-permute-start | bytes 1179656 | tf_op jit(solution)/shard_map/ppermute | solution.py:621
  10.4 4.0 %shard_map.50.refs_3_.refs_1_ = bf16[8,512,128]{2,1,0:T(8,128)(2,1)} custom-call(s32[3]{0:T(128)} %copy-done.5), custom_call_target="tpu_custom_call" | custom-call | flops 10000000 | bytes 2097152 | tf_op jit(solution)/shard_map/pallas_call | solution.py:69
  14.4 2.8 %copy-done.3 = bf16[1024,3072]{1,0:T(8,128)(2,1)S(1)} copy-done((bf16[1024,3072]{1,0:T(8,128)(2,1)S(1)}, bf16[1024,3072]{1,0:T(8,128)(2,1)}, u32[]{:S(2)}) %copy-start.3) | copy-done | bytes 6291480
  17.2 4.9 %shard_map.54.refs_4_.refs_9_ = bf16[512,3072]{1,0:T(8,128)(2,1)S(1)} custom-call(bf16[512,1024]{1,0:T(8,128)(2,1)S(1)} %bitcast.8, bf16[1024,3072]{1,0:T(8,128)(2,1)S(1)} %copy-done.3, bf16[192,1024]{1,0:T(8,128)(2,1)S(1)} %get-tuple-element.54.refs_0_.refs_2_), custom_call_target="tpu_custom_call" | custom-call | flops 1000000000 | bytes 1048576 | tf_op jit(solution)/shard_map/pallas_call | solution.py:342
  22.1 3.3 %collective-permute-done.refs_1_.refs_3_ = bf16[192,1024]{1,0:T(8,128)(2,1)S(1)} collective-permute-done((bf16[192,1024]{1,0:T(8,128)(2,1)S(1)}, bf16[192,1024]{1,0:T(8,128)(2,1)S(1)}, u32[]{:S(2)}, u32[]{:S(2)}) %collective-permute-start) | collective-permute-done | bytes 393248 | tf_op jit(solution)/shard_map/ppermute | solution.py:621
  28.1 16.1 %shard_map.57 = (bf16[2,512,256]{2,1,0:T(8,128)(2,1)S(1)}, bf16[2,2,192,256]{3,2,1,0:T(8,128)(2,1)S(1)}, bf16[2,2,192,256]{3,2,1,0:T(8,128)(2,1)S(1)}, bf16[2,2,...) custom-call(s32[3]{0:T(128)S(1)} %copy-done.6, ...), custom_call_target="tpu_custom_call" | custom-call | flops 28000000000 | bytes 16777216 | tf_op jit(solution)/shard_map/pallas_call | solution.py:275
  44.2 5.5 %collective-permute-start.6 = (bf16[2,2,192,256]{3,2,1,0:T(8,128)(2,1)S(1)}, bf16[2,2,192,256]{3,2,1,0:T(8,128)(2,1)S(1)}, u32[]{:S(2)}, u32[]{:S(2)}) collective-permute-start(bf16[2,2,192,256]{3,2,1,0:T(8,128)(2,1)S(1)} %get-tuple-element.68), channel_id=1, source_target_pairs={{0,4},{8,12},{4,0},{12,8},{1,5},{9,13},{5,1},{13,9},{2,6},{10,14},... | collective-permute-start | bytes 1179656 | tf_op jit(solution)/shard_map/ppermute | solution.py:629
  50.6 8.3 %shard_map.58 = (bf16[1,512,256]{2,1,0:T(8,128)(2,1)S(1)}, bf16[1,2,192,256]{3,2,1,0:T(8,128)(2,1)S(1)}, bf16[1,2,192,256]{3,2,1,0:T(8,128)(2,1)S(1)}, bf16[1,2,...) custom-call(s32[3]{0:T(128)S(1)} %copy-done.6, ...), custom_call_target="tpu_custom_call" | custom-call | flops 14000000000 | bytes 8388608 | tf_op jit(solution)/shard_map/pallas_call | solution.py:275
  59.6 1.7 %collective-permute-start.8 = (bf16[2,2,192,256]{3,2,1,0:T(8,128)(2,1)S(1)}, bf16[2,2,192,256]{3,2,1,0:T(8,128)(2,1)S(1)}, u32[]{:S(2)}, u32[]{:S(2)}) collective-permute-start(bf16[2,2,192,256]{3,2,1,0:T(8,128)(2,1)S(1)} %get-tuple-element.73), channel_id=1, source_target_pairs={{0,1},{1,2},{2,3},{3,0},{4,5},{5,6},{6,7},{7,4},{8,9},{9,10},{10,1... | collective-permute-start | bytes 1179656 | tf_op jit(solution)/shard_map/ppermute | solution.py:621
  61.3 2.2 %collective-permute-start.9 = (bf16[2,2,192,256]{3,2,1,0:T(8,128)(2,1)S(1)}, bf16[2,2,192,256]{3,2,1,0:T(8,128)(2,1)S(1)}, u32[]{:S(2)}, u32[]{:S(2)}) collective-permute-start(bf16[2,2,192,256]{3,2,1,0:T(8,128)(2,1)S(1)} %get-tuple-element.70.refs_14_), channel_id=1, source_target_pairs={{0,3},{1,0},{2,1},{3,2},{4,7},{5,4},{6,5},{7,6},{8,11},{9,8},{10,9... | collective-permute-start | bytes 1179656 | tf_op jit(solution)/shard_map/ppermute | solution.py:621
  63.5 8.4 %shard_map.60 = (bf16[1,512,256]{2,1,0:T(8,128)(2,1)S(1)}, bf16[2,2,192,256]{3,2,1,0:T(8,128)(2,1)S(1)}, bf16[2,2,192,256]{3,2,1,0:T(8,128)(2,1)S(1)}, bf16[1,2,...) custom-call(s32[3]{0:T(128)S(1)} %copy-done.6, ...), custom_call_target="tpu_custom_call" | custom-call | flops 14000000000 | bytes 8388608 | tf_op jit(solution)/shard_map/pallas_call | solution.py:275
  71.8 1.9 %collective-permute-start.10 = (bf16[2,2,192,256]{3,2,1,0:T(8,128)(2,1)S(1)}, bf16[2,2,192,256]{3,2,1,0:T(8,128)(2,1)S(1)}, u32[]{:S(2)}, u32[]{:S(2)}) collective-permute-start(bf16[2,2,192,256]{3,2,1,0:T(8,128)(2,1)S(1)} %get-tuple-element.78), channel_id=1, source_target_pairs={{0,4},{8,12},{4,0},{12,8},{1,5},{9,13},{5,1},{13,9},{2,6},{10,14},... | collective-permute-start | bytes 1179656 | tf_op jit(solution)/shard_map/ppermute | solution.py:629
  74.4 6.9 %collective-permute-done.9.refs_5_ = bf16[2,2,192,256]{3,2,1,0:T(8,128)(2,1)S(1)} collective-permute-done((bf16[2,2,192,256]{3,2,1,0:T(8,128)(2,1)S(1)}, bf16[2,2,192,256]{3,2,1,0:T(8,128)(2,1)S(1)}, u32[]{:S(2)}, u32[]{:S(2)}) %collective-permute-start.9) | collective-permute-done | bytes 393248 | tf_op jit(solution)/shard_map/ppermute | solution.py:621
  85.2 3.4 %collective-permute-start.13 = (bf16[2,2,192,256]{3,2,1,0:T(8,128)(2,1)S(1)}, bf16[2,2,192,256]{3,2,1,0:T(8,128)(2,1)S(1)}, u32[]{:S(2)}, u32[]{:S(2)}) collective-permute-start(bf16[2,2,192,256]{3,2,1,0:T(8,128)(2,1)S(1)} %get-tuple-element.85.refs_6_), channel_id=1, source_target_pairs={{0,3},{1,0},{2,1},{3,2},{4,7},{5,4},{6,5},{7,6},{8,11},{9,8},{10,9... | collective-permute-start | bytes 1179656 | tf_op jit(solution)/shard_map/ppermute | solution.py:621
  90.4 1.6 %collective-permute-start.15 = (bf16[256,2048]{1,0:T(8,128)(2,1)S(1)}, bf16[256,2048]{1,0:T(8,128)(2,1)S(1)}, u32[]{:S(2)}, u32[]{:S(2)}) collective-permute-start(bf16[256,2048]{1,0:T(8,128)(2,1)S(1)} %get-tuple-element.89), channel_id=1, source_target_pairs={{0,16},{4,12},{8,24},{12,4},{16,0},{20,28},{24,8},{28,20},{1,17},{... | collective-permute-start | bytes 3145736 | tf_op jit(solution)/shard_map/ppermute | solution.py:670
  92.0 6.6 %collective-permute-done.12.refs_5_ = bf16[2,2,192,256]{3,2,1,0:T(8,128)(2,1)S(1)} collective-permute-done((bf16[2,2,192,256]{3,2,1,0:T(8,128)(2,1)S(1)}, bf16[2,2,192,256]{3,2,1,0:T(8,128)(2,1)S(1)}, u32[]{:S(2)}, u32[]{:S(2)}) %collective-permute-start.12) | collective-permute-done | bytes 393248 | tf_op jit(solution)/shard_map/ppermute | solution.py:621
  98.6 6.1 %collective-permute-done.13.refs_6_ = bf16[2,2,192,256]{3,2,1,0:T(8,128)(2,1)S(1)} collective-permute-done((bf16[2,2,192,256]{3,2,1,0:T(8,128)(2,1)S(1)}, bf16[2,2,192,256]{3,2,1,0:T(8,128)(2,1)S(1)}, u32[]{:S(2)}, u32[]{:S(2)}) %collective-permute-start.13) | collective-permute-done | bytes 393248 | tf_op jit(solution)/shard_map/ppermute | solution.py:621
  112.1 6.5 %shard_map.72 = (bf16[512,1024]{1,0:T(8,128)(2,1)}, f32[8,128]{1,0:T(8,128)S(1)}) custom-call(bf16[2,512,256]{2,1,0:T(8,128)(2,1)S(1)} %get-tuple-element.62.refs_12_.refs_1_.refs_0_, bf16[1,512,256]{2,1,0:T(8,128)(2,1)S(1)} %get-tuple-element.63.refs_5_.refs_2_.refs_1_, bf16[1,512,256]{2,1,0:T(8,128)(2,1)S(1)} %get-tuple-element.71.refs_7_.refs_3_.refs_2_, ...), custom_call_target="tpu_custom_call" | custom-call | flops 4000000000 | bytes 1048576 | tf_op jit(solution)/shard_map/pallas_call | solution.py:385
  118.6 1.9 %collective-permute-done.17.refs_1_ = bf16[128,2048]{1,0:T(8,128)(2,1)S(1)} collective-permute-done((bf16[128,2048]{1,0:T(8,128)(2,1)S(1)}, bf16[128,2048]{1,0:T(8,128)(2,1)S(1)}, u32[]{:S(2)}, u32[]{:S(2)}) %collective-permute-start.17) | collective-permute-done | bytes 524320 | tf_op jit(solution)/shard_map/ppermute | solution.py:670
  123.4 3.7 %collective-permute-done.18.refs_1_ = bf16[64,2048]{1,0:T(8,128)(2,1)S(1)} collective-permute-done((bf16[64,2048]{1,0:T(8,128)(2,1)S(1)}, bf16[64,2048]{1,0:T(8,128)(2,1)S(1)}, u32[]{:S(2)}, u32[]{:S(2)}) %collective-permute-start.18) | collective-permute-done | bytes 262176 | tf_op jit(solution)/shard_map/ppermute | solution.py:635
  129.4 2.3 %collective-permute-start.20 = (bf16[32,2048]{1,0:T(8,128)(2,1)S(1)}, bf16[32,2048]{1,0:T(8,128)(2,1)S(1)}, u32[]{:S(2)}, u32[]{:S(2)}) collective-permute-start(bf16[32,2048]{1,0:T(8,128)(2,1)S(1)} %get-tuple-element.100), channel_id=1, source_target_pairs={{0,2},{1,3},{2,0},{3,1},{4,6},{5,7},{6,4},{7,5},{8,10},{9,11},{10,... | collective-permute-start | bytes 393224 | tf_op jit(solution)/shard_map/ppermute | solution.py:635
  131.7 4.4 %collective-permute-done.22.refs_1_ = bf16[64,1024]{1,0:T(8,128)(2,1)S(1)} collective-permute-done((bf16[64,1024]{1,0:T(8,128)(2,1)S(1)}, bf16[64,1024]{1,0:T(8,128)(2,1)S(1)}, u32[]{:S(2)}, u32[]{:S(2)}) %collective-permute-start.22) | collective-permute-done | bytes 131104 | tf_op jit(solution)/shard_map/ppermute | solution.py:635
  137.6 1.7 %collective-permute-done.20.refs_1_ = bf16[32,2048]{1,0:T(8,128)(2,1)S(1)} collective-permute-done((bf16[32,2048]{1,0:T(8,128)(2,1)S(1)}, bf16[32,2048]{1,0:T(8,128)(2,1)S(1)}, u32[]{:S(2)}, u32[]{:S(2)}) %collective-permute-start.20) | collective-permute-done | bytes 131104 | tf_op jit(solution)/shard_map/ppermute | solution.py:635
  139.3 2.1 %collective-permute-done.23.refs_3_ = bf16[32,1024]{1,0:T(8,128)(2,1)S(1)} collective-permute-done((bf16[32,1024]{1,0:T(8,128)(2,1)S(1)}, bf16[32,1024]{1,0:T(8,128)(2,1)S(1)}, u32[]{:S(2)}, u32[]{:S(2)}) %collective-permute-start.23) | collective-permute-done | bytes 65568 | tf_op jit(solution)/shard_map/ppermute | solution.py:635
  (70 shorter events, 29.8 us)
Async XLA Ops:
  2.6 19.5 %collective-permute-start.1 = (bf16[192,1024]{1,0:T(8,128)(2,1)S(1)}, bf16[192,1024]{1,0:T(8,128)(2,1)S(1)}, u32[]{:S(2)}, u32[]{:S(2)}) collective-permute-start(bf16[192,1024]{1,0:T(8,128)(2,1)S(1)} %get-tuple-element.56), channel_id=1, source_target_pairs={{0,3},{1,0},{2,1},{3,2},{4,7},{5,4},{6,5},{7,6},{8,11},{9,8},{10,9... | collective-permute-start | bytes 1179656 | tf_op jit(solution)/shard_map/ppermute | solution.py:621
  7.7 17.7 %collective-permute-start = (bf16[192,1024]{1,0:T(8,128)(2,1)S(1)}, bf16[192,1024]{1,0:T(8,128)(2,1)S(1)}, u32[]{:S(2)}, u32[]{:S(2)}) collective-permute-start(bf16[192,1024]{1,0:T(8,128)(2,1)S(1)} %get-tuple-element.54.refs_0_.refs_2_), channel_id=1, source_target_pairs={{0,1},{1,2},{2,3},{3,0},{4,5},{5,6},{6,7},{7,4},{8,9},{9,10},{10,1... | collective-permute-start | bytes 1179656 | tf_op jit(solution)/shard_map/ppermute | solution.py:621
  9.6 18.5 %collective-permute-start.2 = (bf16[96,1024]{1,0:T(8,128)(2,1)S(1)}, bf16[96,1024]{1,0:T(8,128)(2,1)S(1)}, u32[]{:S(2)}, u32[]{:S(2)}) collective-permute-start(bf16[96,1024]{1,0:T(8,128)(2,1)S(1)} %get-tuple-element.57), channel_id=1, source_target_pairs={{0,4},{8,12},{4,0},{12,8},{1,5},{9,13},{5,1},{13,9},{2,6},{10,14},... | collective-permute-start | bytes 589832 | tf_op jit(solution)/shard_map/ppermute | solution.py:629
  9.7 18.4 %collective-permute-start.3 = (bf16[96,1024]{1,0:T(8,128)(2,1)S(1)}, bf16[96,1024]{1,0:T(8,128)(2,1)S(1)}, u32[]{:S(2)}, u32[]{:S(2)}) collective-permute-start(bf16[96,1024]{1,0:T(8,128)(2,1)S(1)} %get-tuple-element.58), channel_id=1, source_target_pairs={{4,8},{8,4},{5,9},{9,5},{6,10},{10,6},{7,11},{11,7},{20,24},{24,20... | collective-permute-start | bytes 589832 | tf_op jit(solution)/shard_map/ppermute | solution.py:629
  26.1 2.1 %collective-permute-start.4 = (bf16[96,1024]{1,0:T(8,128)(2,1)S(1)}, bf16[96,1024]{1,0:T(8,128)(2,1)S(1)}, u32[]{:S(2)}, u32[]{:S(2)}) collective-permute-start(bf16[96,1024]{1,0:T(8,128)(2,1)S(1)} %get-tuple-element.59), channel_id=1, source_target_pairs={{0,4},{8,12},{4,0},{12,8},{1,5},{9,13},{5,1},{13,9},{2,6},{10,14},... | collective-permute-start | bytes 589832 | tf_op jit(solution)/shard_map/ppermute | solution.py:629
  26.1 2.0 %collective-permute-start.5 = (bf16[96,1024]{1,0:T(8,128)(2,1)S(1)}, bf16[96,1024]{1,0:T(8,128)(2,1)S(1)}, u32[]{:S(2)}, u32[]{:S(2)}) collective-permute-start(bf16[96,1024]{1,0:T(8,128)(2,1)S(1)} %get-tuple-element.60), channel_id=1, source_target_pairs={{4,8},{8,4},{5,9},{9,5},{6,10},{10,6},{7,11},{11,7},{20,24},{24,20... | collective-permute-start | bytes 589832 | tf_op jit(solution)/shard_map/ppermute | solution.py:629
  44.2 14.7 %collective-permute-start.6 = (bf16[2,2,192,256]{3,2,1,0:T(8,128)(2,1)S(1)}, bf16[2,2,192,256]{3,2,1,0:T(8,128)(2,1)S(1)}, u32[]{:S(2)}, u32[]{:S(2)}) collective-permute-start(bf16[2,2,192,256]{3,2,1,0:T(8,128)(2,1)S(1)} %get-tuple-element.68), channel_id=1, source_target_pairs={{0,4},{8,12},{4,0},{12,8},{1,5},{9,13},{5,1},{13,9},{2,6},{10,14},... | collective-permute-start | bytes 1179656 | tf_op jit(solution)/shard_map/ppermute | solution.py:629
  49.7 9.2 %collective-permute-start.7 = (bf16[2,2,192,256]{3,2,1,0:T(8,128)(2,1)S(1)}, bf16[2,2,192,256]{3,2,1,0:T(8,128)(2,1)S(1)}, u32[]{:S(2)}, u32[]{:S(2)}) collective-permute-start(bf16[2,2,192,256]{3,2,1,0:T(8,128)(2,1)S(1)} %get-tuple-element.69), channel_id=1, source_target_pairs={{4,8},{8,4},{5,9},{9,5},{6,10},{10,6},{7,11},{11,7},{20,24},{24,20... | collective-permute-start | bytes 1179656 | tf_op jit(solution)/shard_map/ppermute | solution.py:629
  59.6 14.8 %collective-permute-start.8 = (bf16[2,2,192,256]{3,2,1,0:T(8,128)(2,1)S(1)}, bf16[2,2,192,256]{3,2,1,0:T(8,128)(2,1)S(1)}, u32[]{:S(2)}, u32[]{:S(2)}) collective-permute-start(bf16[2,2,192,256]{3,2,1,0:T(8,128)(2,1)S(1)} %get-tuple-element.73), channel_id=1, source_target_pairs={{0,1},{1,2},{2,3},{3,0},{4,5},{5,6},{6,7},{7,4},{8,9},{9,10},{10,1... | collective-permute-start | bytes 1179656 | tf_op jit(solution)/shard_map/ppermute | solution.py:621
  61.3 20.1 %collective-permute-start.9 = (bf16[2,2,192,256]{3,2,1,0:T(8,128)(2,1)S(1)}, bf16[2,2,192,256]{3,2,1,0:T(8,128)(2,1)S(1)}, u32[]{:S(2)}, u32[]{:S(2)}) collective-permute-start(bf16[2,2,192,256]{3,2,1,0:T(8,128)(2,1)S(1)} %get-tuple-element.70.refs_14_), channel_id=1, source_target_pairs={{0,3},{1,0},{2,1},{3,2},{4,7},{5,4},{6,5},{7,6},{8,11},{9,8},{10,9... | collective-permute-start | bytes 1179656 | tf_op jit(solution)/shard_map/ppermute | solution.py:621
  71.8 10.8 %collective-permute-start.10 = (bf16[2,2,192,256]{3,2,1,0:T(8,128)(2,1)S(1)}, bf16[2,2,192,256]{3,2,1,0:T(8,128)(2,1)S(1)}, u32[]{:S(2)}, u32[]{:S(2)}) collective-permute-start(bf16[2,2,192,256]{3,2,1,0:T(8,128)(2,1)S(1)} %get-tuple-element.78), channel_id=1, source_target_pairs={{0,4},{8,12},{4,0},{12,8},{1,5},{9,13},{5,1},{13,9},{2,6},{10,14},... | collective-permute-start | bytes 1179656 | tf_op jit(solution)/shard_map/ppermute | solution.py:629
  73.7 8.9 %collective-permute-start.11 = (bf16[2,2,192,256]{3,2,1,0:T(8,128)(2,1)S(1)}, bf16[2,2,192,256]{3,2,1,0:T(8,128)(2,1)S(1)}, u32[]{:S(2)}, u32[]{:S(2)}) collective-permute-start(bf16[2,2,192,256]{3,2,1,0:T(8,128)(2,1)S(1)} %get-tuple-element.79), channel_id=1, source_target_pairs={{4,8},{8,4},{5,9},{9,5},{6,10},{10,6},{7,11},{11,7},{20,24},{24,20... | collective-permute-start | bytes 1179656 | tf_op jit(solution)/shard_map/ppermute | solution.py:629
  84.6 5.3 %collective-permute-start.14 = (bf16[512,2048]{1,0:T(8,128)(2,1)S(1)}, bf16[512,2048]{1,0:T(8,128)(2,1)S(1)}, u32[]{:S(2)}, u32[]{:S(2)}) collective-permute-start(bf16[512,2048]{1,0:T(8,128)(2,1)S(1)} %shard_map.63.refs_6_), channel_id=1, source_target_pairs={{0,4},{4,0},{8,12},{12,8},{1,5},{5,1},{9,13},{13,9},{2,6},{6,2},{1... | collective-permute-start | bytes 6291464 | tf_op jit(solution)/shard_map/ppermute | solution.py:635
  84.8 13.8 %collective-permute-start.12 = (bf16[2,2,192,256]{3,2,1,0:T(8,128)(2,1)S(1)}, bf16[2,2,192,256]{3,2,1,0:T(8,128)(2,1)S(1)}, u32[]{:S(2)}, u32[]{:S(2)}) collective-permute-start(bf16[2,2,192,256]{3,2,1,0:T(8,128)(2,1)S(1)} %get-tuple-element.84), channel_id=1, source_target_pairs={{0,1},{1,2},{2,3},{3,0},{4,5},{5,6},{6,7},{7,4},{8,9},{9,10},{10,1... | collective-permute-start | bytes 1179656 | tf_op jit(solution)/shard_map/ppermute | solution.py:621
  85.2 19.4 %collective-permute-start.13 = (bf16[2,2,192,256]{3,2,1,0:T(8,128)(2,1)S(1)}, bf16[2,2,192,256]{3,2,1,0:T(8,128)(2,1)S(1)}, u32[]{:S(2)}, u32[]{:S(2)}) collective-permute-start(bf16[2,2,192,256]{3,2,1,0:T(8,128)(2,1)S(1)} %get-tuple-element.85.refs_6_), channel_id=1, source_target_pairs={{0,3},{1,0},{2,1},{3,2},{4,7},{5,4},{6,5},{7,6},{8,11},{9,8},{10,9... | collective-permute-start | bytes 1179656 | tf_op jit(solution)/shard_map/ppermute | solution.py:621
  90.4 15.3 %collective-permute-start.15 = (bf16[256,2048]{1,0:T(8,128)(2,1)S(1)}, bf16[256,2048]{1,0:T(8,128)(2,1)S(1)}, u32[]{:S(2)}, u32[]{:S(2)}) collective-permute-start(bf16[256,2048]{1,0:T(8,128)(2,1)S(1)} %get-tuple-element.89), channel_id=1, source_target_pairs={{0,16},{4,12},{8,24},{12,4},{16,0},{20,28},{24,8},{28,20},{1,17},{... | collective-permute-start | bytes 3145736 | tf_op jit(solution)/shard_map/ppermute | solution.py:670
  107.6 2.7 %collective-permute-start.16 = (bf16[512,1024]{1,0:T(8,128)(2,1)S(1)}, bf16[512,1024]{1,0:T(8,128)(2,1)S(1)}, u32[]{:S(2)}, u32[]{:S(2)}) collective-permute-start(bf16[512,1024]{1,0:T(8,128)(2,1)S(1)} %shard_map.69.refs_3_), channel_id=1, source_target_pairs={{0,4},{4,0},{8,12},{12,8},{1,5},{5,1},{9,13},{13,9},{2,6},{6,2},{1... | collective-permute-start | bytes 3145736 | tf_op jit(solution)/shard_map/ppermute | solution.py:635
  107.7 12.8 %collective-permute-start.17 = (bf16[128,2048]{1,0:T(8,128)(2,1)S(1)}, bf16[128,2048]{1,0:T(8,128)(2,1)S(1)}, u32[]{:S(2)}, u32[]{:S(2)}) collective-permute-start(bf16[128,2048]{1,0:T(8,128)(2,1)S(1)} %get-tuple-element.93), channel_id=1, source_target_pairs={{0,8},{4,20},{8,0},{12,28},{16,24},{20,4},{24,16},{28,12},{1,9},{5... | collective-permute-start | bytes 1572872 | tf_op jit(solution)/shard_map/ppermute | solution.py:670
  110.5 11.5 %collective-permute-start.19 = (bf16[256,1024]{1,0:T(8,128)(2,1)S(1)}, bf16[256,1024]{1,0:T(8,128)(2,1)S(1)}, u32[]{:S(2)}, u32[]{:S(2)}) collective-permute-start(bf16[256,1024]{1,0:T(8,128)(2,1)S(1)} %get-tuple-element.91.refs_8_), channel_id=1, source_target_pairs={{0,16},{4,12},{8,24},{12,4},{16,0},{20,28},{24,8},{28,20},{1,17},{... | collective-permute-start | bytes 1572872 | tf_op jit(solution)/shard_map/ppermute | solution.py:670
  120.6 6.5 %collective-permute-start.18 = (bf16[64,2048]{1,0:T(8,128)(2,1)S(1)}, bf16[64,2048]{1,0:T(8,128)(2,1)S(1)}, u32[]{:S(2)}, u32[]{:S(2)}) collective-permute-start(bf16[64,2048]{1,0:T(8,128)(2,1)S(1)} %get-tuple-element.96), channel_id=1, source_target_pairs={{0,1},{1,0},{2,3},{3,2},{4,5},{5,4},{6,7},{7,6},{8,9},{9,8},{10,11... | collective-permute-start | bytes 786440 | tf_op jit(solution)/shard_map/ppermute | solution.py:635
  122.1 6.4 %collective-permute-start.21 = (bf16[128,1024]{1,0:T(8,128)(2,1)S(1)}, bf16[128,1024]{1,0:T(8,128)(2,1)S(1)}, u32[]{:S(2)}, u32[]{:S(2)}) collective-permute-start(bf16[128,1024]{1,0:T(8,128)(2,1)S(1)} %get-tuple-element.101), channel_id=1, source_target_pairs={{0,8},{4,20},{8,0},{12,28},{16,24},{20,4},{24,16},{28,12},{1,9},{5... | collective-permute-start | bytes 786440 | tf_op jit(solution)/shard_map/ppermute | solution.py:670
  128.6 7.5 %collective-permute-start.22 = (bf16[64,1024]{1,0:T(8,128)(2,1)S(1)}, bf16[64,1024]{1,0:T(8,128)(2,1)S(1)}, u32[]{:S(2)}, u32[]{:S(2)}) collective-permute-start(bf16[64,1024]{1,0:T(8,128)(2,1)S(1)} %get-tuple-element.103), channel_id=1, source_target_pairs={{0,1},{1,0},{2,3},{3,2},{4,5},{5,4},{6,7},{7,6},{8,9},{9,8},{10,11... | collective-permute-start | bytes 393224 | tf_op jit(solution)/shard_map/ppermute | solution.py:635
  129.4 9.9 %collective-permute-start.20 = (bf16[32,2048]{1,0:T(8,128)(2,1)S(1)}, bf16[32,2048]{1,0:T(8,128)(2,1)S(1)}, u32[]{:S(2)}, u32[]{:S(2)}) collective-permute-start(bf16[32,2048]{1,0:T(8,128)(2,1)S(1)} %get-tuple-element.100), channel_id=1, source_target_pairs={{0,2},{1,3},{2,0},{3,1},{4,6},{5,7},{6,4},{7,5},{8,10},{9,11},{10,... | collective-permute-start | bytes 393224 | tf_op jit(solution)/shard_map/ppermute | solution.py:635
  136.1 5.2 %collective-permute-start.23 = (bf16[32,1024]{1,0:T(8,128)(2,1)S(1)}, bf16[32,1024]{1,0:T(8,128)(2,1)S(1)}, u32[]{:S(2)}, u32[]{:S(2)}) collective-permute-start(bf16[32,1024]{1,0:T(8,128)(2,1)S(1)} %get-tuple-element.105), channel_id=1, source_target_pairs={{0,2},{1,3},{2,0},{3,1},{4,6},{5,7},{6,4},{7,5},{8,10},{9,11},{10,... | collective-permute-start | bytes 196616 | tf_op jit(solution)/shard_map/ppermute | solution.py:635
  (8 other events, 41.6 us)
